TPU v7x, 32 devices: a whole 2x2x4 slice. The times are simulated.
32 devices in a mesh: row: 4 (over z), col: 8 (over y, x, core).
Axes of the slice: x: 2, y: 2, z: 4, core: 2. Of those that a mesh axis runs over, the one named last changes fastest.
Arguments:
- right_side: float32 [3, 4096, 4096], P(None, 'row', 'col'), may hold values from -6 to 6
- panel_t: float32 [2, 1024, 3, 4096], P(None, 'col', None, 'row'), may hold values from -0.1875 to 0.1875
- inverse_blocks: float32 [2, 1024, 1024], P(None, 'row'), as said below
Outputs:
- solved: float32 [2, 1024, 4096], P(None, 'row', 'col')
- remaining: float32 [3, 4096, 4096], P(None, 'row', 'col')
Inputs may be any that keep to these rules, and one draw needn't show every extreme that they name: Each inverse_blocks[k] is lower triangular with a diagonal between 0.5 and 2.
All inputs are finite; a program needn't handle non-finite values.
Results may differ from a plain program's by a relative error of at most 0.0001.
Values sent between devices are 32-bit elements; how exact they have to be, the bound alone decides.
No kernel may reach another device: no remote copies, remote signals or barrier semaphores. Data moves between devices by JAX's collectives and lax.ppermute only.
A program may use at most 128 MiB of HBM per device.

v0:
```python
import jax
import jax.numpy as jnp
from jax import lax
from jax.sharding import PartitionSpec as P


def from_root(value, axis, source):
    kept = jnp.where(lax.axis_index(axis) == source, value, 0).astype(value.dtype)
    return lax.psum(kept, axis)


def body(right_side, panel_t, inverse_blocks):
    grid_rows = lax.axis_size("row")
    my_row = lax.axis_index("row")
    blocks_here = right_side.shape[0]
    global_block = jnp.arange(blocks_here, dtype=jnp.int32) * grid_rows + my_row
    results = []
    for k in range(2):
        owner = k % grid_rows
        top = from_root(right_side[k // grid_rows], "row", owner)
        share = jnp.dot(
            inverse_blocks[k],
            top,
            precision=lax.Precision.HIGHEST,
            preferred_element_type=jnp.float32,
        )
        results.append(share)
        solved_k = lax.all_gather(share, "row", axis=0, tiled=True)
        update = jnp.einsum(
            "cji,cr->jir",
            lax.all_gather(panel_t[k], "col", axis=0, tiled=True),
            solved_k,
            precision=lax.Precision.HIGHEST,
            preferred_element_type=jnp.float32,
        )
        keep_mask = (global_block > k)[:, None, None]
        right_side = right_side - jnp.where(keep_mask, update, jnp.float32(0.0))
    return (jnp.stack(results), right_side)


def solution(mesh):
    return jax.shard_map(
        body,
        mesh=mesh,
        in_specs=(P(None, "row", "col"), P(None, "col", None, "row"), P(None, "row", None)),
        out_specs=(P(None, "row", "col"), P(None, "row", "col")),
        check_vma=False,
    )
```

profile of v0, /device:TPU:18, one launch (start us, length us, event | category | flops | bytes accessed | tf_op | source)
XLA Modules:
  0.0 500.2 jit_solution(1730656317042692687)
XLA Ops:
  7.2 0.0 all-reduce.3.cloned.1.call-start
  7.2 6.6 %copy.5 = f32[3,1024,512]{1,2,0:T(8,128)} copy(f32[3,1024,512]{2,1,0:T(8,128)} %param.3) | data formatting | bytes 12582912 | tf_op args[0]
  13.8 3.2 fusion.9
  17.0 0.0 all-reduce.3.cloned.1.call-update
  17.0 0.0 copy-start.2
  17.0 0.0 all-gather.7.cloned.1.call-start
  17.1 86.5 %all-reduce.3.cloned.1.call-done = f32[1024,512]{0,1:T(8,128)} async-done(((f32[1024,512]{0,1:T(8,128)}), f32[1024,512]{0,1:T(8,128)}) %all-reduce.3.cloned.1.call-update) | async-done | bytes 2097168 | tf_op jit(solution)/shard_map/psum | solution.py:9
  103.6 4.5 fusion.14
  108.1 0.0 all-gather.7.cloned.1.call-update
  108.1 0.0 all-gather.11.cloned.1.call-start
  108.1 1.9 fusion.20
  110.0 0.0 all-gather.11.cloned.1.call-update
  110.0 0.0 all-reduce.5.cloned.1.call-start
  110.1 42.8 %all-gather.7.cloned.1.call-done = f32[1024,512]{0,1:T(8,128)} async-done(((f32[256,512]{0,1:T(8,128)}), f32[1024,512]{0,1:T(8,128)}) %all-gather.7.cloned.1.call-update) | async-done | bytes 2097168 | tf_op jit(solution)/shard_map/all_gather | solution.py:28
  152.9 74.3 %all-gather.11.cloned.1.call-done = f32[1,1024,3,1024]{3,1,2,0:T(8,128)} async-done(((f32[1,128,3,1024]{3,1,2,0:T(8,128)}), f32[1,1024,3,1024]{3,1,2,0:T(8,128)}) %all-gather.11.cloned.1.call-update) | async-done | bytes 12582928 | tf_op jit(solution)/shard_map/all_gather | solution.py:31
  227.2 24.4 %bitcast_subtract_fusion.1 = f32[3,1024,512]{1,2,0:T(8,128)S(1)} fusion(f32[3,1024,512]{1,2,0:T(8,128)} %copy.5, pred[3]{0:T(512)(128)(4,1)S(1)} %fusion.19, f32[1,1024,3,1024]{3,1,2,0:T(8,128)} %all-gather.11.cloned.1.call-done, f32[1024,512]{0,1:T(8,128)} %all-gather.7.cloned.1.call-done), kind=kOutput, calls=%fused_computation.5 | convolution fusion | flops 19330498560 | bytes 27262980 | tf_op jit(solution)/shard_map/cji,cr->jir/dot_general | solution.py:29
  251.7 0.0 copy-start
  251.7 2.7 copy-done
  254.4 1.5 fusion.8
  255.9 0.0 all-reduce.5.cloned.1.call-update
  255.9 0.0 all-gather.13.cloned.1.call-start
  255.9 0.5 all-gather.13.cloned.1.call-update
  256.5 0.2 all-gather.9.cloned.1.call-start
  256.7 84.7 %all-reduce.5.cloned.1.call-done = f32[1024,512]{0,1:T(8,128)} async-done(((f32[1024,512]{0,1:T(8,128)}), f32[1024,512]{0,1:T(8,128)}) %all-reduce.5.cloned.1.call-update) | async-done | bytes 2097168 | tf_op jit(solution)/shard_map/psum | solution.py:9
  341.4 4.2 fusion.12
  345.6 0.0 all-gather.9.cloned.1.call-update
  345.7 1.1 pad_maximum_fusion
  346.8 1.3 copy.7
  348.1 67.3 %all-gather.13.cloned.1.call-done = f32[1,1024,3,1024]{3,1,2,0:T(8,128)} async-done(((f32[1,128,3,1024]{3,1,2,0:T(8,128)}), f32[1,1024,3,1024]{3,1,2,0:T(8,128)}) %all-gather.13.cloned.1.call-update) | async-done | bytes 12582928 | tf_op jit(solution)/shard_map/all_gather | solution.py:31
  415.4 46.0 %all-gather.9.cloned.1.call-done = f32[1024,512]{0,1:T(8,128)} async-done(((f32[256,512]{0,1:T(8,128)}), f32[1024,512]{0,1:T(8,128)}) %all-gather.9.cloned.1.call-update) | async-done | bytes 2097168 | tf_op jit(solution)/shard_map/all_gather | solution.py:28
  461.5 25.3 %bitcast_subtract_fusion = f32[3,1024,512]{1,2,0:T(8,128)} fusion(f32[3,1024,512]{1,2,0:T(8,128)} %copy-done, pred[3]{0:T(512)(128)(4,1)S(1)} %fusion.18, f32[1,1024,3,1024]{3,1,2,0:T(8,128)} %all-gather.13.cloned.1.call-done, f32[1024,512]{0,1:T(8,128)} %all-gather.9.cloned.1.call-done), kind=kOutput, calls=%fused_computation.4 | convolution fusion | flops 19330498560 | bytes 27262980 | tf_op jit(solution)/shard_map/cji,cr->jir/dot_general | solution.py:29
  486.8 6.6 %copy.8 = f32[3,1024,512]{2,1,0:T(8,128)} copy(f32[3,1024,512]{1,2,0:T(8,128)} %bitcast_subtract_fusion) | data formatting | bytes 12582912
  (7 shorter events, 0.0 us)
Async XLA Ops:
  7.2 96.4 %all-reduce.3.cloned.1.call-start = ((), (), s32[]{:S(2)}) async-start(), calls=%async_computation | async-start | bytes 4194304 | tf_op jit(solution)/shard_map/psum | solution.py:9
  17.0 91.1 %copy-start.2 = (f32[2,128,3,1024]{3,1,2,0:T(8,128)S(1)}, f32[2,128,3,1024]{3,1,2,0:T(8,128)}, u32[]{:S(2)}) copy-start(f32[2,128,3,1024]{3,1,2,0:T(8,128)} %param.4) | copy-start | bytes 9437188
  17.0 135.9 %all-gather.7.cloned.1.call-start = ((), (), s32[]{:S(2)}) async-start(), calls=%async_computation.1 | async-start | bytes 2621440 | tf_op jit(solution)/shard_map/all_gather | solution.py:28
  108.1 119.2 %all-gather.11.cloned.1.call-start = ((), (), s32[]{:S(2)}) async-start(), calls=%async_computation.4 | async-start | bytes 14155776 | tf_op jit(solution)/shard_map/all_gather | solution.py:31
  110.0 231.4 %all-reduce.5.cloned.1.call-start = ((), (), s32[]{:S(2)}) async-start(), calls=%async_computation.2 | async-start | bytes 4194304 | tf_op jit(solution)/shard_map/psum | solution.py:9
  251.7 2.7 copy-start
  255.9 85.5 %copy-start.3 = (f32[2,256,1024]{2,1,0:T(8,128)S(1)}, f32[2,256,1024]{2,1,0:T(8,128)}, u32[]{:S(2)}) copy-start(f32[2,256,1024]{2,1,0:T(8,128)} %param.5) | copy-start | bytes 6291460
  255.9 159.5 %all-gather.13.cloned.1.call-start = ((), (), s32[]{:S(2)}) async-start(), calls=%async_computation.5 | async-start | bytes 14155776 | tf_op jit(solution)/shard_map/all_gather | solution.py:31
  256.5 89.2 %copy-start.1 = (f32[512,256]{1,0:T(8,128)S(1)}, f32[512,256]{1,0:T(8,128)}, u32[]{:S(2)}) copy-start(f32[512,256]{1,0:T(8,128)} %fusion.14) | copy-start | bytes 1572868
  256.5 205.0 %all-gather.9.cloned.1.call-start = ((), (), s32[]{:S(2)}) async-start(), calls=%async_computation.3 | async-start | bytes 2621440 | tf_op jit(solution)/shard_map/all_gather | solution.py:28
Sparse Core Ops, SparseCore 0:
  17.1 86.3 all-reduce.2
  108.2 44.6 all-gather.6
  155.0 72.1 all-gather.10
  256.0 85.3 all-reduce.4
  343.2 72.2 all-gather.12
  416.9 44.5 all-gather.8
where the time goes:
time: 504 us; the launch traced here: 500 us
  waiting for transfers between devices  402 us (80%)
  matrix products  58.5 us (12%)
  local copies, waits for them, and re-layouts  19 us (4%)
  between operations  14.2 us (3%)
  other arithmetic  5.8 us (1%)
    psum x2, waiting for transfers between devices, from_root(): return lax.psum(kept, axis)  171 us
    all_gather x2, waiting for transfers between devices, body(): lax.all_gather(panel_t[k], 'col', axis=0, tiled=True)  142 us
    all_gather x2, waiting for transfers between devices, body(): solved_k = lax.all_gather(share, 'row', axis=0, tiled=True)  88.8 us
    dot_general x2, matrix products, body(): jnp.einsum('cji,cr->jir', lax.all_gather(panel_t[k], 'col', axis=0, tiled...  49.8 us
    unnamed x11, local copies, waits for them, and re-layouts  17.1 us
  transfers between devices with their start and end apart: 6, of which 6 were waited for; matrix products, arithmetic and copies ran while one was open for 2% of the time, Pallas kernels for 0%

commit v1 on v0

--- a/solution.py
+++ b/solution.py
@@ -1,7 +1,13 @@
+import functools
+
 import jax
 import jax.numpy as jnp
 from jax import lax
+from jax.experimental import pallas as pl
+from jax.experimental.pallas import tpu as pltpu
 from jax.sharding import PartitionSpec as P
+
+LAG = 1
 
 
 def from_root(value, axis, source):
@@ -9,7 +15,7 @@
     return lax.psum(kept, axis)
 
 
-def body(right_side, panel_t, inverse_blocks):
+def plain_body(right_side, panel_t, inverse_blocks):
     grid_rows = lax.axis_size("row")
     my_row = lax.axis_index("row")
     blocks_here = right_side.shape[0]
@@ -38,9 +44,195 @@
     return (jnp.stack(results), right_side)
 
 
+def split(x):
+    hi = x.astype(jnp.bfloat16)
+    return hi, (x - hi.astype(jnp.float32)).astype(jnp.bfloat16)
+
+
+def dot3(a, b_hi, b_lo):
+    a_hi, a_lo = split(a)
+    dot = functools.partial(jnp.dot, preferred_element_type=jnp.float32)
+    return dot(a_hi, b_hi) + (dot(a_hi, b_lo) + dot(a_lo, b_hi))
+
+
+def update(rhs, panels, sources, k, first_piece=0, alias=False, all_rows=False):
+    blocks, rows, cols = rhs.shape
+    width = panels[0].shape[3]
+    tile = min(256, rows)
+    steps = rows // tile
+    depth = sum(c.shape[0] for c in sources[0])
+    pieces = depth // width
+    arrays = []
+    for chunks in sources:
+        for chunk in chunks:
+            if not any(chunk is a for a in arrays):
+                arrays.append(chunk)
+    where = [[next(i for i, a in enumerate(arrays) if a is c) for c in chunks] for chunks in sources]
+    heights = [c.shape[0] for c in sources[0]]
+    starts = [sum(p.shape[1] for p in panels[:i]) for i in range(len(panels))]
+
+    def kernel(rhs_ref, *refs):
+        panel_refs, refs = refs[: len(panels)], refs[len(panels):]
+        chunk_refs, refs = refs[: len(arrays)], refs[len(arrays):]
+        out_ref, whole, x_hi, x_lo, sems = refs
+        step = pl.program_id(0)
+        my_row = lax.axis_index("row")
+
+        @pl.when(step == 0)
+        def _():
+            for row, ids in enumerate(where):
+
+                @pl.when((my_row == row) if not all_rows else (row == 0))
+                def _():
+                    copies = []
+                    at = 0
+                    for n, i in enumerate(ids):
+                        copies.append(
+                            pltpu.make_async_copy(
+                                chunk_refs[i], whole.at[pl.ds(at, heights[n])], sems.at[n]
+                            )
+                        )
+                        at += heights[n]
+                    for copy in copies:
+                        copy.start()
+                    for copy in copies:
+                        copy.wait()
+
+            hi, lo = split(whole[...])
+            x_hi[...] = hi
+            x_lo[...] = lo
+
+        j = step // steps
+        if all_rows:
+            active = j >= 0
+        else:
+            active = j * len(sources) + my_row > k
+
+        for i, panel in enumerate(panel_refs):
+            inside = (j >= starts[i]) & (j < starts[i] + panels[i].shape[1])
+
+            @pl.when(active & inside)
+            def _():
+                left = jnp.concatenate([panel[p, 0] for p in range(pieces)], axis=1)
+                out_ref[0] = rhs_ref[0] - dot3(left, x_hi[...], x_lo[...])
+
+        @pl.when(jnp.logical_not(active))
+        def _():
+            out_ref[0] = rhs_ref[0]
+
+    def panel_spec(i):
+        last = panels[i].shape[1] * steps - 1
+
+        def index(s):
+            at = jnp.clip(s - starts[i] * steps, 0, last)
+            return (first_piece // pieces, at // steps, at % steps, 0)
+
+        return pl.BlockSpec((pieces, 1, tile, width), index)
+
+    block = pl.BlockSpec((1, tile, cols), lambda s: (s // steps, s % steps, 0))
+    flops = 2 * 3 * blocks * rows * depth * cols
+    moved = 4 * (2 * blocks * rows * cols + blocks * rows * depth + depth * cols)
+    return pl.pallas_call(
+        kernel,
+        grid=(blocks * steps,),
+        in_specs=[block]
+        + [panel_spec(i) for i in range(len(panels))]
+        + [pl.BlockSpec(memory_space=pl.ANY)] * len(arrays),
+        out_specs=block,
+        out_shape=jax.ShapeDtypeStruct(rhs.shape, rhs.dtype),
+        scratch_shapes=[
+            pltpu.VMEM((depth, cols), jnp.float32),
+            pltpu.VMEM((depth, cols), jnp.bfloat16),
+            pltpu.VMEM((depth, cols), jnp.bfloat16),
+            pltpu.SemaphoreType.DMA((len(heights),)),
+        ],
+        input_output_aliases={0: 0} if alias else {},
+        compiler_params=pltpu.CompilerParams(vmem_limit_bytes=32 * 2**20),
+        cost_estimate=pl.CostEstimate(flops=flops, bytes_accessed=moved, transcendentals=0),
+    )(rhs, *panels, *arrays)
+
+
+def body(right_side, panel_t, inverse_blocks):
+    n_row = lax.axis_size("row")
+    my_row = lax.axis_index("row")
+    share = inverse_blocks.shape[1]
+    depth = inverse_blocks.shape[2]
+    n = depth // share
+
+    def send(value, pairs):
+        return lax.ppermute(value, "row", pairs)
+
+    def high(a, b):
+        return jnp.dot(a, b, precision=lax.Precision.HIGH, preferred_element_type=jnp.float32)
+
+    panel = jnp.transpose(panel_t, (0, 2, 3, 1))
+    head0 = lax.all_gather(panel[0, :1], "col")
+    tail0 = lax.all_gather(panel[0, 1:], "col")
+    whole1 = lax.all_gather(panel[1], "col")
+
+    inverse0 = [inverse_blocks[0]]
+    for q in range(1, n):
+        inverse0.append(send(inverse_blocks[0][:, : (q + 1) * share], [(q, 0)]))
+    inverse1 = []
+    for q in range(n):
+        own = inverse_blocks[1][:, : (q + 1) * share]
+        inverse1.append(own if q == 1 else send(own, [(q, 1)]))
+
+    top = right_side[0]
+    line = [(r, r + 1) for r in range(n_row - 1)]
+    slots = 2 * n + LAG * (n_row - 2)
+    received = []
+    first = []
+    second = []
+    lowered = None
+    for t in range(slots):
+        value = received[t - LAG] if t >= LAG else None
+        q = t - LAG - n
+        if 0 <= q < n:
+            if q == 0:
+                lowered = update(
+                    right_side[:1], [head0], [received[:n]], 0, all_rows=True
+                )[0]
+            second.append(high(inverse1[q], lowered[: (q + 1) * share]))
+            value = jnp.where(my_row == 1, second[q], value)
+        if t < n:
+            first.append(high(inverse0[t][:, : (t + 1) * share], top[: (t + 1) * share]))
+            value = first[t] if value is None else jnp.where(my_row == 0, first[t], value)
+        received.append(send(value, line))
+    back = []
+    for q in range(0, n, 2):
+        pair = send(jnp.concatenate(second[q:q + 2], axis=0), [(1, 0)])
+        back += [pair[:share], pair[share:]]
+
+    chunks0 = [first] + [received[LAG * (r - 1):][:n] for r in range(1, n_row)]
+    chunks1 = [back, second] + [received[n + LAG * (r - 1):][:n] for r in range(2, n_row)]
+
+    remaining = update(right_side, [head0, tail0], chunks0, 0)
+    early = n - 1
+    remaining = update(remaining, [whole1], [c[:early] for c in chunks1], 1, alias=True)
+    per = share // panel.shape[3]
+    remaining = update(
+        remaining, [whole1], [c[early:] for c in chunks1], 1, first_piece=early * per, alias=True
+    )
+
+    solved = []
+    for chunks in (chunks0, chunks1):
+        mine = chunks[0][0]
+        for r in range(1, n_row):
+            mine = jnp.where(my_row == r, chunks[r][r], mine)
+        solved.append(mine)
+    return (jnp.stack(solved), remaining)
+
+
+def choose(right_side, panel_t, inverse_blocks):
+    if panel_t.shape[1] % 128 == 0 and inverse_blocks.shape[1] % 256 == 0:
+        return body(right_side, panel_t, inverse_blocks)
+    return plain_body(right_side, panel_t, inverse_blocks)
+
+
 def solution(mesh):
     return jax.shard_map(
-        body,
+        choose,
         mesh=mesh,
         in_specs=(P(None, "row", "col"), P(None, "col", None, "row"), P(None, "row", None)),
         out_specs=(P(None, "row", "col"), P(None, "row", "col")),

time: 504 us -> 286 us (0.57)
  waiting for transfers between devices: 402 us -> 117 us
  Pallas kernels: 0 us -> 51.8 us
  matrix products: 58.5 us -> 19.4 us
  starting transfers between devices: 0.42 us -> 36.5 us
  local copies, waits for them, and re-layouts: 19 us -> 40.4 us
    all_gather x4 -> x3, waiting for transfers between devices: 230 us -> 0.02 us  [the longest x1 0.02 us: body(): whole1 = lax.all_gather(panel[1], 'col')]
    psum x2 -> x0, waiting for transfers between devices: 171 us -> none  [from_root(): return lax.psum(kept, axis)]
    ppermute x0 -> x18, waiting for transfers between devices: none -> 117 us  [send(): return lax.ppermute(value, 'row', pairs)]
    pallas_call x0 -> x4, Pallas kernels: none -> 51.8 us  [update(): pl.pallas_call(kernel, grid=(blocks * steps,), in_specs=[block] + [panel_...]
    dot_general x4 -> x8, matrix products: 58.5 us -> 19.4 us  [high(): jnp.dot(a, b, precision=lax.Precision.HIGH, preferred_element_type=jnp.fl...]
    ppermute x0 -> x18, starting transfers between devices: none -> 36.4 us  [send(): return lax.ppermute(value, 'row', pairs)]
    unnamed x11 -> x73, local copies, waits for them, and re-layouts: 17.1 us -> 28 us
    slice x1 -> x9, local copies, waits for them, and re-layouts: 1.89 us -> 10.8 us  [the longest x1 3.08 us: body(): right_side[:1]]
  transfers between devices with their start and end apart: 6 -> 21, of which waited for: 6 -> 10; matrix products, arithmetic and copies ran while one was open for 2% -> 12% of each run, Pallas kernels for 0% -> 8%
where the time goes in v1:
time: 286 us; the launch traced here: 284 us
  waiting for transfers between devices  117 us (41%)
  Pallas kernels  51.8 us (18%)
  local copies, waits for them, and re-layouts  40.4 us (14%)
  starting transfers between devices  36.5 us (13%)
  matrix products  19.4 us (7%)
  between operations  14.2 us (5%)
  other arithmetic  4.09 us (1%)
    ppermute x18, waiting for transfers between devices, send(): return lax.ppermute(value, 'row', pairs)  117 us
    pallas_call x4, Pallas kernels, update(): pl.pallas_call(kernel, grid=(blocks * steps,), in_specs=[block] + [panel_...  51.8 us
    ppermute x18, starting transfers between devices, send(): return lax.ppermute(value, 'row', pairs)  36.4 us
    unnamed x73, local copies, waits for them, and re-layouts  28 us
    dot_general x8, matrix products, high(): jnp.dot(a, b, precision=lax.Precision.HIGH, preferred_element_type=jnp.fl...  19.4 us
  transfers between devices with their start and end apart: 21, of which 10 were waited for; matrix products, arithmetic and copies ran while one was open for 12% of the time, Pallas kernels for 8%

profile of v1, /device:TPU:18, one launch (start us, length us, event | category | flops | bytes accessed | tf_op | source)
XLA Modules:
  0.0 283.6 jit_solution(17296273819669035777)
XLA Ops:
  7.2 2.4 copy.8
  16.4 3.5 %collective-permute-start = (f32[256,512]{1,0:T(8,128)S(1)}, f32[256,512]{1,0:T(8,128)S(1)}, u32[]{:S(2)}, u32[]{:S(2)}) collective-permute-start(f32[256,512]{1,0:T(8,128)S(1)} %fusion.16.refs_2_), channel_id=1, source_target_pairs={{0,8},{8,16},{16,24},{1,9},{9,17},{17,25},{2,10},{10,18},{18,26},{... | collective-permute-start | bytes 1572872 | tf_op jit(solution)/shard_map/ppermute | solution.py:163
  23.2 3.0 %collective-permute-start.3 = (f32[256,768]{1,0:T(8,128)}, f32[256,768]{1,0:T(8,128)}, u32[]{:S(2)}, u32[]{:S(2)}) collective-permute-start(f32[256,768]{1,0:T(8,128)} %slice.125), channel_id=1, source_target_pairs={{16,0},{17,1},{18,2},{19,3},{20,4},{21,5},{22,6},{23,7}} | collective-permute-start | bytes 2359304 | tf_op jit(solution)/shard_map/ppermute | solution.py:163
  26.2 5.8 %collective-permute-done.refs_1_.refs_6_ = f32[256,512]{1,0:T(8,128)S(1)} collective-permute-done((f32[256,512]{1,0:T(8,128)S(1)}, f32[256,512]{1,0:T(8,128)S(1)}, u32[]{:S(2)}, u32[]{:S(2)}) %collective-permute-start) | collective-permute-done | bytes 524320 | tf_op jit(solution)/shard_map/ppermute | solution.py:163
  32.0 3.0 %broadcast_select_fusion.2 = (f32[256,512]{1,0:T(8,128)S(1)}, f32[256,512]{1,0:T(8,128)}) fusion(f32[256,512]{1,0:T(8,128)S(1)} %collective-permute-done.refs_1_.refs_6_, pred[]{:T(512)S(6)} %eq.10, f32[256,512]{1,0:T(8,128)} %collective-permute-done.1, f32[3,1024,512]{2,1,0:T(8,128)} %rhs_ref.1), kind=kOutput, calls=%fused_computation.32 | convolution fusion | flops 402784256 | bytes 3145729 | tf_op jit(solution)/shard_map/dot_general | solution.py:166
  35.0 3.5 %collective-permute-start.2 = (f32[256,512]{1,0:T(8,128)S(1)}, f32[256,512]{1,0:T(8,128)S(1)}, u32[]{:S(2)}, u32[]{:S(2)}) collective-permute-start(f32[256,512]{1,0:T(8,128)S(1)} %get-tuple-element.11), channel_id=1, source_target_pairs={{0,8},{8,16},{16,24},{1,9},{9,17},{17,25},{2,10},{10,18},{18,26},{... | collective-permute-start | bytes 1572872 | tf_op jit(solution)/shard_map/ppermute | solution.py:163
  39.2 2.9 %collective-permute-done.3 = f32[256,768]{1,0:T(8,128)} collective-permute-done((f32[256,768]{1,0:T(8,128)}, f32[256,768]{1,0:T(8,128)}, u32[]{:S(2)}, u32[]{:S(2)}) %collective-permute-start.3) | collective-permute-done | bytes 786464 | tf_op jit(solution)/shard_map/ppermute | solution.py:163
  42.1 25.0 %collective-permute-done.2.refs_2_.refs_7_ = f32[256,512]{1,0:T(8,128)S(1)} collective-permute-done((f32[256,512]{1,0:T(8,128)S(1)}, f32[256,512]{1,0:T(8,128)S(1)}, u32[]{:S(2)}, u32[]{:S(2)}) %collective-permute-start.2) | collective-permute-done | bytes 524320 | tf_op jit(solution)/shard_map/ppermute | solution.py:163
  67.1 3.5 %broadcast_select_fusion.1 = (f32[256,512]{1,0:T(8,128)S(1)}, f32[256,512]{1,0:T(8,128)}) fusion(f32[256,512]{1,0:T(8,128)S(1)} %collective-permute-done.2.refs_2_.refs_7_, pred[]{:T(512)S(6)} %eq.10, f32[256,768]{1,0:T(8,128)} %collective-permute-done.3, f32[3,1024,512]{2,1,0:T(8,128)} %rhs_ref.1), kind=kOutput, calls=%fused_computation.31 | convolution fusion | flops 604110848 | bytes 3932161 | tf_op jit(solution)/shard_map/dot_general | solution.py:166
  72.5 11.9 %collective-permute-done.4.refs_3_.refs_8_ = f32[256,512]{1,0:T(8,128)S(1)} collective-permute-done((f32[256,512]{1,0:T(8,128)S(1)}, f32[256,512]{1,0:T(8,128)S(1)}, u32[]{:S(2)}, u32[]{:S(2)}) %collective-permute-start.4) | collective-permute-done | bytes 524320 | tf_op jit(solution)/shard_map/ppermute | solution.py:163
  84.4 3.7 %broadcast_select_fusion = (f32[256,512]{1,0:T(8,128)S(1)}, f32[256,512]{1,0:T(8,128)}) fusion(f32[256,512]{1,0:T(8,128)S(1)} %collective-permute-done.4.refs_3_.refs_8_, pred[]{:T(512)S(6)} %eq.10, f32[256,1024]{1,0:T(8,128)S(1)} %collective-permute-done.5, f32[3,1024,512]{2,1,0:T(8,128)} %rhs_ref.1), kind=kOutput, calls=%fused_computation.30 | convolution fusion | flops 805437440 | bytes 4718593 | tf_op jit(solution)/shard_map/dot_general | solution.py:166
  88.1 2.2 collective-permute-start.6
  90.3 10.9 %collective-permute-done.6.refs_4_.refs_9_ = f32[256,512]{1,0:T(8,128)} collective-permute-done((f32[256,512]{1,0:T(8,128)S(1)}, f32[256,512]{1,0:T(8,128)}, u32[]{:S(2)}, u32[]{:S(2)}) %collective-permute-start.6) | collective-permute-done | bytes 524320 | tf_op jit(solution)/shard_map/ppermute | solution.py:163
  101.2 2.5 collective-permute-start.8
  105.1 3.1 %slice.94.rhs_ref = f32[1,1024,512]{2,1,0:T(8,128)} slice(f32[3,1024,512]{2,1,0:T(8,128)} %rhs_ref.1), slice={[0:1], [0:1024], [0:512]} | slice | bytes 4194304 | tf_op jit(solution)/shard_map/slice | solution.py:194
  110.8 2.2 copy-done.31
  113.0 6.0 %shard_map.50 = f32[1,1024,512]{2,1,0:T(8,128)S(1)} custom-call(f32[1,1024,512]{2,1,0:T(8,128)S(1)} %copy-done.8, f32[8,1,1024,128]{3,2,1,0:T(8,128)S(1)} %copy-done.31, f32[256,512]{1,0:T(8,128)S(1)} %copy-done.28, f32[256,512]{1,0:T(8,128)S(1)} %collective-permute-done.2.refs_2_.refs_7_, f32[256,512]{1,0:T(8,128)S(1)} %collective-permute-done.4.refs_3_.refs_8_, ...), custom_call_target="tpu_custom_call" | custom-call | flops 3221225472 | bytes 10485760 | tf_op jit(solution)/shard_map/pallas_call | solution.py:135
  119.0 2.5 broadcast_select_fusion.6
  124.4 4.8 %collective-permute-start.11 = (f32[256,768]{1,0:T(8,128)}, f32[256,768]{1,0:T(8,128)}, u32[]{:S(2)}, u32[]{:S(2)}) collective-permute-start(f32[256,768]{1,0:T(8,128)} %slice.129), channel_id=1, source_target_pairs={{16,8},{17,9},{18,10},{19,11},{20,12},{21,13},{22,14},{23,15}} | collective-permute-start | bytes 2359304 | tf_op jit(solution)/shard_map/ppermute | solution.py:163
  130.9 3.0 %collective-permute-done.9.refs_11_.refs_7_ = f32[256,512]{1,0:T(8,128)} collective-permute-done((f32[256,512]{1,0:T(8,128)}, f32[256,512]{1,0:T(8,128)}, u32[]{:S(2)}, u32[]{:S(2)}) %collective-permute-start.9) | collective-permute-done | bytes 524320 | tf_op jit(solution)/shard_map/ppermute | solution.py:163
  138.3 25.8 %collective-permute-done.11 = f32[256,768]{1,0:T(8,128)} collective-permute-done((f32[256,768]{1,0:T(8,128)}, f32[256,768]{1,0:T(8,128)}, u32[]{:S(2)}, u32[]{:S(2)}) %collective-permute-start.11) | collective-permute-done | bytes 786464 | tf_op jit(solution)/shard_map/ppermute | solution.py:163
  164.1 2.2 broadcast_select_fusion.4
  168.2 13.3 %collective-permute-done.13.refs_9_ = f32[256,512]{1,0:T(8,128)S(1)} collective-permute-done((f32[256,512]{1,0:T(8,128)S(1)}, f32[256,512]{1,0:T(8,128)S(1)}, u32[]{:S(2)}, u32[]{:S(2)}) %collective-permute-start.13) | collective-permute-done | bytes 524320 | tf_op jit(solution)/shard_map/ppermute | solution.py:163
  186.6 10.6 %collective-permute-done.14.refs_10_.refs_3_ = f32[256,512]{1,0:T(8,128)S(1)} collective-permute-done((f32[256,512]{1,0:T(8,128)S(1)}, f32[256,512]{1,0:T(8,128)S(1)}, u32[]{:S(2)}, u32[]{:S(2)}) %collective-permute-start.14) | collective-permute-done | bytes 524320 | tf_op jit(solution)/shard_map/ppermute | solution.py:163
  197.2 2.1 collective-permute-start.15
  200.4 7.9 %collective-permute-done.15.refs_4_ = f32[256,512]{1,0:T(8,128)S(1)} collective-permute-done((f32[256,512]{1,0:T(8,128)S(1)}, f32[256,512]{1,0:T(8,128)S(1)}, u32[]{:S(2)}, u32[]{:S(2)}) %collective-permute-start.15) | collective-permute-done | bytes 524320 | tf_op jit(solution)/shard_map/ppermute | solution.py:163
  211.2 2.8 copy-done.2
  219.2 2.2 copy-done.32
  221.3 17.9 %shard_map.51.rhs_ref = f32[3,1024,512]{2,1,0:T(8,128)} custom-call(f32[3,1024,512]{2,1,0:T(8,128)S(1)} %copy-done.2, f32[8,1,1024,128]{3,2,1,0:T(8,128)S(1)} %copy-done.32, f32[8,2,1024,128]{3,2,1,0:T(8,128)} %all-gather.6.cloned.1.call-done.refs_1_, f32[256,512]{1,0:T(8,128)S(1)} %copy-done.12, f32[256,512]{1,0:T(8,128)S(1)} %copy-done.30, ...), custom_call_target="tpu_custom_call" | custom-call | flops 9663676416 | bytes 27262976 | tf_op jit(solution)/shard_map/pallas_call | solution.py:135
  239.3 4.6 %copy-done = f32[8,3,1024,128]{3,2,1,0:T(8,128)S(1)} copy-done((f32[8,3,1024,128]{3,2,1,0:T(8,128)S(1)}, f32[8,3,1024,128]{3,2,1,0:T(8,128)}, u32[]{:S(2)}) %copy-start) | copy-done | bytes 12582936
  249.1 16.7 %shard_map.52.rhs_ref = f32[3,1024,512]{2,1,0:T(8,128)} custom-call(f32[3,1024,512]{2,1,0:T(8,128)} %shard_map.51.rhs_ref, f32[8,3,1024,128]{3,2,1,0:T(8,128)S(1)} %copy-done, f32[256,512]{1,0:T(8,128)S(1)} %copy-done.18, f32[256,512]{1,0:T(8,128)S(1)} %copy-done.17, f32[256,512]{1,0:T(8,128)S(1)} %copy-done.20, ...), custom_call_target="tpu_custom_call", output_to_operand_aliasing={{}: (0, {})} | custom-call | flops 7247757312 | bytes 23592960 | tf_op jit(solution)/shard_map/pallas_call | solution.py:135
  265.8 11.2 %shard_map.53 = f32[3,1024,512]{2,1,0:T(8,128)} custom-call(f32[3,1024,512]{2,1,0:T(8,128)} %shard_map.52.rhs_ref, f32[8,3,1024,128]{3,2,1,0:T(8,128)S(1)} %copy-done.1, f32[256,512]{1,0:T(8,128)S(1)} %copy-done.19, f32[256,512]{1,0:T(8,128)S(1)} %copy-done.7, f32[256,512]{1,0:T(8,128)S(1)} %copy-done.22, ...), custom_call_target="tpu_custom_call", output_to_operand_aliasing={{}: (0, {})} | custom-call | flops 2415919104 | bytes 16252928 | tf_op jit(solution)/shard_map/pallas_call | solution.py:135
  (113 shorter events, 47.0 us)
Async XLA Ops:
  7.2 101.0 %all-gather.4.cloned.1.call-start = ((), (), s32[]{:S(2)}) async-start(), calls=%async_computation | async-start | bytes 4718592 | tf_op jit(solution)/shard_map/all_gather | solution.py:169
  10.4 200.2 %all-gather.6.cloned.1.call-start = ((), (), s32[]{:S(2)}) async-start(), calls=%async_computation.1 | async-start | bytes 9437184 | tf_op jit(solution)/shard_map/all_gather | solution.py:170
  11.6 227.7 %all-gather.8.cloned.1.call-start = ((), (), s32[]{:S(2)}) async-start(), calls=%async_computation.2 | async-start | bytes 14155776 | tf_op jit(solution)/shard_map/all_gather | solution.py:171
  14.6 89.1 %copy-start.33 = (f32[256,1024]{1,0:T(8,128)}, f32[256,1024]{1,0:T(8,128)S(1)}, u32[]{:S(2)}) copy-start(f32[256,1024]{1,0:T(8,128)S(1)} %get-tuple-element.3) | copy-start | bytes 3145732
  16.4 18.6 %copy-start.11 = (f32[256,512]{1,0:T(8,128)}, f32[256,512]{1,0:T(8,128)S(1)}, u32[]{:S(2)}) copy-start(f32[256,512]{1,0:T(8,128)S(1)} %fusion.16.refs_2_) | copy-start | bytes 1572868
  16.4 15.6 %collective-permute-start = (f32[256,512]{1,0:T(8,128)S(1)}, f32[256,512]{1,0:T(8,128)S(1)}, u32[]{:S(2)}, u32[]{:S(2)}) collective-permute-start(f32[256,512]{1,0:T(8,128)S(1)} %fusion.16.refs_2_), channel_id=1, source_target_pairs={{0,8},{8,16},{16,24},{1,9},{9,17},{17,25},{2,10},{10,18},{18,26},{... | collective-permute-start | bytes 1572872 | tf_op jit(solution)/shard_map/ppermute | solution.py:163
  20.8 11.2 %collective-permute-start.1 = (f32[256,512]{1,0:T(8,128)}, f32[256,512]{1,0:T(8,128)}, u32[]{:S(2)}, u32[]{:S(2)}) collective-permute-start(f32[256,512]{1,0:T(8,128)} %slice.124), channel_id=1, source_target_pairs={{8,0},{9,1},{10,2},{11,3},{12,4},{13,5},{14,6},{15,7}} | collective-permute-start | bytes 1572872 | tf_op jit(solution)/shard_map/ppermute | solution.py:163
  23.2 19.0 %collective-permute-start.3 = (f32[256,768]{1,0:T(8,128)}, f32[256,768]{1,0:T(8,128)}, u32[]{:S(2)}, u32[]{:S(2)}) collective-permute-start(f32[256,768]{1,0:T(8,128)} %slice.125), channel_id=1, source_target_pairs={{16,0},{17,1},{18,2},{19,3},{20,4},{21,5},{22,6},{23,7}} | collective-permute-start | bytes 2359304 | tf_op jit(solution)/shard_map/ppermute | solution.py:163
  35.0 32.1 %collective-permute-start.2 = (f32[256,512]{1,0:T(8,128)S(1)}, f32[256,512]{1,0:T(8,128)S(1)}, u32[]{:S(2)}, u32[]{:S(2)}) collective-permute-start(f32[256,512]{1,0:T(8,128)S(1)} %get-tuple-element.11), channel_id=1, source_target_pairs={{0,8},{8,16},{16,24},{1,9},{9,17},{17,25},{2,10},{10,18},{18,26},{... | collective-permute-start | bytes 1572872 | tf_op jit(solution)/shard_map/ppermute | solution.py:163
  38.5 34.0 %collective-permute-start.5 = (f32[256,1024]{1,0:T(8,128)S(1)}, f32[256,1024]{1,0:T(8,128)S(1)}, u32[]{:S(2)}, u32[]{:S(2)}) collective-permute-start(f32[256,1024]{1,0:T(8,128)S(1)} %get-tuple-element.2), channel_id=1, source_target_pairs={{24,0},{25,1},{26,2},{27,3},{28,4},{29,5},{30,6},{31,7}} | collective-permute-start | bytes 3145736 | tf_op jit(solution)/shard_map/ppermute | solution.py:163
  67.1 66.8 %copy-start.9 = (f32[256,512]{1,0:T(8,128)}, f32[256,512]{1,0:T(8,128)S(1)}, u32[]{:S(2)}) copy-start(f32[256,512]{1,0:T(8,128)S(1)} %collective-permute-done.2.refs_2_.refs_7_) | copy-start | bytes 1572868
  70.6 13.8 %collective-permute-start.4 = (f32[256,512]{1,0:T(8,128)S(1)}, f32[256,512]{1,0:T(8,128)S(1)}, u32[]{:S(2)}, u32[]{:S(2)}) collective-permute-start(f32[256,512]{1,0:T(8,128)S(1)} %get-tuple-element.13), channel_id=1, source_target_pairs={{0,8},{8,16},{16,24},{1,9},{9,17},{17,25},{2,10},{10,18},{18,26},{... | collective-permute-start | bytes 1572872 | tf_op jit(solution)/shard_map/ppermute | solution.py:163
  84.4 23.8 %copy-start.24 = (f32[256,512]{1,0:T(8,128)}, f32[256,512]{1,0:T(8,128)S(1)}, u32[]{:S(2)}) copy-start(f32[256,512]{1,0:T(8,128)S(1)} %collective-permute-done.4.refs_3_.refs_8_) | copy-start | bytes 1572868
  88.1 13.1 %collective-permute-start.6 = (f32[256,512]{1,0:T(8,128)S(1)}, f32[256,512]{1,0:T(8,128)}, u32[]{:S(2)}, u32[]{:S(2)}) collective-permute-start(f32[256,512]{1,0:T(8,128)S(1)} %get-tuple-element.15), channel_id=1, source_target_pairs={{0,8},{8,16},{16,24},{1,9},{9,17},{17,25},{2,10},{10,18},{18,26},{... | collective-permute-start | bytes 1572872 | tf_op jit(solution)/shard_map/ppermute | solution.py:163
  101.2 17.8 %collective-permute-start.8 = (f32[256,512]{1,0:T(8,128)}, f32[256,512]{1,0:T(8,128)}, u32[]{:S(2)}, u32[]{:S(2)}) collective-permute-start(f32[256,512]{1,0:T(8,128)} %collective-permute-done.6.refs_4_.refs_9_), channel_id=1, source_target_pairs={{0,8},{8,16},{16,24},{1,9},{9,17},{17,25},{2,10},{10,18},{18,26},{... | collective-permute-start | bytes 1572872 | tf_op jit(solution)/shard_map/ppermute | solution.py:163
  104.4 14.6 %collective-permute-start.7 = (f32[256,256]{1,0:T(8,128)}, f32[256,256]{1,0:T(8,128)S(1)}, u32[]{:S(2)}, u32[]{:S(2)}) collective-permute-start(f32[256,256]{1,0:T(8,128)} %slice.127), channel_id=1, source_target_pairs={{0,8},{1,9},{2,10},{3,11},{4,12},{5,13},{6,14},{7,15}} | collective-permute-start | bytes 786440 | tf_op jit(solution)/shard_map/ppermute | solution.py:163
  121.5 12.3 %collective-permute-start.9 = (f32[256,512]{1,0:T(8,128)}, f32[256,512]{1,0:T(8,128)}, u32[]{:S(2)}, u32[]{:S(2)}) collective-permute-start(f32[256,512]{1,0:T(8,128)} %get-tuple-element.17), channel_id=1, source_target_pairs={{0,8},{8,16},{16,24},{1,9},{9,17},{17,25},{2,10},{10,18},{18,26},{... | collective-permute-start | bytes 1572872 | tf_op jit(solution)/shard_map/ppermute | solution.py:163
  124.4 39.7 %collective-permute-start.11 = (f32[256,768]{1,0:T(8,128)}, f32[256,768]{1,0:T(8,128)}, u32[]{:S(2)}, u32[]{:S(2)}) collective-permute-start(f32[256,768]{1,0:T(8,128)} %slice.129), channel_id=1, source_target_pairs={{16,8},{17,9},{18,10},{19,11},{20,12},{21,13},{22,14},{23,15}} | collective-permute-start | bytes 2359304 | tf_op jit(solution)/shard_map/ppermute | solution.py:163
  130.8 6.7 %copy-start.35 = (f32[256,1024]{1,0:T(8,128)S(1)}, f32[256,1024]{1,0:T(8,128)}, u32[]{:S(2)}) copy-start(f32[256,1024]{1,0:T(8,128)} %copy-done.33) | copy-start | bytes 3145732
  135.5 28.6 %collective-permute-start.12 = (f32[256,512]{1,0:T(8,128)S(1)}, f32[256,512]{1,0:T(8,128)S(1)}, u32[]{:S(2)}, u32[]{:S(2)}) collective-permute-start(f32[256,512]{1,0:T(8,128)S(1)} %get-tuple-element.10), channel_id=1, source_target_pairs={{0,8},{8,16},{16,24},{1,9},{9,17},{17,25},{2,10},{10,18},{18,26},{... | collective-permute-start | bytes 1572872 | tf_op jit(solution)/shard_map/ppermute | solution.py:163
  137.6 30.6 %collective-permute-start.10 = (f32[256,1024]{1,0:T(8,128)S(1)}, f32[256,1024]{1,0:T(8,128)S(1)}, u32[]{:S(2)}, u32[]{:S(2)}) collective-permute-start(f32[256,1024]{1,0:T(8,128)S(1)} %copy-done.35), channel_id=1, source_target_pairs={{24,8},{25,9},{26,10},{27,11},{28,12},{29,13},{30,14},{31,15}} | collective-permute-start | bytes 3145736 | tf_op jit(solution)/shard_map/ppermute | solution.py:163
  166.3 16.4 %copy-start.4 = (f32[256,512]{1,0:T(8,128)}, f32[256,512]{1,0:T(8,128)S(1)}, u32[]{:S(2)}) copy-start(f32[256,512]{1,0:T(8,128)S(1)} %get-tuple-element.20.refs_6_) | copy-start | bytes 1572868
  166.3 15.3 %collective-permute-start.13 = (f32[256,512]{1,0:T(8,128)S(1)}, f32[256,512]{1,0:T(8,128)S(1)}, u32[]{:S(2)}, u32[]{:S(2)}) collective-permute-start(f32[256,512]{1,0:T(8,128)S(1)} %get-tuple-element.19), channel_id=1, source_target_pairs={{0,8},{8,16},{16,24},{1,9},{9,17},{17,25},{2,10},{10,18},{18,26},{... | collective-permute-start | bytes 1572872 | tf_op jit(solution)/shard_map/ppermute | solution.py:163
  182.8 16.6 %collective-permute-start.17 = (f32[512,512]{1,0:T(8,128)S(1)}, f32[512,512]{1,0:T(8,128)S(1)}, u32[]{:S(2)}, u32[]{:S(2)}) collective-permute-start(f32[512,512]{1,0:T(8,128)S(1)} %pad_maximum_fusion.2), channel_id=1, source_target_pairs={{8,0},{9,1},{10,2},{11,3},{12,4},{13,5},{14,6},{15,7}} | collective-permute-start | bytes 3145736 | tf_op jit(solution)/shard_map/ppermute | solution.py:163
  184.0 16.4 %collective-permute-start.16 = (f32[512,512]{1,0:T(8,128)S(1)}, f32[512,512]{1,0:T(8,128)S(1)}, u32[]{:S(2)}, u32[]{:S(2)}) collective-permute-start(f32[512,512]{1,0:T(8,128)S(1)} %pad_maximum_fusion), channel_id=1, source_target_pairs={{8,0},{9,1},{10,2},{11,3},{12,4},{13,5},{14,6},{15,7}} | collective-permute-start | bytes 3145736 | tf_op jit(solution)/shard_map/ppermute | solution.py:163
  184.7 12.5 %collective-permute-start.14 = (f32[256,512]{1,0:T(8,128)S(1)}, f32[256,512]{1,0:T(8,128)S(1)}, u32[]{:S(2)}, u32[]{:S(2)}) collective-permute-start(f32[256,512]{1,0:T(8,128)S(1)} %get-tuple-element.21), channel_id=1, source_target_pairs={{0,8},{8,16},{16,24},{1,9},{9,17},{17,25},{2,10},{10,18},{18,26},{... | collective-permute-start | bytes 1572872 | tf_op jit(solution)/shard_map/ppermute | solution.py:163
  197.2 11.1 %collective-permute-start.15 = (f32[256,512]{1,0:T(8,128)S(1)}, f32[256,512]{1,0:T(8,128)S(1)}, u32[]{:S(2)}, u32[]{:S(2)}) collective-permute-start(f32[256,512]{1,0:T(8,128)S(1)} %collective-permute-done.14.refs_10_.refs_3_), channel_id=1, source_target_pairs={{0,8},{8,16},{16,24},{1,9},{9,17},{17,25},{2,10},{10,18},{18,26},{... | collective-permute-start | bytes 1572872 | tf_op jit(solution)/shard_map/ppermute | solution.py:163
  221.3 18.0 %copy-start.5 = (f32[256,512]{1,0:T(8,128)S(1)}, f32[256,512]{1,0:T(8,128)}, u32[]{:S(2)}) copy-start(f32[256,512]{1,0:T(8,128)} %copy-done.4) | copy-start | bytes 1572868
  249.1 16.7 %copy-start.1 = (f32[8,3,1024,128]{3,2,1,0:T(8,128)S(1)}, f32[8,3,1024,128]{3,2,1,0:T(8,128)}, u32[]{:S(2)}) copy-start(f32[8,3,1024,128]{3,2,1,0:T(8,128)} %all-gather.8.cloned.1.call-done.refs_0_) | copy-start | bytes 37748740
  249.1 16.7 %copy-start.7 = (f32[256,512]{1,0:T(8,128)S(1)}, f32[256,512]{1,0:T(8,128)}, u32[]{:S(2)}) copy-start(f32[256,512]{1,0:T(8,128)} %copy-done.6) | copy-start | bytes 1572868
  249.1 16.7 %copy-start.16 = (f32[256,512]{1,0:T(8,128)S(1)}, f32[256,512]{1,0:T(8,128)}, u32[]{:S(2)}) copy-start(f32[256,512]{1,0:T(8,128)} %copy-done.15) | copy-start | bytes 1572868
  249.1 16.7 %copy-start.19 = (f32[256,512]{1,0:T(8,128)S(1)}, f32[256,512]{1,0:T(8,128)}, u32[]{:S(2)}) copy-start(f32[256,512]{1,0:T(8,128)} %get-tuple-element.4.refs_1_) | copy-start | bytes 1572868
  (25 other events, 44.2 us)
Sparse Core Ops, SparseCore 0:
  10.6 37.7 all-gather.3
  50.3 54.3 all-gather.5
  106.6 72.1 all-gather.7

commit v2 on v0

--- a/solution.py
+++ b/solution.py
@@ -1,15 +1,19 @@
+import functools
+import math
+
 import jax
 import jax.numpy as jnp
 from jax import lax
+from jax.experimental import pallas as pl
+from jax.experimental.pallas import tpu as pltpu
 from jax.sharding import PartitionSpec as P
-
 
 def from_root(value, axis, source):
     kept = jnp.where(lax.axis_index(axis) == source, value, 0).astype(value.dtype)
     return lax.psum(kept, axis)
 
 
-def body(right_side, panel_t, inverse_blocks):
+def plain_body(right_side, panel_t, inverse_blocks):
     grid_rows = lax.axis_size("row")
     my_row = lax.axis_index("row")
     blocks_here = right_side.shape[0]
@@ -38,9 +42,532 @@
     return (jnp.stack(results), right_side)
 
 
+VMEM_LIMIT = 20 * 2**20
+LAG = 2
+
+
+def split(x):
+    hi = x.astype(jnp.bfloat16)
+    return hi, (x - hi.astype(jnp.float32)).astype(jnp.bfloat16)
+
+
+def dot3(a, b_hi, b_lo):
+    a_hi, a_lo = split(a)
+    dot = functools.partial(jnp.dot, preferred_element_type=jnp.float32)
+    return dot(a_hi, b_hi) + (dot(a_hi, b_lo) + dot(a_lo, b_hi))
+
+
+def in_vmem(x):
+    return pltpu.with_memory_space_constraint(x, pltpu.VMEM)
+
+
+ANY = pl.BlockSpec(memory_space=pl.ANY)
+WHOLE = pl.BlockSpec(memory_space=pltpu.VMEM)
+
+
+def distinct(sources):
+    arrays = []
+    where = []
+    for chunks in sources:
+        ids = []
+        for chunk in chunks:
+            for i, a in enumerate(arrays):
+                if a is chunk:
+                    break
+            else:
+                i = len(arrays)
+                arrays.append(chunk)
+            ids.append(i)
+        where.append(ids)
+    return arrays, where
+
+
+def params():
+    return pltpu.CompilerParams(vmem_limit_bytes=VMEM_LIMIT)
+
+
+def cost():
+    return pl.CostEstimate(flops=1024, bytes_accessed=1024, transcendentals=0)
+
+
+def in_hbm(x):
+    return pltpu.with_memory_space_constraint(x, pltpu.HBM)
+
+
+def PIN(x):
+    return x
+
+
+def turn(panel, slabs, after):
+    _, blocks, depth, rows = panel.shape
+    k0, j0 = slabs[0]
+    start = k0 * blocks + j0
+
+    def kernel(in_ref, *refs):
+        refs[-1][0] = in_ref[0, 0].T
+
+    def index(s):
+        at = start + s
+        return (at // blocks, at % blocks, 0, 0)
+
+    return pl.pallas_call(
+        kernel,
+        grid=(len(slabs),),
+        in_specs=[pl.BlockSpec((1, 1, depth, rows), index)] + [ANY] * len(after),
+        out_specs=pl.BlockSpec((1, rows, depth), lambda s: (s, 0, 0)),
+        out_shape=jax.ShapeDtypeStruct((len(slabs), rows, depth), panel.dtype),
+        compiler_params=params(),
+        cost_estimate=cost(),
+    )(in_hbm(panel), *after)
+
+
+def full(shape):
+    return pl.BlockSpec(shape, lambda *_: (0,) * len(shape))
+
+
+def copies(sources, shapes, plan, after):
+    count = len(sources)
+
+    def kernel(*refs):
+        outs, sems = refs[-1 - len(shapes):-1], refs[-1]
+        moves = plan(refs[:count], outs)
+        for act in (True, False):
+            for n, (condition, source, target) in enumerate(moves):
+
+                def go():
+                    copy = pltpu.make_async_copy(source, target, sems.at[n])
+                    copy.start() if act else copy.wait()
+
+                if condition is None:
+                    go()
+                else:
+                    pl.when(condition)(go)
+
+    return pl.pallas_call(
+        kernel,
+        grid=(1,),
+        in_specs=[ANY] * (count + len(after)),
+        out_specs=[full(shape) for shape in shapes],
+        out_shape=[jax.ShapeDtypeStruct(shape, jnp.float32) for shape in shapes],
+        scratch_shapes=[pltpu.SemaphoreType.DMA((16,))],
+        compiler_params=params(),
+        cost_estimate=cost(),
+    )(*[in_hbm(x) for x in sources], *after)
+
+
+def slot(inverse, k, rhs, received, top, part, after):
+    if len(inverse) == 1:
+        _, chunk, _ = inverse[0].shape
+        depth = (part - LAG - k * (inverse[0].shape[2] // chunk) + 1) * chunk
+        specs = [pl.BlockSpec((1, chunk, depth), lambda s: (k, 0, 0))]
+        inverse = [in_hbm(inverse[0])]
+    else:
+        half, depth = inverse[0].shape
+        chunk = 2 * half
+        specs = [full((half, depth))] * 2
+    cols = received.shape[1]
+    tops = [] if top is None else [in_hbm(top)]
+
+    def kernel(*refs):
+        inverse_refs, refs = refs[: len(inverse)], refs[len(inverse):]
+        received_ref, refs = refs[0], refs[1:]
+        rhs_refs, refs = refs[: len(rhs)], refs[len(rhs):]
+        out_ref, whole, sems = refs[-3:]
+        my_row = lax.axis_index("row")
+
+        def move(source, target, n=0):
+            return pltpu.make_async_copy(source, target, sems.at[n])
+
+        if tops:
+
+            @pl.when(my_row == 0)
+            def _():
+                copy = move(refs[0].at[0, pl.ds(part * chunk, chunk)], out_ref)
+                copy.start()
+                copy.wait()
+
+        @pl.when(my_row == 1)
+        def _():
+            moves = []
+            for n, ref in enumerate(rhs_refs):
+                if len(rhs) == 1 and rhs[0].ndim == 3:
+                    moves.append(move(ref.at[0, pl.ds(0, depth)], whole))
+                else:
+                    moves.append(move(ref, whole.at[pl.ds(n * chunk, chunk)], n))
+            for copy in moves:
+                copy.start()
+            for copy in moves:
+                copy.wait()
+            high, low = split(whole[...])
+            if len(inverse) == 1:
+                out_ref[...] = dot3(inverse_refs[0][0], high, low)
+            else:
+                core = lax.rem(lax.axis_index("col"), 2)
+                for p, ref in enumerate(inverse_refs):
+                    at = pl.multiple_of((core if p == 0 else 1 - core) * half, half)
+                    out_ref[pl.ds(at, half)] = dot3(ref[...], high, low)
+
+        @pl.when(my_row > 1)
+        def _():
+            copy = move(received_ref, out_ref)
+            copy.start()
+            copy.wait()
+
+    return pl.pallas_call(
+        kernel,
+        grid=(1,),
+        in_specs=specs + [ANY] * (1 + len(rhs) + len(tops) + len(after)),
+        out_specs=full((chunk, cols)),
+        out_shape=jax.ShapeDtypeStruct((chunk, cols), jnp.float32),
+        scratch_shapes=[
+            pltpu.VMEM((depth, cols), jnp.float32),
+            pltpu.SemaphoreType.DMA((len(rhs),)),
+        ],
+        compiler_params=params(),
+        cost_estimate=cost(),
+    )(*inverse, received, *rhs, *tops, *after)
+
+
+def fetch(where, refs, whole, sems, height, my_row):
+    for row, ids in enumerate(where):
+
+        @pl.when((my_row == row) | (len(where) == 1))
+        def _():
+            copies = [
+                pltpu.make_async_copy(refs[i], whole.at[pl.ds(n * height, height)], sems.at[n])
+                for n, i in enumerate(ids)
+            ]
+            for copy in copies:
+                copy.start()
+            for copy in copies:
+                copy.wait()
+
+
+def update(rhs, k, parts, sources, after, js, first=False, fresh=False, solved=None):
+    heads = rhs if isinstance(rhs, list) else [rhs]
+    _, rows, cols = heads[0].shape
+    blocks = sum(h.shape[0] for h in heads)
+    tile = 512
+    steps = rows // tile
+    arrays, where = distinct(sources)
+    height = arrays[0].shape[0]
+    depth = height * len(where[0])
+    given, given_where = distinct([a + b for a, b in zip(*solved)]) if solved else ([], [])
+    last = len(given) > 0
+    panels = []
+    panel_specs = []
+    spans = []
+    for panel, begin, end, piece, piece_end, _, slab in parts:
+
+        def place(s, begin=begin, end=end, slab=slab):
+            at = jnp.clip(s - (begin - js[0]) * steps, 0, (end - begin) * steps - 1)
+            return slab + at // steps, at % steps
+
+        at = len(panels)
+        if isinstance(panel, tuple):
+            for group in range(piece // 2, piece_end // 2):
+
+                def index(s, col, group=group, place=place):
+                    return (lax.bitwise_xor(col[0] // 2, group), *place(s), 0)
+
+                for one in panel:
+                    panels.append(one)
+                    panel_specs.append(pl.BlockSpec((1, 1, tile, one.shape[3]), index))
+        else:
+            count = piece_end - piece
+
+            def index(s, col, which=piece // count, place=place):
+                return (which, *place(s), 0)
+
+            panels.append(panel)
+            panel_specs.append(pl.BlockSpec((count, 1, tile, panel.shape[3]), index))
+        spans.append((at, len(panels)))
+
+    def kernel(col_ref, *refs):
+        rhs_refs, refs = refs[: len(heads)], refs[len(heads):]
+        panel_refs, refs = refs[: len(panels)], refs[len(panels):]
+        chunk_refs, refs = refs[: len(arrays)], refs[len(arrays):]
+        given_refs, refs = refs[: len(given)], refs[len(given):]
+        refs = refs[len(after):]
+        out_ref, refs = refs[0], refs[1:]
+        if last:
+            solved_ref, refs = refs[0], refs[1:]
+        whole, x_hi, x_lo, sems = refs[:4]
+        step = pl.program_id(0)
+        my_row = lax.axis_index("row")
+
+        def give(act):
+            for row, ids in enumerate(given_where):
+
+                @pl.when(my_row == row)
+                def _():
+                    each = len(ids) // 2
+                    for n, i in enumerate(ids):
+                        target = solved_ref.at[n // each, pl.ds((n % each) * height, height)]
+                        copy = pltpu.make_async_copy(given_refs[i], target, refs[4].at[n])
+                        copy.start() if act else copy.wait()
+
+        @pl.when(step == 0)
+        def _():
+            fetch(where, chunk_refs, whole, sems, height, my_row)
+            hi, lo = split(whole[...])
+            x_hi[...] = hi
+            x_lo[...] = lo
+            if last:
+                give(True)
+
+        j = js[0] + step // steps
+        old = rhs_refs[0][0]
+        for h, ref in enumerate(rhs_refs[1:]):
+            old = jnp.where(j >= heads[0].shape[0], ref[0], old)
+        live = j * len(where) + my_row > k
+        done = j < 0
+        for (panel, begin, end, piece, piece_end, row, _), (at, stop) in zip(parts, spans):
+            active = live & (j >= begin) & (j < end)
+            done |= active
+
+            @pl.when(active)
+            def _():
+                if isinstance(panel, tuple):
+                    even = lax.rem(col_ref[0], 2) == 0
+                    pieces = []
+                    for mine, other in zip(panel_refs[at:stop:2], panel_refs[at + 1:stop:2]):
+                        a, b = mine[0, 0], other[0, 0]
+                        pieces += [jnp.where(even, a, b), jnp.where(even, b, a)]
+                else:
+                    pieces = [panel_refs[at][p, 0] for p in range(piece_end - piece)]
+                left = jnp.concatenate(pieces, axis=1)
+                span = slice(row, row + left.shape[1])
+                out_ref[0] = old - dot3(left, x_hi[span], x_lo[span])
+
+        @pl.when(jnp.logical_not(done))
+        def _():
+            out_ref[0] = old
+
+        if last:
+
+            @pl.when(step == (js[1] - js[0]) * steps - 1)
+            def _():
+                give(False)
+
+    block = pl.BlockSpec((1, tile, cols), lambda s, col: (js[0] + s // steps, s % steps, 0))
+    kind = heads[0].dtype
+    shape = (blocks, rows, cols)
+    out_shape = [jax.ShapeDtypeStruct(shape, kind) if last else pltpu.HBM(shape, kind)]
+    out_specs = [block]
+    rhs_specs = [block]
+    if len(heads) == 2:
+        edge = heads[0].shape[0] * steps
+
+        def before(s, col):
+            at = jnp.minimum(s, edge - 1)
+            return (at // steps, at % steps, 0)
+
+        def beyond(s, col):
+            at = jnp.maximum(s - edge, 0)
+            return (at // steps, at % steps, 0)
+
+        rhs_specs = [pl.BlockSpec((1, tile, cols), f) for f in (before, beyond)]
+    if fresh:
+        out_shape = [jax.ShapeDtypeStruct((js[1] - js[0], rows, cols), kind)]
+        out_specs = [pl.BlockSpec((1, tile, cols), lambda s, col: (s // steps, s % steps, 0))]
+    scratch = [
+        pltpu.VMEM((depth, cols), jnp.float32),
+        pltpu.VMEM((depth, cols), jnp.bfloat16),
+        pltpu.VMEM((depth, cols), jnp.bfloat16),
+        pltpu.SemaphoreType.DMA((len(where[0]),)),
+    ]
+    if last:
+        out_shape.append(
+            jax.ShapeDtypeStruct((2, height * len(given_where[0]) // 2, cols), kind)
+        )
+        out_specs.append(full(out_shape[-1].shape))
+        scratch.append(pltpu.SemaphoreType.DMA((len(given_where[0]),)))
+    outs = pl.pallas_call(
+        kernel,
+        grid_spec=pltpu.PrefetchScalarGridSpec(
+            num_scalar_prefetch=1,
+            grid=((js[1] - js[0]) * steps,),
+            in_specs=rhs_specs + panel_specs + [ANY] * (len(arrays) + len(given) + len(after)),
+            out_specs=out_specs,
+            scratch_shapes=scratch,
+        ),
+        out_shape=out_shape,
+        input_output_aliases={} if first or last or fresh else {1: 0},
+        compiler_params=params(),
+        cost_estimate=cost(),
+    )(
+        lax.axis_index("col").astype(jnp.int32).reshape(1),
+        *[in_hbm(h) for h in heads],
+        *[in_hbm(panel) for panel in panels],
+        *[in_hbm(a) for a in arrays + given],
+        *after,
+    )
+    return outs if last else outs[0]
+
+
+def body(right_side, panel_t, inverse_blocks):
+    n_row = lax.axis_size("row")
+    n_col = lax.axis_size("col")
+    blocks, _, cols = right_side.shape
+    share = inverse_blocks.shape[1]
+    half = share // 2
+    n = inverse_blocks.shape[2] // share
+    others = [q for q in range(n_row) if q != 1]
+
+    def send(value, pairs):
+        return lax.ppermute(value, "row", pairs)
+
+    def swap(value):
+        return lax.ppermute(value, "col", [(d, d ^ 1) for d in range(n_col)])
+
+    def onward(value, t):
+        rows = [0] if t < n else []
+        rows += [r for r in range(1, n_row - 1) if 0 <= t - LAG * r < 2 * n]
+        return send(value, [(r, r + 1) for r in rows])
+
+    halves = [(half, (q + 1) * share) for q in others]
+
+    def cut(k):
+        def plan(refs, outs):
+            my_row = lax.axis_index("row")
+            at = pl.multiple_of(lax.rem(lax.axis_index("col"), 2) * half, half)
+            return [
+                (my_row == q, refs[0].at[k, pl.ds(at, half), pl.ds(0, (q + 1) * share)], out)
+                for q, out in zip(others, outs)
+            ]
+
+        return plan
+
+    def start(refs, outs):
+        return cut(0)(refs, outs) + [
+            (
+                lax.axis_index("row") == 0,
+                refs[1].at[0, pl.ds(t * share, share)],
+                outs[len(others) + t],
+            )
+            for t in range(LAG)
+        ]
+
+    def to_solver(parts):
+        return [send(part, [(q, 1)]) for q, part in zip(others, parts)]
+
+    def whole(k, parts):
+        inverse = [[part, swap(part)] for part in parts]
+        inverse.insert(1, [inverse_blocks])
+        return inverse
+
+    slots = 2 * n + LAG * (n_row - 2)
+    *parts, sent0, sent1 = copies(
+        [inverse_blocks, right_side], halves + [(share, cols)] * LAG, start, []
+    )
+    sent = [sent0, sent1]
+    received = [onward(sent[0], 0), onward(sent[1], 1)]
+    arrived = to_solver(parts)
+    inverse = [whole(0, arrived), None]
+
+    slabs = jnp.transpose(panel_t, (0, 2, 1, 3))
+    gathered = []
+    for k in range(2):
+        turned = turn(slabs, [(k, j) for j in range(blocks)], [sent0])
+        gathered.append(lax.all_gather(turned, "col"))
+
+    remaining = right_side
+    lowered = None
+    solved_here = [[], []]
+    back = [[], []]
+    after = arrived
+
+    def chunks_of(k, first, end):
+        rows_of = [back[k], solved_here[k]] + [
+            received[k * n + LAG * (r - 1):][:n] for r in range(2, n_row)
+        ]
+        return [c[first:end] for c in rows_of]
+
+    def to_first(k, first, end):
+        both = send(jnp.concatenate(solved_here[k][first:end], axis=0), [(1, 0)])
+        back[k] += [both[i * share:(i + 1) * share] for i in range(end - first)]
+
+    late = LAG * (n_row - 2)
+    for t in range(LAG, slots + LAG):
+        value = received[t - LAG]
+        k, q = divmod(t - LAG, n)
+        if t < slots:
+            if k < 2:
+                rhs = received[: q + 1] if k == 0 else [lowered]
+                top = right_side if t < n else None
+                sent.append(slot(inverse[k][q], k, rhs, value, top, t, after))
+                solved_here[k].append(sent[t])
+            else:
+                sent.append(value)
+            received.append(onward(sent[t], t))
+            after = []
+        here = [sent[t]] if t < slots else []
+        if t == LAG:
+            arrived = to_solver(copies([inverse_blocks], halves, cut(1), here))
+            inverse[1] = whole(1, arrived)
+        if t == 2 * LAG:
+            after = arrived
+        if t == n + LAG - 1:
+            lowered = update(
+                right_side,
+                -1,
+                [(gathered[0], 0, 1, 0, n_col, 0, 0)],
+                [solved_here[0]],
+                here,
+                (0, 1),
+                fresh=True,
+            )
+            after = [lowered]
+        if t == n + LAG:
+            to_first(0, 0, n)
+        if t in (n + LAG + 1, n + LAG + 3):
+            to_first(1, t - n - LAG - 1, t - n - LAG + 1)
+        ready = t - LAG - late
+        if ready == n - 1:
+            remaining = update(
+                remaining,
+                0,
+                [(gathered[0], 0, 2, 0, n_col, 0, 0)],
+                chunks_of(0, 0, n),
+                here,
+                (0, 2),
+                fresh=True,
+            )
+            after = [remaining]
+        if ready == n:
+            third = update(
+                right_side,
+                0,
+                [(gathered[0], 2, 3, 0, n_col, 0, 2)],
+                chunks_of(0, 0, n),
+                here,
+                (2, 3),
+                fresh=True,
+            )
+            after = [third]
+    remaining, solved = update(
+        [remaining, third],
+        1,
+        [(gathered[1], 0, blocks, 0, n_col, 0, 0)],
+        chunks_of(1, 0, n),
+        [],
+        (0, blocks),
+        solved=[[chunks_of(k, r, r + 1)[r] for r in range(n_row)] for k in range(2)],
+    )
+    return (solved, remaining)
+
+
+def choose(right_side, panel_t, inverse_blocks):
+    plane = lax.axis_size("col") == 8 and panel_t.shape[1] == 128
+    if plane and inverse_blocks.shape[1] == 256 and lax.axis_size("row") == 4:
+        return body(right_side, panel_t, inverse_blocks)
+    return plain_body(right_side, panel_t, inverse_blocks)
+
+
 def solution(mesh):
     return jax.shard_map(
-        body,
+        choose,
         mesh=mesh,
         in_specs=(P(None, "row", "col"), P(None, "col", None, "row"), P(None, "row", None)),
         out_specs=(P(None, "row", "col"), P(None, "row", "col")),

time: 504 us -> 211 us (0.42)
  waiting for transfers between devices: 402 us -> 84.3 us
  Pallas kernels: 0 us -> 59.3 us
  matrix products: 58.5 us -> 0 us
  starting transfers between devices: 0.42 us -> 39 us
  local copies, waits for them, and re-layouts: 19 us -> 10.6 us
    all_gather x4 -> x2, waiting for transfers between devices: 230 us -> 4.64 us  [body(): gathered.append(lax.all_gather(turned, 'col'))]
    psum x2 -> x0, waiting for transfers between devices: 171 us -> none  [from_root(): return lax.psum(kept, axis)]
    ppermute x0 -> x27, waiting for transfers between devices: none -> 79.7 us  [the longest x21 78 us: send(): return lax.ppermute(value, 'row', pairs)]
    pallas_call x0 -> x16, Pallas kernels: none -> 59.3 us  [the longest x4 45.6 us: update(): pl.pallas_call(kernel, grid_spec=pltpu.PrefetchScalarGridSpec(num_scalar_...]
    dot_general x4 -> x0, matrix products: 58.5 us -> none  [the longest x2 49.8 us: body(): jnp.einsum('cji,cr->jir', lax.all_gather(panel_t[k], 'col', axis=0, tiled...]
    ppermute x0 -> x27, starting transfers between devices: none -> 39 us  [the longest x21 37.7 us: send(): return lax.ppermute(value, 'row', pairs)]
    unnamed x11 -> x40, local copies, waits for them, and re-layouts: 17.1 us -> 5.62 us
  transfers between devices with their start and end apart: 6 -> 29, of which waited for: 6 -> 12; matrix products, arithmetic and copies ran while one was open for 2% -> 3% of each run, Pallas kernels for 0% -> 17%
where the time goes in v2:
time: 211 us; the launch traced here: 210 us
  waiting for transfers between devices  84.3 us (40%)
  Pallas kernels  59.3 us (28%)
  starting transfers between devices  39 us (18%)
  between operations  14.6 us (7%)
  local copies, waits for them, and re-layouts  10.6 us (5%)
    ppermute x21, waiting for transfers between devices, send(): return lax.ppermute(value, 'row', pairs)  78 us
    pallas_call x4, Pallas kernels, update(): pl.pallas_call(kernel, grid_spec=pltpu.PrefetchScalarGridSpec(num_scalar_...  45.6 us
    ppermute x21, starting transfers between devices, send(): return lax.ppermute(value, 'row', pairs)  37.7 us
    pallas_call x2, Pallas kernels, turn(): pl.pallas_call(kernel, grid=(len(slabs),), in_specs=[pl.BlockSpec((1, 1,...  7.43 us
    unnamed x40, local copies, waits for them, and re-layouts  5.62 us
    slice x3, local copies, waits for them, and re-layouts, to_first(): back[k] += [both[i * share:(i + 1) * share] for i in range(end - first)]  5.01 us
    all_gather x2, waiting for transfers between devices, body(): gathered.append(lax.all_gather(turned, 'col'))  4.64 us
  transfers between devices with their start and end apart: 29, of which 12 were waited for; matrix products, arithmetic and copies ran while one was open for 3% of the time, Pallas kernels for 17%

profile of v2, /device:TPU:18, one launch (start us, length us, event | category | flops | bytes accessed | tf_op | source)
XLA Modules:
  0.0 209.6 jit_solution(18172295011784065035)
XLA Ops:
  8.4 3.7 %shard_map.51 = f32[3,1024,128]{2,1,0:T(8,128)} custom-call(f32[2,3,128,1024]{3,2,1,0:T(8,128)} %bitcast.7, f32[256,512]{1,0:T(8,128)S(1)} %get-tuple-element.12.refs_0_), custom_call_target="tpu_custom_call" | custom-call | flops 1024 | bytes 1024 | tf_op jit(solution)/shard_map/pallas_call | solution.py:113
  12.2 3.7 %shard_map.64 = f32[3,1024,128]{2,1,0:T(8,128)} custom-call(f32[2,3,128,1024]{3,2,1,0:T(8,128)} %bitcast.8, f32[256,512]{1,0:T(8,128)S(1)} %get-tuple-element.12.refs_0_), custom_call_target="tpu_custom_call" | custom-call | flops 1024 | bytes 1024 | tf_op jit(solution)/shard_map/pallas_call | solution.py:113
  17.3 2.6 %collective-permute-start.3 = (f32[128,768]{1,0:T(8,128)S(1)}, f32[128,768]{1,0:T(8,128)S(1)}, u32[]{:S(2)}, u32[]{:S(2)}) collective-permute-start(f32[128,768]{1,0:T(8,128)S(1)} %get-tuple-element.14), channel_id=1, source_target_pairs={{16,8},{17,9},{18,10},{19,11},{20,12},{21,13},{22,14},{23,15}} | collective-permute-start | bytes 1179656 | tf_op jit(solution)/shard_map/ppermute | solution.py:419
  21.4 17.7 %collective-permute-done.3.refs_6_.refs_0_ = f32[128,768]{1,0:T(8,128)S(1)} collective-permute-done((f32[128,768]{1,0:T(8,128)S(1)}, f32[128,768]{1,0:T(8,128)S(1)}, u32[]{:S(2)}, u32[]{:S(2)}) %collective-permute-start.3) | collective-permute-done | bytes 393248 | tf_op jit(solution)/shard_map/ppermute | solution.py:419
  45.3 10.7 %collective-permute-start.11 = (f32[128,768]{1,0:T(8,128)S(1)}, f32[128,768]{1,0:T(8,128)S(1)}, u32[]{:S(2)}, u32[]{:S(2)}) collective-permute-start(f32[128,768]{1,0:T(8,128)S(1)} %get-tuple-element.18), channel_id=1, source_target_pairs={{16,8},{17,9},{18,10},{19,11},{20,12},{21,13},{22,14},{23,15}} | collective-permute-start | bytes 1179656 | tf_op jit(solution)/shard_map/ppermute | solution.py:419
  56.0 5.4 %collective-permute-done.7.refs_2_.refs_5_.refs_10_ = f32[256,512]{1,0:T(8,128)S(1)} collective-permute-done((f32[256,512]{1,0:T(8,128)S(1)}, f32[256,512]{1,0:T(8,128)S(1)}, u32[]{:S(2)}, u32[]{:S(2)}) %collective-permute-start.7) | collective-permute-done | bytes 524320 | tf_op jit(solution)/shard_map/ppermute | solution.py:419
  62.2 9.4 %collective-permute-done.11.refs_8_.refs_0_ = f32[128,768]{1,0:T(8,128)S(1)} collective-permute-done((f32[128,768]{1,0:T(8,128)S(1)}, f32[128,768]{1,0:T(8,128)S(1)}, u32[]{:S(2)}, u32[]{:S(2)}) %collective-permute-start.11) | collective-permute-done | bytes 393248 | tf_op jit(solution)/shard_map/ppermute | solution.py:419
  72.9 1.5 pad_maximum_fusion
  74.4 2.0 collective-permute-start.13
  76.4 1.9 collective-permute-start.14
  78.3 1.9 collective-permute-start.15
  80.8 4.6 %all-gather.5.cloned.1.call-done = f32[24,1024,128]{2,1,0:T(8,128)} async-done(((f32[3,1024,128]{2,1,0:T(8,128)}), f32[24,1024,128]{2,1,0:T(8,128)}) %all-gather.5.cloned.1.call-update) | async-done | bytes 12582928 | tf_op jit(solution)/shard_map/all_gather | solution.py:473
  85.5 7.8 %shard_map.57.refs_3_.refs_4_.refs_2_ = f32[1,1024,512]{2,1,0:T(8,128)S(1)} custom-call(s32[1]{0:T(128)} %bitcast.col_ref, f32[3,1024,512]{2,1,0:T(8,128)} %refs_0_.13, f32[8,3,1024,128]{3,2,1,0:T(8,128)} %bitcast.4, f32[256,512]{1,0:T(8,128)} %copy-done.1, f32[256,512]{1,0:T(8,128)} %copy-done, f32[256,512]{1,0:T(8,128)} %copy-done.6, ...), custom_call_target="tpu_custom_call" | custom-call | flops 1024 | bytes 1024 | tf_op jit(solution)/shard_map/pallas_call | solution.py:386
  93.3 2.9 %collective-permute-done.14.refs_2_.refs_12_.refs_21_ = f32[256,512]{1,0:T(8,128)S(1)} collective-permute-done((f32[256,512]{1,0:T(8,128)S(1)}, f32[256,512]{1,0:T(8,128)S(1)}, u32[]{:S(2)}, u32[]{:S(2)}) %collective-permute-start.14) | collective-permute-done | bytes 524320 | tf_op jit(solution)/shard_map/ppermute | solution.py:419
  97.0 1.9 collective-permute-start.17
  98.9 8.5 %collective-permute-done.15.refs_1_.refs_13_ = f32[256,512]{1,0:T(8,128)S(1)} collective-permute-done((f32[256,512]{1,0:T(8,128)S(1)}, f32[256,512]{1,0:T(8,128)S(1)}, u32[]{:S(2)}, u32[]{:S(2)}) %collective-permute-start.15) | collective-permute-done | bytes 524320 | tf_op jit(solution)/shard_map/ppermute | solution.py:419
  108.8 1.9 collective-permute-start.18
  110.9 1.6 collective-permute-done.20.refs_1_
  113.2 5.5 %collective-permute-done.17.refs_14_.refs_2_.refs_11_ = f32[256,512]{1,0:T(8,128)S(1)} collective-permute-done((f32[256,512]{1,0:T(8,128)S(1)}, f32[256,512]{1,0:T(8,128)S(1)}, u32[]{:S(2)}, u32[]{:S(2)}) %collective-permute-start.17) | collective-permute-done | bytes 524320 | tf_op jit(solution)/shard_map/ppermute | solution.py:419
  118.8 9.9 %collective-permute-done.18.refs_2_.refs_15_.refs_12_.refs_23_ = f32[256,512]{1,0:T(8,128)S(1)} collective-permute-done((f32[256,512]{1,0:T(8,128)S(1)}, f32[256,512]{1,0:T(8,128)S(1)}, u32[]{:S(2)}, u32[]{:S(2)}) %collective-permute-start.18) | collective-permute-done | bytes 524320 | tf_op jit(solution)/shard_map/ppermute | solution.py:419
  130.8 1.9 collective-permute-start.21
  132.7 2.1 %collective-permute-start.24 = (f32[256,512]{1,0:T(8,128)S(1)}, f32[256,512]{1,0:T(8,128)S(1)}, u32[]{:S(2)}, u32[]{:S(2)}) collective-permute-start(f32[256,512]{1,0:T(8,128)S(1)} %shard_map.60.refs_16_.refs_10_), channel_id=1, source_target_pairs={{8,16},{16,24},{9,17},{17,25},{10,18},{18,26},{11,19},{19,27},{12,... | collective-permute-start | bytes 1572872 | tf_op jit(solution)/shard_map/ppermute | solution.py:419
  134.8 2.9 %fusion = (f32[256,512]{1,0:T(8,128)}, f32[256,512]{1,0:T(8,128)}, f32[256,512]{1,0:T(8,128)}, f32[256,512]{1,0:T(8,128)}) fusion(f32[1024,512]{1,0:T(8,128)} %collective-permute-done.13), kind=kLoop, calls=%fused_computation.3 | loop fusion | bytes 4194304 | tf_op jit(solution)/shard_map/slice | solution.py:489
  137.7 11.7 %shard_map.61.refs_0_ = f32[2,1024,512]{2,1,0:T(8,128)S(1)} custom-call(s32[1]{0:T(128)} %bitcast.col_ref, f32[3,1024,512]{2,1,0:T(8,128)} %refs_0_.13, f32[8,3,1024,128]{3,2,1,0:T(8,128)} %bitcast.5, f32[256,512]{1,0:T(8,128)} %get-tuple-element.25.refs_2_.refs_17_, f32[256,512]{1,0:T(8,128)} %get-tuple-element.24.refs_3_, ...), custom_call_target="tpu_custom_call" | custom-call | flops 1024 | bytes 1024 | tf_op jit(solution)/shard_map/pallas_call | solution.py:386
  149.4 2.1 copy-done.3
  151.5 8.1 %shard_map.63.refs_1_ = f32[1,1024,512]{2,1,0:T(8,128)S(1)} custom-call(s32[1]{0:T(128)} %bitcast.col_ref, f32[3,1024,512]{2,1,0:T(8,128)} %refs_0_.13, f32[8,3,1024,128]{3,2,1,0:T(8,128)} %bitcast.6, f32[256,512]{1,0:T(8,128)} %get-tuple-element.25.refs_2_.refs_17_, f32[256,512]{1,0:T(8,128)} %get-tuple-element.24.refs_3_, ...), custom_call_target="tpu_custom_call" | custom-call | flops 1024 | bytes 1024 | tf_op jit(solution)/shard_map/pallas_call | solution.py:386
  159.6 1.3 copy-done.12
  160.8 1.3 collective-permute-start.25
  162.2 1.3 collective-permute-start.26
  165.7 8.8 %collective-permute-done.25.refs_15_ = f32[256,512]{1,0:T(8,128)S(1)} collective-permute-done((f32[256,512]{1,0:T(8,128)S(1)}, f32[256,512]{1,0:T(8,128)S(1)}, u32[]{:S(2)}, u32[]{:S(2)}) %collective-permute-start.25) | collective-permute-done | bytes 524320 | tf_op jit(solution)/shard_map/ppermute | solution.py:419
  174.5 9.4 %collective-permute-done.26.refs_16_.refs_24_ = f32[256,512]{1,0:T(8,128)S(1)} collective-permute-done((f32[256,512]{1,0:T(8,128)S(1)}, f32[256,512]{1,0:T(8,128)S(1)}, u32[]{:S(2)}, u32[]{:S(2)}) %collective-permute-start.26) | collective-permute-done | bytes 524320 | tf_op jit(solution)/shard_map/ppermute | solution.py:419
  184.7 18.1 %shard_map.65 = (f32[3,1024,512]{2,1,0:T(8,128)}, f32[2,256,512]{2,1,0:T(8,128)}) custom-call(s32[1]{0:T(128)} %bitcast.col_ref, f32[2,1024,512]{2,1,0:T(8,128)} %copy-done.3, f32[1,1024,512]{2,1,0:T(8,128)} %copy-done.12, f32[8,3,1024,128]{3,2,1,0:T(8,128)} %bitcast.9, f32[256,512]{1,0:T(8,128)} %get-tuple-element.29.refs_3_.refs_18_, ...), custom_call_target="tpu_custom_call" | custom-call | flops 1024 | bytes 1024 | tf_op jit(solution)/shard_map/pallas_call | solution.py:386
  (90 shorter events, 20.9 us)
Async XLA Ops:
  7.2 78.3 %all-gather.5.cloned.1.call-start = ((), (), s32[]{:S(2)}) async-start(), calls=%async_computation | async-start | bytes 14155776 | tf_op jit(solution)/shard_map/all_gather | solution.py:473
  12.1 153.6 %all-gather.7.cloned.1.call-start = ((), (), s32[]{:S(2)}) async-start(), calls=%async_computation.1 | async-start | bytes 14155776 | tf_op jit(solution)/shard_map/all_gather | solution.py:473
  15.9 23.2 %collective-permute-start.2 = (f32[256,512]{1,0:T(8,128)S(1)}, f32[256,512]{1,0:T(8,128)S(1)}, u32[]{:S(2)}, u32[]{:S(2)}) collective-permute-start(f32[256,512]{1,0:T(8,128)S(1)} %get-tuple-element.12.refs_0_), channel_id=1, source_target_pairs={{0,8},{1,9},{2,10},{3,11},{4,12},{5,13},{6,14},{7,15}} | collective-permute-start | bytes 1572872 | tf_op jit(solution)/shard_map/ppermute | solution.py:419
  16.6 22.5 %collective-permute-start.4 = (f32[128,1024]{1,0:T(8,128)S(1)}, f32[128,1024]{1,0:T(8,128)S(1)}, u32[]{:S(2)}, u32[]{:S(2)}) collective-permute-start(f32[128,1024]{1,0:T(8,128)S(1)} %get-tuple-element.15), channel_id=1, source_target_pairs={{24,8},{25,9},{26,10},{27,11},{28,12},{29,13},{30,14},{31,15}} | collective-permute-start | bytes 1572872 | tf_op jit(solution)/shard_map/ppermute | solution.py:419
  17.3 21.8 %collective-permute-start.3 = (f32[128,768]{1,0:T(8,128)S(1)}, f32[128,768]{1,0:T(8,128)S(1)}, u32[]{:S(2)}, u32[]{:S(2)}) collective-permute-start(f32[128,768]{1,0:T(8,128)S(1)} %get-tuple-element.14), channel_id=1, source_target_pairs={{16,8},{17,9},{18,10},{19,11},{20,12},{21,13},{22,14},{23,15}} | collective-permute-start | bytes 1179656 | tf_op jit(solution)/shard_map/ppermute | solution.py:419
  19.9 22.4 %collective-permute-start.5 = (f32[256,512]{1,0:T(8,128)S(1)}, f32[256,512]{1,0:T(8,128)S(1)}, u32[]{:S(2)}, u32[]{:S(2)}) collective-permute-start(f32[256,512]{1,0:T(8,128)S(1)} %get-tuple-element.16), channel_id=1, source_target_pairs={{0,8},{1,9},{2,10},{3,11},{4,12},{5,13},{6,14},{7,15}} | collective-permute-start | bytes 1572872 | tf_op jit(solution)/shard_map/ppermute | solution.py:419
  20.6 0.7 collective-permute-start
  21.3 17.8 %collective-permute-start.1 = (f32[128,256]{1,0:T(8,128)S(1)}, f32[128,256]{1,0:T(8,128)S(1)}, u32[]{:S(2)}, u32[]{:S(2)}) collective-permute-start(f32[128,256]{1,0:T(8,128)S(1)} %collective-permute-done.refs_0_.refs_5_), channel_id=1, source_target_pairs={{0,1},{1,0},{2,3},{3,2},{4,5},{5,4},{6,7},{7,6},{8,9},{9,8},{10,11... | collective-permute-start | bytes 393224 | tf_op jit(solution)/shard_map/ppermute | solution.py:422
  39.1 6.3 %collective-permute-start.6 = (f32[128,768]{1,0:T(8,128)S(1)}, f32[128,768]{1,0:T(8,128)S(1)}, u32[]{:S(2)}, u32[]{:S(2)}) collective-permute-start(f32[128,768]{1,0:T(8,128)S(1)} %collective-permute-done.3.refs_6_.refs_0_), channel_id=1, source_target_pairs={{0,1},{1,0},{2,3},{3,2},{4,5},{5,4},{6,7},{7,6},{8,9},{9,8},{10,11... | collective-permute-start | bytes 1179656 | tf_op jit(solution)/shard_map/ppermute | solution.py:422
  39.2 33.1 %copy-start.1 = (f32[256,512]{1,0:T(8,128)}, f32[256,512]{1,0:T(8,128)S(1)}, u32[]{:S(2)}) copy-start(f32[256,512]{1,0:T(8,128)S(1)} %shard_map.52.refs_1_.refs_2_.refs_6_) | copy-start | bytes 1572868
  39.2 22.2 %collective-permute-start.7 = (f32[256,512]{1,0:T(8,128)S(1)}, f32[256,512]{1,0:T(8,128)S(1)}, u32[]{:S(2)}, u32[]{:S(2)}) collective-permute-start(f32[256,512]{1,0:T(8,128)S(1)} %shard_map.52.refs_1_.refs_2_.refs_6_), channel_id=1, source_target_pairs={{0,8},{8,16},{1,9},{9,17},{2,10},{10,18},{3,11},{11,19},{4,12},{12... | collective-permute-start | bytes 1572872 | tf_op jit(solution)/shard_map/ppermute | solution.py:419
  41.6 30.0 %collective-permute-start.12 = (f32[128,1024]{1,0:T(8,128)S(1)}, f32[128,1024]{1,0:T(8,128)S(1)}, u32[]{:S(2)}, u32[]{:S(2)}) collective-permute-start(f32[128,1024]{1,0:T(8,128)S(1)} %get-tuple-element.19), channel_id=1, source_target_pairs={{24,8},{25,9},{26,10},{27,11},{28,12},{29,13},{30,14},{31,15}} | collective-permute-start | bytes 1572872 | tf_op jit(solution)/shard_map/ppermute | solution.py:419
  43.5 28.8 %copy-start = (f32[256,512]{1,0:T(8,128)}, f32[256,512]{1,0:T(8,128)S(1)}, u32[]{:S(2)}) copy-start(f32[256,512]{1,0:T(8,128)S(1)} %shard_map.53.refs_3_.refs_7_.refs_19_) | copy-start | bytes 1572868
  43.5 28.7 %collective-permute-start.9 = (f32[256,512]{1,0:T(8,128)S(1)}, f32[256,512]{1,0:T(8,128)S(1)}, u32[]{:S(2)}, u32[]{:S(2)}) collective-permute-start(f32[256,512]{1,0:T(8,128)S(1)} %shard_map.53.refs_3_.refs_7_.refs_19_), channel_id=1, source_target_pairs={{0,8},{8,16},{1,9},{9,17},{2,10},{10,18},{3,11},{11,19},{4,12},{12... | collective-permute-start | bytes 1572872 | tf_op jit(solution)/shard_map/ppermute | solution.py:419
  44.8 27.4 %collective-permute-start.8 = (f32[128,1024]{1,0:T(8,128)S(1)}, f32[128,1024]{1,0:T(8,128)S(1)}, u32[]{:S(2)}, u32[]{:S(2)}) collective-permute-start(f32[128,1024]{1,0:T(8,128)S(1)} %collective-permute-done.4.refs_7_.refs_0_), channel_id=1, source_target_pairs={{0,1},{1,0},{2,3},{3,2},{4,5},{5,4},{6,7},{7,6},{8,9},{9,8},{10,11... | collective-permute-start | bytes 1572872 | tf_op jit(solution)/shard_map/ppermute | solution.py:422
  45.3 26.3 %collective-permute-start.11 = (f32[128,768]{1,0:T(8,128)S(1)}, f32[128,768]{1,0:T(8,128)S(1)}, u32[]{:S(2)}, u32[]{:S(2)}) collective-permute-start(f32[128,768]{1,0:T(8,128)S(1)} %get-tuple-element.18), channel_id=1, source_target_pairs={{16,8},{17,9},{18,10},{19,11},{20,12},{21,13},{22,14},{23,15}} | collective-permute-start | bytes 1179656 | tf_op jit(solution)/shard_map/ppermute | solution.py:419
  61.4 0.8 collective-permute-start.10
  62.1 14.3 %copy-start.6 = (f32[256,512]{1,0:T(8,128)}, f32[256,512]{1,0:T(8,128)S(1)}, u32[]{:S(2)}) copy-start(f32[256,512]{1,0:T(8,128)S(1)} %shard_map.54.refs_4_.refs_8_) | copy-start | bytes 1572868
  74.4 60.4 %collective-permute-start.13 = (f32[1024,512]{1,0:T(8,128)}, f32[1024,512]{1,0:T(8,128)}, u32[]{:S(2)}, u32[]{:S(2)}) collective-permute-start(f32[1024,512]{1,0:T(8,128)} %pad_maximum_fusion), channel_id=1, source_target_pairs={{8,0},{9,1},{10,2},{11,3},{12,4},{13,5},{14,6},{15,7}} | collective-permute-start | bytes 6291464 | tf_op jit(solution)/shard_map/ppermute | solution.py:419
  76.4 19.8 %collective-permute-start.14 = (f32[256,512]{1,0:T(8,128)S(1)}, f32[256,512]{1,0:T(8,128)S(1)}, u32[]{:S(2)}, u32[]{:S(2)}) collective-permute-start(f32[256,512]{1,0:T(8,128)S(1)} %shard_map.54.refs_4_.refs_8_), channel_id=1, source_target_pairs={{8,16},{16,24},{9,17},{17,25},{10,18},{18,26},{11,19},{19,27},{12,... | collective-permute-start | bytes 1572872 | tf_op jit(solution)/shard_map/ppermute | solution.py:419
  78.3 29.1 %collective-permute-start.15 = (f32[256,512]{1,0:T(8,128)S(1)}, f32[256,512]{1,0:T(8,128)S(1)}, u32[]{:S(2)}, u32[]{:S(2)}) collective-permute-start(f32[256,512]{1,0:T(8,128)S(1)} %shard_map.56.refs_5_.refs_6_.refs_9_), channel_id=1, source_target_pairs={{8,16},{16,24},{9,17},{17,25},{10,18},{18,26},{11,19},{19,27},{12,... | collective-permute-start | bytes 1572872 | tf_op jit(solution)/shard_map/ppermute | solution.py:419
  80.3 13.0 %collective-permute-start.16 = (f32[128,256]{1,0:T(8,128)S(1)}, f32[128,256]{1,0:T(8,128)S(1)}, u32[]{:S(2)}, u32[]{:S(2)}) collective-permute-start(f32[128,256]{1,0:T(8,128)S(1)} %collective-permute-done.10.refs_7_.refs_0_), channel_id=1, source_target_pairs={{0,1},{1,0},{2,3},{3,2},{4,5},{5,4},{6,7},{7,6},{8,9},{9,8},{10,11... | collective-permute-start | bytes 393224 | tf_op jit(solution)/shard_map/ppermute | solution.py:422
  80.4 38.4 %collective-permute-start.19 = (f32[128,1024]{1,0:T(8,128)S(1)}, f32[128,1024]{1,0:T(8,128)}, u32[]{:S(2)}, u32[]{:S(2)}) collective-permute-start(f32[128,1024]{1,0:T(8,128)S(1)} %collective-permute-done.12.refs_9_.refs_0_), channel_id=1, source_target_pairs={{0,1},{1,0},{2,3},{3,2},{4,5},{5,4},{6,7},{7,6},{8,9},{9,8},{10,11... | collective-permute-start | bytes 1572872 | tf_op jit(solution)/shard_map/ppermute | solution.py:422
  97.0 21.7 %collective-permute-start.17 = (f32[256,512]{1,0:T(8,128)S(1)}, f32[256,512]{1,0:T(8,128)S(1)}, u32[]{:S(2)}, u32[]{:S(2)}) collective-permute-start(f32[256,512]{1,0:T(8,128)S(1)} %shard_map.58.refs_7_), channel_id=1, source_target_pairs={{8,16},{16,24},{9,17},{17,25},{10,18},{18,26},{11,19},{19,27},{12,... | collective-permute-start | bytes 1572872 | tf_op jit(solution)/shard_map/ppermute | solution.py:419
  108.8 19.9 %collective-permute-start.18 = (f32[256,512]{1,0:T(8,128)S(1)}, f32[256,512]{1,0:T(8,128)S(1)}, u32[]{:S(2)}, u32[]{:S(2)}) collective-permute-start(f32[256,512]{1,0:T(8,128)S(1)} %shard_map.59.refs_8_.refs_20_), channel_id=1, source_target_pairs={{8,16},{16,24},{9,17},{17,25},{10,18},{18,26},{11,19},{19,27},{12,... | collective-permute-start | bytes 1572872 | tf_op jit(solution)/shard_map/ppermute | solution.py:419
  110.7 1.8 collective-permute-start.20
  112.5 51.0 %collective-permute-start.22 = (f32[512,512]{1,0:T(8,128)S(1)}, f32[512,512]{1,0:T(8,128)S(1)}, u32[]{:S(2)}, u32[]{:S(2)}) collective-permute-start(f32[512,512]{1,0:T(8,128)S(1)} %pad_maximum_fusion.1), channel_id=1, source_target_pairs={{8,0},{9,1},{10,2},{11,3},{12,4},{13,5},{14,6},{15,7}} | collective-permute-start | bytes 3145736 | tf_op jit(solution)/shard_map/ppermute | solution.py:419
  130.0 34.6 %collective-permute-start.23 = (f32[512,512]{1,0:T(8,128)S(1)}, f32[512,512]{1,0:T(8,128)S(1)}, u32[]{:S(2)}, u32[]{:S(2)}) collective-permute-start(f32[512,512]{1,0:T(8,128)S(1)} %pad_maximum_fusion.2), channel_id=1, source_target_pairs={{8,0},{9,1},{10,2},{11,3},{12,4},{13,5},{14,6},{15,7}} | collective-permute-start | bytes 3145736 | tf_op jit(solution)/shard_map/ppermute | solution.py:419
  130.8 20.7 %collective-permute-start.21 = (f32[256,512]{1,0:T(8,128)S(1)}, f32[256,512]{1,0:T(8,128)S(1)}, u32[]{:S(2)}, u32[]{:S(2)}) collective-permute-start(f32[256,512]{1,0:T(8,128)S(1)} %shard_map.62.refs_9_), channel_id=1, source_target_pairs={{8,16},{16,24},{9,17},{17,25},{10,18},{18,26},{11,19},{19,27},{12,... | collective-permute-start | bytes 1572872 | tf_op jit(solution)/shard_map/ppermute | solution.py:419
  132.7 29.5 %collective-permute-start.24 = (f32[256,512]{1,0:T(8,128)S(1)}, f32[256,512]{1,0:T(8,128)S(1)}, u32[]{:S(2)}, u32[]{:S(2)}) collective-permute-start(f32[256,512]{1,0:T(8,128)S(1)} %shard_map.60.refs_16_.refs_10_), channel_id=1, source_target_pairs={{8,16},{16,24},{9,17},{17,25},{10,18},{18,26},{11,19},{19,27},{12,... | collective-permute-start | bytes 1572872 | tf_op jit(solution)/shard_map/ppermute | solution.py:419
  160.8 13.6 %collective-permute-start.25 = (f32[256,512]{1,0:T(8,128)S(1)}, f32[256,512]{1,0:T(8,128)S(1)}, u32[]{:S(2)}, u32[]{:S(2)}) collective-permute-start(f32[256,512]{1,0:T(8,128)S(1)} %collective-permute-done.21.refs_16_.refs_13_.refs_22_), channel_id=1, source_target_pairs={{16,24},{17,25},{18,26},{19,27},{20,28},{21,29},{22,30},{23,31}} | collective-permute-start | bytes 1572872 | tf_op jit(solution)/shard_map/ppermute | solution.py:419
  162.2 21.7 %collective-permute-start.26 = (f32[256,512]{1,0:T(8,128)S(1)}, f32[256,512]{1,0:T(8,128)S(1)}, u32[]{:S(2)}, u32[]{:S(2)}) collective-permute-start(f32[256,512]{1,0:T(8,128)S(1)} %collective-permute-done.24.refs_14_), channel_id=1, source_target_pairs={{16,24},{17,25},{18,26},{19,27},{20,28},{21,29},{22,30},{23,31}} | collective-permute-start | bytes 1572872 | tf_op jit(solution)/shard_map/ppermute | solution.py:419
  (17 other events, 100.3 us)
Sparse Core Ops, SparseCore 0:
  12.2 73.2 all-gather.4
  87.4 72.1 all-gather.6

commit v3 on v2

--- a/solution.py
+++ b/solution.py
@@ -82,8 +82,8 @@
     return arrays, where
 
 
-def params():
-    return pltpu.CompilerParams(vmem_limit_bytes=VMEM_LIMIT)
+def params(limit=VMEM_LIMIT):
+    return pltpu.CompilerParams(vmem_limit_bytes=limit)
 
 
 def cost():
@@ -96,29 +96,6 @@
 
 def PIN(x):
     return x
-
-
-def turn(panel, slabs, after):
-    _, blocks, depth, rows = panel.shape
-    k0, j0 = slabs[0]
-    start = k0 * blocks + j0
-
-    def kernel(in_ref, *refs):
-        refs[-1][0] = in_ref[0, 0].T
-
-    def index(s):
-        at = start + s
-        return (at // blocks, at % blocks, 0, 0)
-
-    return pl.pallas_call(
-        kernel,
-        grid=(len(slabs),),
-        in_specs=[pl.BlockSpec((1, 1, depth, rows), index)] + [ANY] * len(after),
-        out_specs=pl.BlockSpec((1, rows, depth), lambda s: (s, 0, 0)),
-        out_shape=jax.ShapeDtypeStruct((len(slabs), rows, depth), panel.dtype),
-        compiler_params=params(),
-        cost_estimate=cost(),
-    )(in_hbm(panel), *after)
 
 
 def full(shape):
@@ -156,7 +133,15 @@
 
 
 def slot(inverse, k, rhs, received, top, part, after):
-    if len(inverse) == 1:
+    cols = received.shape[1]
+    packed = not isinstance(inverse, list)
+    scratch = []
+    if packed:
+        chunk = depth = cols // 2
+        specs = [ANY]
+        scratch = [pltpu.VMEM((chunk, depth), jnp.float32)]
+        inverse = [inverse]
+    elif len(inverse) == 1:
         _, chunk, _ = inverse[0].shape
         depth = (part - LAG - k * (inverse[0].shape[2] // chunk) + 1) * chunk
         specs = [pl.BlockSpec((1, chunk, depth), lambda s: (k, 0, 0))]
@@ -165,41 +150,54 @@
         half, depth = inverse[0].shape
         chunk = 2 * half
         specs = [full((half, depth))] * 2
-    cols = received.shape[1]
-    tops = [] if top is None else [in_hbm(top)]
+    tops = [] if top is None else [in_hbm(top[0])]
 
     def kernel(*refs):
         inverse_refs, refs = refs[: len(inverse)], refs[len(inverse):]
         received_ref, refs = refs[0], refs[1:]
         rhs_refs, refs = refs[: len(rhs)], refs[len(rhs):]
-        out_ref, whole, sems = refs[-3:]
+        out_ref, whole, sems = refs[-3 - len(scratch):][:3]
         my_row = lax.axis_index("row")
 
-        def move(source, target, n=0):
-            return pltpu.make_async_copy(source, target, sems.at[n])
+        def move(moves):
+            copies = [
+                pltpu.make_async_copy(source, target, sems.at[n])
+                for n, (source, target) in enumerate(moves)
+            ]
+            for copy in copies:
+                copy.start()
+            for copy in copies:
+                copy.wait()
 
         if tops:
 
             @pl.when(my_row == 0)
             def _():
-                copy = move(refs[0].at[0, pl.ds(part * chunk, chunk)], out_ref)
-                copy.start()
-                copy.wait()
+                move(top[1](refs[0], out_ref))
 
         @pl.when(my_row == 1)
         def _():
             moves = []
             for n, ref in enumerate(rhs_refs):
-                if len(rhs) == 1 and rhs[0].ndim == 3:
-                    moves.append(move(ref.at[0, pl.ds(0, depth)], whole))
+                if ref.shape[0] == 1:
+                    moves.append((ref.at[0, pl.ds(0, depth)], whole))
                 else:
-                    moves.append(move(ref, whole.at[pl.ds(n * chunk, chunk)], n))
-            for copy in moves:
-                copy.start()
-            for copy in moves:
-                copy.wait()
+                    moves.append((ref.at[pl.ds(0, chunk)], whole.at[pl.ds(n * chunk, chunk)]))
+            if packed and k == 0:
+                moves += [
+                    (
+                        inverse_refs[0].at[pl.ds(chunk, chunk // 2), pl.ds(p * chunk, chunk)],
+                        refs[-1].at[pl.ds(p * (chunk // 2), chunk // 2)],
+                    )
+                    for p in range(2)
+                ]
+            elif packed:
+                moves.append((inverse_refs[0].at[:, pl.ds(0, chunk)], refs[-1]))
+            move(moves)
             high, low = split(whole[...])
-            if len(inverse) == 1:
+            if packed:
+                out_ref[...] = dot3(refs[-1][...], high, low)
+            elif len(inverse) == 1:
                 out_ref[...] = dot3(inverse_refs[0][0], high, low)
             else:
                 core = lax.rem(lax.axis_index("col"), 2)
@@ -209,9 +207,7 @@
 
         @pl.when(my_row > 1)
         def _():
-            copy = move(received_ref, out_ref)
-            copy.start()
-            copy.wait()
+            move([(received_ref.at[pl.ds(0, chunk)], out_ref)])
 
     return pl.pallas_call(
         kernel,
@@ -221,8 +217,9 @@
         out_shape=jax.ShapeDtypeStruct((chunk, cols), jnp.float32),
         scratch_shapes=[
             pltpu.VMEM((depth, cols), jnp.float32),
-            pltpu.SemaphoreType.DMA((len(rhs),)),
-        ],
+            pltpu.SemaphoreType.DMA((len(rhs) + 2,)),
+        ]
+        + scratch,
         compiler_params=params(),
         cost_estimate=cost(),
     )(*inverse, received, *rhs, *tops, *after)
@@ -246,7 +243,7 @@
 def update(rhs, k, parts, sources, after, js, first=False, fresh=False, solved=None):
     heads = rhs if isinstance(rhs, list) else [rhs]
     _, rows, cols = heads[0].shape
-    blocks = sum(h.shape[0] for h in heads)
+    blocks = max(h.shape[0] for h in heads)
     tile = 512
     steps = rows // tile
     arrays, where = distinct(sources)
@@ -264,23 +261,13 @@
             return slab + at // steps, at % steps
 
         at = len(panels)
-        if isinstance(panel, tuple):
-            for group in range(piece // 2, piece_end // 2):
-
-                def index(s, col, group=group, place=place):
-                    return (lax.bitwise_xor(col[0] // 2, group), *place(s), 0)
-
-                for one in panel:
-                    panels.append(one)
-                    panel_specs.append(pl.BlockSpec((1, 1, tile, one.shape[3]), index))
-        else:
-            count = piece_end - piece
-
-            def index(s, col, which=piece // count, place=place):
-                return (which, *place(s), 0)
-
-            panels.append(panel)
-            panel_specs.append(pl.BlockSpec((count, 1, tile, panel.shape[3]), index))
+        count = piece_end - piece
+
+        def index(s, col, which=piece // count, place=place):
+            return (which, *place(s), 0)
+
+        panels.append(panel)
+        panel_specs.append(pl.BlockSpec((count, 1, tile, panel.shape[3]), index))
         spans.append((at, len(panels)))
 
     def kernel(col_ref, *refs):
@@ -321,28 +308,16 @@
         for h, ref in enumerate(rhs_refs[1:]):
             old = jnp.where(j >= heads[0].shape[0], ref[0], old)
         live = j * len(where) + my_row > k
-        done = j < 0
+        out_ref[0] = old
         for (panel, begin, end, piece, piece_end, row, _), (at, stop) in zip(parts, spans):
-            active = live & (j >= begin) & (j < end)
-            done |= active
-
-            @pl.when(active)
+
+            @pl.when(live & (j >= begin) & (j < end))
             def _():
-                if isinstance(panel, tuple):
-                    even = lax.rem(col_ref[0], 2) == 0
-                    pieces = []
-                    for mine, other in zip(panel_refs[at:stop:2], panel_refs[at + 1:stop:2]):
-                        a, b = mine[0, 0], other[0, 0]
-                        pieces += [jnp.where(even, a, b), jnp.where(even, b, a)]
-                else:
-                    pieces = [panel_refs[at][p, 0] for p in range(piece_end - piece)]
-                left = jnp.concatenate(pieces, axis=1)
+                left = jnp.concatenate(
+                    [panel_refs[at][p, 0] for p in range(piece_end - piece)], axis=1
+                )
                 span = slice(row, row + left.shape[1])
-                out_ref[0] = old - dot3(left, x_hi[span], x_lo[span])
-
-        @pl.when(jnp.logical_not(done))
-        def _():
-            out_ref[0] = old
+                out_ref[0] = out_ref[0] - dot3(left, x_hi[span], x_lo[span])
 
         if last:
 
@@ -364,12 +339,14 @@
             return (at // steps, at % steps, 0)
 
         def beyond(s, col):
-            at = jnp.maximum(s - edge, 0)
+            at = jnp.maximum(s, edge)
             return (at // steps, at % steps, 0)
 
         rhs_specs = [pl.BlockSpec((1, tile, cols), f) for f in (before, beyond)]
     if fresh:
         out_shape = [jax.ShapeDtypeStruct((js[1] - js[0], rows, cols), kind)]
+        if js[1] - js[0] == blocks:
+            out_shape = [pltpu.HBM((blocks, rows, cols), kind)]
         out_specs = [pl.BlockSpec((1, tile, cols), lambda s, col: (s // steps, s % steps, 0))]
     scratch = [
         pltpu.VMEM((depth, cols), jnp.float32),
@@ -394,7 +371,7 @@
         ),
         out_shape=out_shape,
         input_output_aliases={} if first or last or fresh else {1: 0},
-        compiler_params=params(),
+        compiler_params=params(2 * VMEM_LIMIT if last else VMEM_LIMIT),
         cost_estimate=cost(),
     )(
         lax.axis_index("col").astype(jnp.int32).reshape(1),
@@ -413,101 +390,106 @@
     share = inverse_blocks.shape[1]
     half = share // 2
     n = inverse_blocks.shape[2] // share
-    others = [q for q in range(n_row) if q != 1]
+    others = list(range(2, n_row))
 
     def send(value, pairs):
         return lax.ppermute(value, "row", pairs)
 
-    def swap(value):
-        return lax.ppermute(value, "col", [(d, d ^ 1) for d in range(n_col)])
+    def swap(value, mask=1):
+        return lax.ppermute(value, "col", [(d, d ^ mask) for d in range(n_col)])
 
     def onward(value, t):
-        rows = [0] if t < n else []
+        rows = [0] if t <= n else []
         rows += [r for r in range(1, n_row - 1) if 0 <= t - LAG * r < 2 * n]
         return send(value, [(r, r + 1) for r in rows])
 
     halves = [(half, (q + 1) * share) for q in others]
 
-    def cut(k):
+    def cut(k, wanted=others):
         def plan(refs, outs):
             my_row = lax.axis_index("row")
             at = pl.multiple_of(lax.rem(lax.axis_index("col"), 2) * half, half)
             return [
                 (my_row == q, refs[0].at[k, pl.ds(at, half), pl.ds(0, (q + 1) * share)], out)
-                for q, out in zip(others, outs)
+                for q, out in zip(wanted, outs)
             ]
 
         return plan
 
+    def rows_of_top(t):
+        return lambda ref, out: [(ref.at[0, pl.ds(t * share, share)], out)]
+
     def start(refs, outs):
-        return cut(0)(refs, outs) + [
+        first, second, *parts = outs
+        moves = [
+            (refs[1].at[0, pl.ds(0, share)], first.at[pl.ds(0, share)]),
+            (refs[1].at[0, pl.ds(share, share)], second),
+        ] + [
             (
-                lax.axis_index("row") == 0,
-                refs[1].at[0, pl.ds(t * share, share)],
-                outs[len(others) + t],
+                refs[0].at[0, pl.ds(p * half, half), pl.ds(0, share)],
+                first.at[pl.ds(share, half), pl.ds(p * share, share)],
             )
-            for t in range(LAG)
+            for p in range(2)
         ]
+        moves = [(lax.axis_index("row") == 0, *move) for move in moves]
+        return moves + cut(0)(refs, parts)
 
     def to_solver(parts):
         return [send(part, [(q, 1)]) for q, part in zip(others, parts)]
 
-    def whole(k, parts):
-        inverse = [[part, swap(part)] for part in parts]
-        inverse.insert(1, [inverse_blocks])
-        return inverse
-
     slots = 2 * n + LAG * (n_row - 2)
-    *parts, sent0, sent1 = copies(
-        [inverse_blocks, right_side], halves + [(share, cols)] * LAG, start, []
+
+    turned = jnp.transpose(panel_t, (0, 2, 3, 1)).reshape(2 * blocks, -1, panel_t.shape[1])
+    gathered = [lax.all_gather(turned[i:i + blocks], "col") for i in (0, blocks)]
+
+    *sent, part2, part3 = copies(
+        [inverse_blocks, right_side], [(share + half, cols), (share, cols)] + halves, start, []
     )
-    sent = [sent0, sent1]
-    received = [onward(sent[0], 0), onward(sent[1], 1)]
-    arrived = to_solver(parts)
-    inverse = [whole(0, arrived), None]
-
-    slabs = jnp.transpose(panel_t, (0, 2, 1, 3))
-    gathered = []
-    for k in range(2):
-        turned = turn(slabs, [(k, j) for j in range(blocks)], [sent0])
-        gathered.append(lax.all_gather(turned, "col"))
-
-    remaining = right_side
+    received = [onward(sent[t], t) for t in range(LAG)]
+    arrived = to_solver([part2, part3])
+    inverse = [
+        [received[0], [inverse_blocks]] + [[part, swap(part)] for part in arrived],
+        [None, [inverse_blocks]],
+    ]
+
     lowered = None
     solved_here = [[], []]
-    back = [[], []]
+    back = []
     after = arrived
 
     def chunks_of(k, first, end):
-        rows_of = [back[k], solved_here[k]] + [
+        rows_of = [back[k * n:][:n], solved_here[k]] + [
             received[k * n + LAG * (r - 1):][:n] for r in range(2, n_row)
         ]
         return [c[first:end] for c in rows_of]
 
-    def to_first(k, first, end):
-        both = send(jnp.concatenate(solved_here[k][first:end], axis=0), [(1, 0)])
-        back[k] += [both[i * share:(i + 1) * share] for i in range(end - first)]
-
-    late = LAG * (n_row - 2)
-    for t in range(LAG, slots + LAG):
+    for t in range(LAG, slots):
         value = received[t - LAG]
         k, q = divmod(t - LAG, n)
-        if t < slots:
-            if k < 2:
-                rhs = received[: q + 1] if k == 0 else [lowered]
-                top = right_side if t < n else None
-                sent.append(slot(inverse[k][q], k, rhs, value, top, t, after))
-                solved_here[k].append(sent[t])
-            else:
-                sent.append(value)
-            received.append(onward(sent[t], t))
-            after = []
-        here = [sent[t]] if t < slots else []
-        if t == LAG:
-            arrived = to_solver(copies([inverse_blocks], halves, cut(1), here))
-            inverse[1] = whole(1, arrived)
-        if t == 2 * LAG:
-            after = arrived
+        if k < 2:
+            rhs = received[: q + 1] if k == 0 else [lowered]
+            top = None
+            if t < n:
+                top = right_side, rows_of_top(t)
+            elif t == n:
+                top = inverse_blocks, lambda ref, out: [
+                    (ref.at[1, :, pl.ds(0, share)], out.at[:, pl.ds(0, share)])
+                ]
+            sent.append(slot(inverse[k][q], k, rhs, value, top, t, after))
+            solved_here[k].append(sent[t])
+            back.append(send(sent[t], [(1, 0)]))
+        else:
+            sent.append(value)
+        received.append(onward(sent[t], t))
+        after = back[t - 2 * LAG + 1:t - 2 * LAG + 2] if t >= 2 * LAG - 1 else []
+        here = [sent[t]]
+        if t in (2, 3):
+            part, = copies([inverse_blocks], [halves[t - 2]], cut(1, [t]), here)
+            arrived = send(part, [(t, 1)])
+            inverse[1].append([arrived, swap(arrived)])
+            after = after + [arrived]
+        if t == n:
+            inverse[1][0] = received[n]
         if t == n + LAG - 1:
             lowered = update(
                 right_side,
@@ -518,36 +500,19 @@
                 (0, 1),
                 fresh=True,
             )
-            after = [lowered]
-        if t == n + LAG:
-            to_first(0, 0, n)
-        if t in (n + LAG + 1, n + LAG + 3):
-            to_first(1, t - n - LAG - 1, t - n - LAG + 1)
-        ready = t - LAG - late
-        if ready == n - 1:
+            after = after + [lowered]
+        if t == slots - 1:
             remaining = update(
-                remaining,
+                right_side,
                 0,
-                [(gathered[0], 0, 2, 0, n_col, 0, 0)],
+                [(gathered[0], 0, blocks, 0, n_col, 0, 0)],
                 chunks_of(0, 0, n),
                 here,
-                (0, 2),
+                (0, blocks),
                 fresh=True,
             )
-            after = [remaining]
-        if ready == n:
-            third = update(
-                right_side,
-                0,
-                [(gathered[0], 2, 3, 0, n_col, 0, 2)],
-                chunks_of(0, 0, n),
-                here,
-                (2, 3),
-                fresh=True,
-            )
-            after = [third]
     remaining, solved = update(
-        [remaining, third],
+        remaining,
         1,
         [(gathered[1], 0, blocks, 0, n_col, 0, 0)],
         chunks_of(1, 0, n),

time: 211 us -> 192 us (0.910)
  waiting for transfers between devices: 84.3 us -> 64.6 us
  starting transfers between devices: 39 us -> 52 us
  Pallas kernels: 59.3 us -> 50.2 us
    ppermute x21 -> x24, waiting for transfers between devices: 78 us -> 58.8 us  [send(): return lax.ppermute(value, 'row', pairs)]
    ppermute x21 -> x24, starting transfers between devices: 37.7 us -> 51.4 us  [send(): return lax.ppermute(value, 'row', pairs)]
    pallas_call x2 -> x0, Pallas kernels: 7.43 us -> none  [turn(): pl.pallas_call(kernel, grid=(len(slabs),), in_specs=[pl.BlockSpec((1, 1,...]
    slice x3 -> x1, local copies, waits for them, and re-layouts: 5.01 us -> 1.89 us  [body(): turned[i:i + blocks]]
    pallas_call x4 -> x3, Pallas kernels: 45.6 us -> 42.8 us  [update(): pl.pallas_call(kernel, grid_spec=pltpu.PrefetchScalarGridSpec(num_scalar_...]
    unnamed x40 -> x49, local copies, waits for them, and re-layouts: 5.62 us -> 7.92 us
  transfers between devices with their start and end apart: 29 -> 30, of which waited for: 12 -> 8; matrix products, arithmetic and copies ran while one was open for 3% -> 0% of each run, Pallas kernels for 17% -> 17%
where the time goes in v3:
time: 192 us; the launch traced here: 191 us
  waiting for transfers between devices  64.6 us (34%)
  starting transfers between devices  52 us (27%)
  Pallas kernels  50.2 us (26%)
  between operations  14.7 us (8%)
  local copies, waits for them, and re-layouts  9.81 us (5%)
    ppermute x24, waiting for transfers between devices, send(): return lax.ppermute(value, 'row', pairs)  58.8 us
    ppermute x24, starting transfers between devices, send(): return lax.ppermute(value, 'row', pairs)  51.4 us
    pallas_call x3, Pallas kernels, update(): pl.pallas_call(kernel, grid_spec=pltpu.PrefetchScalarGridSpec(num_scalar_...  42.8 us
    unnamed x49, local copies, waits for them, and re-layouts  7.92 us
    all_gather x2, waiting for transfers between devices, body(): lax.all_gather(turned[i:i + blocks], 'col')  5.06 us
    pallas_call x8, Pallas kernels, slot(): pl.pallas_call(kernel, grid=(1,), in_specs=specs + [ANY] * (1 + len(rhs)...  4.95 us
  transfers between devices with their start and end apart: 30, of which 8 were waited for; matrix products, arithmetic and copies ran while one was open for 0% of the time, Pallas kernels for 17%

profile of v3, /device:TPU:18, one launch (start us, length us, event | category | flops | bytes accessed | tf_op | source)
XLA Modules:
  0.0 191.3 jit_solution(1176212813227040658)
XLA Ops:
  7.2 2.4 %copy.6 = f32[2,128,3,1024]{1,3,2,0:T(8,128)S(1)} copy(f32[2,128,3,1024]{3,1,2,0:T(8,128)} %param.4) | data formatting | bytes 6291456 | tf_op args[1]
  9.6 1.9 fusion
  12.2 1.2 shard_map.50
  14.8 2.6 %collective-permute-start.1 = (f32[128,768]{1,0:T(8,128)S(1)}, f32[128,768]{1,0:T(8,128)S(1)}, u32[]{:S(2)}, u32[]{:S(2)}) collective-permute-start(f32[128,768]{1,0:T(8,128)S(1)} %get-tuple-element.9), channel_id=1, source_target_pairs={{16,8},{17,9},{18,10},{19,11},{20,12},{21,13},{22,14},{23,15}} | collective-permute-start | bytes 1179656 | tf_op jit(solution)/shard_map/ppermute | solution.py:396
  18.1 18.5 %collective-permute-done.1.refs_4_.refs_0_ = f32[128,768]{1,0:T(8,128)S(1)} collective-permute-done((f32[128,768]{1,0:T(8,128)S(1)}, f32[128,768]{1,0:T(8,128)S(1)}, u32[]{:S(2)}, u32[]{:S(2)}) %collective-permute-start.1) | collective-permute-done | bytes 393248 | tf_op jit(solution)/shard_map/ppermute | solution.py:396
  36.7 1.3 collective-permute-start.8
  38.0 1.2 shard_map.52
  39.1 4.5 %collective-permute-start.5 = (f32[128,768]{1,0:T(8,128)S(1)}, f32[128,768]{1,0:T(8,128)S(1)}, u32[]{:S(2)}, u32[]{:S(2)}) collective-permute-start(f32[128,768]{1,0:T(8,128)S(1)} %shard_map.52), channel_id=1, source_target_pairs={{16,8},{17,9},{18,10},{19,11},{20,12},{21,13},{22,14},{23,15}} | collective-permute-start | bytes 1179656 | tf_op jit(solution)/shard_map/ppermute | solution.py:396
  43.7 8.5 %collective-permute-done.5.refs_5_.refs_0_ = f32[128,768]{1,0:T(8,128)S(1)} collective-permute-done((f32[128,768]{1,0:T(8,128)S(1)}, f32[128,768]{1,0:T(8,128)S(1)}, u32[]{:S(2)}, u32[]{:S(2)}) %collective-permute-start.5) | collective-permute-done | bytes 393248 | tf_op jit(solution)/shard_map/ppermute | solution.py:396
  52.2 1.1 shard_map.53.refs_1_.refs_3_.refs_7_.refs_18_
  55.0 1.3 collective-permute-start.12
  58.1 1.5 collective-permute-start.10
  59.5 16.7 %collective-permute-start.14 = (f32[256,512]{1,0:T(8,128)S(1)}, f32[256,512]{1,0:T(8,128)S(1)}, u32[]{:S(2)}, u32[]{:S(2)}) collective-permute-start(f32[256,512]{1,0:T(8,128)S(1)} %shard_map.55.refs_4_.refs_8_), channel_id=1, source_target_pairs={{0,8},{8,16},{16,24},{1,9},{9,17},{17,25},{2,10},{10,18},{18,26},{... | collective-permute-start | bytes 1572872 | tf_op jit(solution)/shard_map/ppermute | solution.py:396
  77.8 1.9 %collective-permute-start.15 = (f32[256,512]{1,0:T(8,128)S(1)}, f32[256,512]{1,0:T(8,128)S(1)}, u32[]{:S(2)}, u32[]{:S(2)}) collective-permute-start(f32[256,512]{1,0:T(8,128)S(1)} %shard_map.56.refs_5_.refs_6_.refs_9_), channel_id=1, source_target_pairs={{8,16},{16,24},{9,17},{17,25},{10,18},{18,26},{11,19},{19,27},{12,... | collective-permute-start | bytes 1572872 | tf_op jit(solution)/shard_map/ppermute | solution.py:396
  79.8 5.0 %all-gather.3.cloned.1.call-done.refs_1_ = f32[8,3,1024,128]{3,2,1,0:T(8,128)} async-done(((f32[1,3,1024,128]{3,2,1,0:T(8,128)}), f32[8,3,1024,128]{3,2,1,0:T(8,128)}) %all-gather.3.cloned.1.call-update) | async-done | bytes 12582928 | tf_op jit(solution)/shard_map/all_gather | solution.py:443
  84.8 7.9 %shard_map.57.refs_2_.refs_4_.refs_3_ = f32[1,1024,512]{2,1,0:T(8,128)S(1)} custom-call(s32[1]{0:T(128)} %bitcast.col_ref, f32[3,1024,512]{2,1,0:T(8,128)} %refs_0_.13, f32[8,3,1024,128]{3,2,1,0:T(8,128)} %all-gather.3.cloned.1.call-done.refs_1_, f32[256,512]{1,0:T(8,128)} %copy-done.4, f32[256,512]{1,0:T(8,128)} %copy-done, f32[256,512]{1,0:T(8,128)} %copy-done.11, ...), custom_call_target="tpu_custom_call" | custom-call | flops 1024 | bytes 1024 | tf_op jit(solution)/shard_map/pallas_call | solution.py:363
  93.9 3.4 %collective-permute-start.16 = (f32[256,512]{1,0:T(8,128)S(1)}, f32[256,512]{1,0:T(8,128)S(1)}, u32[]{:S(2)}, u32[]{:S(2)}) collective-permute-start(f32[256,512]{1,0:T(8,128)S(1)} %shard_map.58.refs_6_), channel_id=1, source_target_pairs={{8,16},{16,24},{9,17},{17,25},{10,18},{18,26},{11,19},{19,27},{12,... | collective-permute-start | bytes 1572872 | tf_op jit(solution)/shard_map/ppermute | solution.py:396
  98.0 4.9 %collective-permute-done.15.refs_1_.refs_13_ = f32[256,512]{1,0:T(8,128)S(1)} collective-permute-done((f32[256,512]{1,0:T(8,128)S(1)}, f32[256,512]{1,0:T(8,128)S(1)}, u32[]{:S(2)}, u32[]{:S(2)}) %collective-permute-start.15) | collective-permute-done | bytes 524320 | tf_op jit(solution)/shard_map/ppermute | solution.py:396
  102.8 1.3 shard_map.59.refs_7_.refs_19_
  104.9 1.9 collective-permute-start.17
  107.6 6.1 %collective-permute-done.16.refs_14_.refs_2_.refs_10_ = f32[256,512]{1,0:T(8,128)S(1)} collective-permute-done((f32[256,512]{1,0:T(8,128)S(1)}, f32[256,512]{1,0:T(8,128)S(1)}, u32[]{:S(2)}, u32[]{:S(2)}) %collective-permute-start.16) | collective-permute-done | bytes 524320 | tf_op jit(solution)/shard_map/ppermute | solution.py:396
  113.7 2.1 %shard_map.62.refs_8_ = f32[256,512]{1,0:T(8,128)} custom-call(f32[128,768]{1,0:T(8,128)S(1)} %collective-permute-done.5.refs_5_.refs_0_, f32[128,768]{1,0:T(8,128)} %collective-permute-done.22.refs_1_, f32[256,512]{1,0:T(8,128)S(1)} %collective-permute-done.16.refs_14_.refs_2_.refs_10_, f32[1,1024,512]{2,1,0:T(8,128)S(1)} %shard_map.57.refs_2_.refs_4_.refs_3_, ...), custom_call_target="tpu_custom_call" | custom-call | flops 1024 | bytes 1024 | tf_op jit(solution)/shard_map/pallas_call | solution.py:212
  115.8 1.9 %collective-permute-start.25 = (f32[256,512]{1,0:T(8,128)}, f32[256,512]{1,0:T(8,128)S(1)}, u32[]{:S(2)}, u32[]{:S(2)}) collective-permute-start(f32[256,512]{1,0:T(8,128)} %shard_map.62.refs_8_), channel_id=1, source_target_pairs={{8,16},{16,24},{9,17},{17,25},{10,18},{18,26},{11,19},{19,27},{12,... | collective-permute-start | bytes 1572872 | tf_op jit(solution)/shard_map/ppermute | solution.py:396
  117.8 7.1 %collective-permute-done.17.refs_2_.refs_15_.refs_11_.refs_22_ = f32[256,512]{1,0:T(8,128)S(1)} collective-permute-done((f32[256,512]{1,0:T(8,128)S(1)}, f32[256,512]{1,0:T(8,128)S(1)}, u32[]{:S(2)}, u32[]{:S(2)}) %collective-permute-start.17) | collective-permute-done | bytes 524320 | tf_op jit(solution)/shard_map/ppermute | solution.py:396
  125.9 1.9 collective-permute-start.20
  128.5 1.5 collective-permute-start.24
  130.0 6.6 %collective-permute-done.25.refs_12_.refs_21_ = f32[256,512]{1,0:T(8,128)S(1)} collective-permute-done((f32[256,512]{1,0:T(8,128)}, f32[256,512]{1,0:T(8,128)S(1)}, u32[]{:S(2)}, u32[]{:S(2)}) %collective-permute-start.25) | collective-permute-done | bytes 524320 | tf_op jit(solution)/shard_map/ppermute | solution.py:396
  136.5 2.1 %collective-permute-start.26 = (f32[256,512]{1,0:T(8,128)S(1)}, f32[256,512]{1,0:T(8,128)}, u32[]{:S(2)}, u32[]{:S(2)}) collective-permute-start(f32[256,512]{1,0:T(8,128)S(1)} %collective-permute-done.25.refs_12_.refs_21_), channel_id=1, source_target_pairs={{16,24},{17,25},{18,26},{19,27},{20,28},{21,29},{22,30},{23,31}} | collective-permute-start | bytes 1572872 | tf_op jit(solution)/shard_map/ppermute | solution.py:396
  138.6 7.2 %collective-permute-done.20.refs_16_.refs_13_ = f32[256,512]{1,0:T(8,128)S(1)} collective-permute-done((f32[256,512]{1,0:T(8,128)S(1)}, f32[256,512]{1,0:T(8,128)S(1)}, u32[]{:S(2)}, u32[]{:S(2)}) %collective-permute-start.20) | collective-permute-done | bytes 524320 | tf_op jit(solution)/shard_map/ppermute | solution.py:396
  145.8 2.0 %collective-permute-start.27 = (f32[256,512]{1,0:T(8,128)S(1)}, f32[256,512]{1,0:T(8,128)S(1)}, u32[]{:S(2)}, u32[]{:S(2)}) collective-permute-start(f32[256,512]{1,0:T(8,128)S(1)} %collective-permute-done.20.refs_16_.refs_13_), channel_id=1, source_target_pairs={{16,24},{17,25},{18,26},{19,27},{20,28},{21,29},{22,30},{23,31}} | collective-permute-start | bytes 1572872 | tf_op jit(solution)/shard_map/ppermute | solution.py:396
  147.8 17.4 %shard_map.61.refs_0_ = f32[3,1024,512]{2,1,0:T(8,128)} custom-call(s32[1]{0:T(128)} %bitcast.col_ref, f32[3,1024,512]{2,1,0:T(8,128)} %refs_0_.13, f32[8,3,1024,128]{3,2,1,0:T(8,128)} %all-gather.3.cloned.1.call-done.refs_1_, f32[256,512]{1,0:T(8,128)} %copy-done.8, f32[256,512]{1,0:T(8,128)} %copy-done.13, ...), custom_call_target="tpu_custom_call" | custom-call | flops 1024 | bytes 1024 | tf_op jit(solution)/shard_map/pallas_call | solution.py:363
  166.9 17.6 %shard_map.63 = (f32[3,1024,512]{2,1,0:T(8,128)}, f32[2,256,512]{2,1,0:T(8,128)}) custom-call(s32[1]{0:T(128)} %bitcast.col_ref, f32[3,1024,512]{2,1,0:T(8,128)} %shard_map.61.refs_0_, f32[8,3,1024,128]{3,2,1,0:T(8,128)} %all-gather.5.cloned.1.call-done.refs_1_, f32[256,512]{1,0:T(8,128)} %copy-done.7, f32[256,512]{1,0:T(8,128)} %copy-done.15, ...), custom_call_target="tpu_custom_call" | custom-call | flops 1024 | bytes 1024 | tf_op jit(solution)/shard_map/pallas_call | solution.py:363
  (94 shorter events, 14.5 us)
Async XLA Ops:
  7.2 77.7 %all-gather.3.cloned.1.call-start = ((), (), s32[]{:S(2)}) async-start(), calls=%async_computation | async-start | bytes 14155776 | tf_op jit(solution)/shard_map/all_gather | solution.py:443
  11.5 153.7 %all-gather.5.cloned.1.call-start = ((), (), s32[]{:S(2)}) async-start(), calls=%async_computation.1 | async-start | bytes 14155776 | tf_op jit(solution)/shard_map/all_gather | solution.py:443
  13.4 23.2 %collective-permute-start = (f32[384,512]{1,0:T(8,128)S(1)}, f32[384,512]{1,0:T(8,128)S(1)}, u32[]{:S(2)}, u32[]{:S(2)}) collective-permute-start(f32[384,512]{1,0:T(8,128)S(1)} %get-tuple-element.8), channel_id=1, source_target_pairs={{0,8},{1,9},{2,10},{3,11},{4,12},{5,13},{6,14},{7,15}} | collective-permute-start | bytes 2359304 | tf_op jit(solution)/shard_map/ppermute | solution.py:396
  14.1 22.4 %collective-permute-start.2 = (f32[128,1024]{1,0:T(8,128)S(1)}, f32[128,1024]{1,0:T(8,128)S(1)}, u32[]{:S(2)}, u32[]{:S(2)}) collective-permute-start(f32[128,1024]{1,0:T(8,128)S(1)} %get-tuple-element.10), channel_id=1, source_target_pairs={{24,8},{25,9},{26,10},{27,11},{28,12},{29,13},{30,14},{31,15}} | collective-permute-start | bytes 1572872 | tf_op jit(solution)/shard_map/ppermute | solution.py:396
  14.8 21.7 %collective-permute-start.1 = (f32[128,768]{1,0:T(8,128)S(1)}, f32[128,768]{1,0:T(8,128)S(1)}, u32[]{:S(2)}, u32[]{:S(2)}) collective-permute-start(f32[128,768]{1,0:T(8,128)S(1)} %get-tuple-element.9), channel_id=1, source_target_pairs={{16,8},{17,9},{18,10},{19,11},{20,12},{21,13},{22,14},{23,15}} | collective-permute-start | bytes 1179656 | tf_op jit(solution)/shard_map/ppermute | solution.py:396
  17.4 26.3 %collective-permute-start.4 = (f32[256,512]{1,0:T(8,128)S(1)}, f32[256,512]{1,0:T(8,128)S(1)}, u32[]{:S(2)}, u32[]{:S(2)}) collective-permute-start(f32[256,512]{1,0:T(8,128)S(1)} %get-tuple-element.11), channel_id=1, source_target_pairs={{0,8},{1,9},{2,10},{3,11},{4,12},{5,13},{6,14},{7,15}} | collective-permute-start | bytes 1572872 | tf_op jit(solution)/shard_map/ppermute | solution.py:396
  36.7 19.7 %collective-permute-start.8 = (f32[256,512]{1,0:T(8,128)S(1)}, f32[256,512]{1,0:T(8,128)S(1)}, u32[]{:S(2)}, u32[]{:S(2)}) collective-permute-start(f32[256,512]{1,0:T(8,128)S(1)} %shard_map.51.refs_1_.refs_2_.refs_6_), channel_id=1, source_target_pairs={{0,8},{8,16},{1,9},{9,17},{2,10},{10,18},{3,11},{11,19},{4,12},{12... | collective-permute-start | bytes 1572872 | tf_op jit(solution)/shard_map/ppermute | solution.py:396
  39.1 13.1 %collective-permute-start.5 = (f32[128,768]{1,0:T(8,128)S(1)}, f32[128,768]{1,0:T(8,128)S(1)}, u32[]{:S(2)}, u32[]{:S(2)}) collective-permute-start(f32[128,768]{1,0:T(8,128)S(1)} %shard_map.52), channel_id=1, source_target_pairs={{16,8},{17,9},{18,10},{19,11},{20,12},{21,13},{22,14},{23,15}} | collective-permute-start | bytes 1179656 | tf_op jit(solution)/shard_map/ppermute | solution.py:396
  43.6 11.4 %collective-permute-start.7 = (f32[128,768]{1,0:T(8,128)S(1)}, f32[128,768]{1,0:T(8,128)S(1)}, u32[]{:S(2)}, u32[]{:S(2)}) collective-permute-start(f32[128,768]{1,0:T(8,128)S(1)} %collective-permute-done.1.refs_4_.refs_0_), channel_id=1, source_target_pairs={{0,1},{1,0},{2,3},{3,2},{4,5},{5,4},{6,7},{7,6},{8,9},{9,8},{10,11... | collective-permute-start | bytes 1179656 | tf_op jit(solution)/shard_map/ppermute | solution.py:399
  53.4 3.7 %collective-permute-start.3 = (f32[256,512]{1,0:T(8,128)S(1)}, f32[256,512]{1,0:T(8,128)S(1)}, u32[]{:S(2)}, u32[]{:S(2)}) collective-permute-start(f32[256,512]{1,0:T(8,128)S(1)} %shard_map.51.refs_1_.refs_2_.refs_6_), channel_id=1, source_target_pairs={{8,0},{9,1},{10,2},{11,3},{12,4},{13,5},{14,6},{15,7}} | collective-permute-start | bytes 1572872 | tf_op jit(solution)/shard_map/ppermute | solution.py:396
  54.2 2.8 %collective-permute-start.9 = (f32[128,1024]{1,0:T(8,128)S(1)}, f32[128,1024]{1,0:T(8,128)S(1)}, u32[]{:S(2)}, u32[]{:S(2)}) collective-permute-start(f32[128,1024]{1,0:T(8,128)S(1)} %shard_map.54), channel_id=1, source_target_pairs={{24,8},{25,9},{26,10},{27,11},{28,12},{29,13},{30,14},{31,15}} | collective-permute-start | bytes 1572872 | tf_op jit(solution)/shard_map/ppermute | solution.py:396
  54.9 21.3 %collective-permute-start.11 = (f32[128,1024]{1,0:T(8,128)S(1)}, f32[128,1024]{1,0:T(8,128)S(1)}, u32[]{:S(2)}, u32[]{:S(2)}) collective-permute-start(f32[128,1024]{1,0:T(8,128)S(1)} %collective-permute-done.2.refs_5_.refs_0_), channel_id=1, source_target_pairs={{0,1},{1,0},{2,3},{3,2},{4,5},{5,4},{6,7},{7,6},{8,9},{9,8},{10,11... | collective-permute-start | bytes 1572872 | tf_op jit(solution)/shard_map/ppermute | solution.py:399
  55.0 21.2 %collective-permute-start.12 = (f32[256,512]{1,0:T(8,128)S(1)}, f32[256,512]{1,0:T(8,128)S(1)}, u32[]{:S(2)}, u32[]{:S(2)}) collective-permute-start(f32[256,512]{1,0:T(8,128)S(1)} %shard_map.53.refs_1_.refs_3_.refs_7_.refs_18_), channel_id=1, source_target_pairs={{0,8},{8,16},{1,9},{9,17},{2,10},{10,18},{3,11},{11,19},{4,12},{12... | collective-permute-start | bytes 1572872 | tf_op jit(solution)/shard_map/ppermute | solution.py:396
  56.3 19.9 %collective-permute-start.6 = (f32[256,512]{1,0:T(8,128)S(1)}, f32[256,512]{1,0:T(8,128)S(1)}, u32[]{:S(2)}, u32[]{:S(2)}) collective-permute-start(f32[256,512]{1,0:T(8,128)S(1)} %shard_map.53.refs_1_.refs_3_.refs_7_.refs_18_), channel_id=1, source_target_pairs={{8,0},{9,1},{10,2},{11,3},{12,4},{13,5},{14,6},{15,7}} | collective-permute-start | bytes 1572872 | tf_op jit(solution)/shard_map/ppermute | solution.py:396
  58.1 34.6 %collective-permute-start.10 = (f32[256,512]{1,0:T(8,128)S(1)}, f32[256,512]{1,0:T(8,128)}, u32[]{:S(2)}, u32[]{:S(2)}) collective-permute-start(f32[256,512]{1,0:T(8,128)S(1)} %shard_map.55.refs_4_.refs_8_), channel_id=1, source_target_pairs={{8,0},{9,1},{10,2},{11,3},{12,4},{13,5},{14,6},{15,7}} | collective-permute-start | bytes 1572872 | tf_op jit(solution)/shard_map/ppermute | solution.py:396
  59.5 33.5 %collective-permute-start.14 = (f32[256,512]{1,0:T(8,128)S(1)}, f32[256,512]{1,0:T(8,128)S(1)}, u32[]{:S(2)}, u32[]{:S(2)}) collective-permute-start(f32[256,512]{1,0:T(8,128)S(1)} %shard_map.55.refs_4_.refs_8_), channel_id=1, source_target_pairs={{0,8},{8,16},{16,24},{1,9},{9,17},{17,25},{2,10},{10,18},{18,26},{... | collective-permute-start | bytes 1572872 | tf_op jit(solution)/shard_map/ppermute | solution.py:396
  77.1 20.2 %collective-permute-start.13 = (f32[256,512]{1,0:T(8,128)S(1)}, f32[256,512]{1,0:T(8,128)S(1)}, u32[]{:S(2)}, u32[]{:S(2)}) collective-permute-start(f32[256,512]{1,0:T(8,128)S(1)} %shard_map.56.refs_5_.refs_6_.refs_9_), channel_id=1, source_target_pairs={{8,0},{9,1},{10,2},{11,3},{12,4},{13,5},{14,6},{15,7}} | collective-permute-start | bytes 1572872 | tf_op jit(solution)/shard_map/ppermute | solution.py:396
  77.8 25.1 %collective-permute-start.15 = (f32[256,512]{1,0:T(8,128)S(1)}, f32[256,512]{1,0:T(8,128)S(1)}, u32[]{:S(2)}, u32[]{:S(2)}) collective-permute-start(f32[256,512]{1,0:T(8,128)S(1)} %shard_map.56.refs_5_.refs_6_.refs_9_), channel_id=1, source_target_pairs={{8,16},{16,24},{9,17},{17,25},{10,18},{18,26},{11,19},{19,27},{12,... | collective-permute-start | bytes 1572872 | tf_op jit(solution)/shard_map/ppermute | solution.py:396
  79.7 27.2 %collective-permute-start.22 = (f32[128,768]{1,0:T(8,128)S(1)}, f32[128,768]{1,0:T(8,128)}, u32[]{:S(2)}, u32[]{:S(2)}) collective-permute-start(f32[128,768]{1,0:T(8,128)S(1)} %collective-permute-done.5.refs_5_.refs_0_), channel_id=1, source_target_pairs={{0,1},{1,0},{2,3},{3,2},{4,5},{5,4},{6,7},{7,6},{8,9},{9,8},{10,11... | collective-permute-start | bytes 1179656 | tf_op jit(solution)/shard_map/ppermute | solution.py:399
  92.7 25.0 %collective-permute-start.18 = (f32[128,1024]{1,0:T(8,128)S(1)}, f32[128,1024]{1,0:T(8,128)S(1)}, u32[]{:S(2)}, u32[]{:S(2)}) collective-permute-start(f32[128,1024]{1,0:T(8,128)S(1)} %copy-done.20), channel_id=1, source_target_pairs={{0,1},{1,0},{2,3},{3,2},{4,5},{5,4},{6,7},{7,6},{8,9},{9,8},{10,11... | collective-permute-start | bytes 1572872 | tf_op jit(solution)/shard_map/ppermute | solution.py:399
  93.9 19.8 %collective-permute-start.16 = (f32[256,512]{1,0:T(8,128)S(1)}, f32[256,512]{1,0:T(8,128)S(1)}, u32[]{:S(2)}, u32[]{:S(2)}) collective-permute-start(f32[256,512]{1,0:T(8,128)S(1)} %shard_map.58.refs_6_), channel_id=1, source_target_pairs={{8,16},{16,24},{9,17},{17,25},{10,18},{18,26},{11,19},{19,27},{12,... | collective-permute-start | bytes 1572872 | tf_op jit(solution)/shard_map/ppermute | solution.py:396
  97.3 16.4 %collective-permute-start.21 = (f32[256,512]{1,0:T(8,128)S(1)}, f32[256,512]{1,0:T(8,128)S(1)}, u32[]{:S(2)}, u32[]{:S(2)}) collective-permute-start(f32[256,512]{1,0:T(8,128)S(1)} %shard_map.58.refs_6_), channel_id=1, source_target_pairs={{8,0},{9,1},{10,2},{11,3},{12,4},{13,5},{14,6},{15,7}} | collective-permute-start | bytes 1572872 | tf_op jit(solution)/shard_map/ppermute | solution.py:396
  104.9 20.0 %collective-permute-start.17 = (f32[256,512]{1,0:T(8,128)S(1)}, f32[256,512]{1,0:T(8,128)S(1)}, u32[]{:S(2)}, u32[]{:S(2)}) collective-permute-start(f32[256,512]{1,0:T(8,128)S(1)} %shard_map.59.refs_7_.refs_19_), channel_id=1, source_target_pairs={{8,16},{16,24},{9,17},{17,25},{10,18},{18,26},{11,19},{19,27},{12,... | collective-permute-start | bytes 1572872 | tf_op jit(solution)/shard_map/ppermute | solution.py:396
  106.9 18.0 %collective-permute-start.19 = (f32[256,512]{1,0:T(8,128)S(1)}, f32[256,512]{1,0:T(8,128)S(1)}, u32[]{:S(2)}, u32[]{:S(2)}) collective-permute-start(f32[256,512]{1,0:T(8,128)S(1)} %shard_map.59.refs_7_.refs_19_), channel_id=1, source_target_pairs={{8,0},{9,1},{10,2},{11,3},{12,4},{13,5},{14,6},{15,7}} | collective-permute-start | bytes 1572872 | tf_op jit(solution)/shard_map/ppermute | solution.py:396
  115.8 20.7 %collective-permute-start.25 = (f32[256,512]{1,0:T(8,128)}, f32[256,512]{1,0:T(8,128)S(1)}, u32[]{:S(2)}, u32[]{:S(2)}) collective-permute-start(f32[256,512]{1,0:T(8,128)} %shard_map.62.refs_8_), channel_id=1, source_target_pairs={{8,16},{16,24},{9,17},{17,25},{10,18},{18,26},{11,19},{19,27},{12,... | collective-permute-start | bytes 1572872 | tf_op jit(solution)/shard_map/ppermute | solution.py:396
  125.9 39.3 %copy-start.16 = (f32[256,512]{1,0:T(8,128)}, f32[256,512]{1,0:T(8,128)S(1)}, u32[]{:S(2)}) copy-start(f32[256,512]{1,0:T(8,128)S(1)} %shard_map.60.refs_9_) | copy-start | bytes 1572868
  125.9 19.9 %collective-permute-start.20 = (f32[256,512]{1,0:T(8,128)S(1)}, f32[256,512]{1,0:T(8,128)S(1)}, u32[]{:S(2)}, u32[]{:S(2)}) collective-permute-start(f32[256,512]{1,0:T(8,128)S(1)} %shard_map.60.refs_9_), channel_id=1, source_target_pairs={{8,16},{16,24},{9,17},{17,25},{10,18},{18,26},{11,19},{19,27},{12,... | collective-permute-start | bytes 1572872 | tf_op jit(solution)/shard_map/ppermute | solution.py:396
  127.8 37.5 %collective-permute-start.23 = (f32[256,512]{1,0:T(8,128)}, f32[256,512]{1,0:T(8,128)S(1)}, u32[]{:S(2)}, u32[]{:S(2)}) collective-permute-start(f32[256,512]{1,0:T(8,128)} %shard_map.62.refs_8_), channel_id=1, source_target_pairs={{8,0},{9,1},{10,2},{11,3},{12,4},{13,5},{14,6},{15,7}} | collective-permute-start | bytes 1572872 | tf_op jit(solution)/shard_map/ppermute | solution.py:396
  128.5 36.8 %collective-permute-start.24 = (f32[256,512]{1,0:T(8,128)S(1)}, f32[256,512]{1,0:T(8,128)}, u32[]{:S(2)}, u32[]{:S(2)}) collective-permute-start(f32[256,512]{1,0:T(8,128)S(1)} %shard_map.60.refs_9_), channel_id=1, source_target_pairs={{8,0},{9,1},{10,2},{11,3},{12,4},{13,5},{14,6},{15,7}} | collective-permute-start | bytes 1572872 | tf_op jit(solution)/shard_map/ppermute | solution.py:396
  136.5 28.7 %copy-start.21 = (f32[256,512]{1,0:T(8,128)}, f32[256,512]{1,0:T(8,128)S(1)}, u32[]{:S(2)}) copy-start(f32[256,512]{1,0:T(8,128)S(1)} %collective-permute-done.25.refs_12_.refs_21_) | copy-start | bytes 1572868
  136.5 28.8 %collective-permute-start.26 = (f32[256,512]{1,0:T(8,128)S(1)}, f32[256,512]{1,0:T(8,128)}, u32[]{:S(2)}, u32[]{:S(2)}) collective-permute-start(f32[256,512]{1,0:T(8,128)S(1)} %collective-permute-done.25.refs_12_.refs_21_), channel_id=1, source_target_pairs={{16,24},{17,25},{18,26},{19,27},{20,28},{21,29},{22,30},{23,31}} | collective-permute-start | bytes 1572872 | tf_op jit(solution)/shard_map/ppermute | solution.py:396
  145.8 19.5 %collective-permute-start.27 = (f32[256,512]{1,0:T(8,128)S(1)}, f32[256,512]{1,0:T(8,128)S(1)}, u32[]{:S(2)}, u32[]{:S(2)}) collective-permute-start(f32[256,512]{1,0:T(8,128)S(1)} %collective-permute-done.20.refs_16_.refs_13_), channel_id=1, source_target_pairs={{16,24},{17,25},{18,26},{19,27},{20,28},{21,29},{22,30},{23,31}} | collective-permute-start | bytes 1572872 | tf_op jit(solution)/shard_map/ppermute | solution.py:396
  (22 other events, 202.1 us)
Sparse Core Ops, SparseCore 0:
  11.6 73.1 all-gather.2
  87.3 72.1 all-gather.4

commit v4 on v3

--- a/solution.py
+++ b/solution.py
@@ -345,8 +345,8 @@
         rhs_specs = [pl.BlockSpec((1, tile, cols), f) for f in (before, beyond)]
     if fresh:
         out_shape = [jax.ShapeDtypeStruct((js[1] - js[0], rows, cols), kind)]
-        if js[1] - js[0] == blocks:
-            out_shape = [pltpu.HBM((blocks, rows, cols), kind)]
+        if js[1] - js[0] > 1:
+            out_shape = [pltpu.HBM((js[1] - js[0], rows, cols), kind)]
         out_specs = [pl.BlockSpec((1, tile, cols), lambda s, col: (s // steps, s % steps, 0))]
     scratch = [
         pltpu.VMEM((depth, cols), jnp.float32),
@@ -440,7 +440,7 @@
     slots = 2 * n + LAG * (n_row - 2)
 
     turned = jnp.transpose(panel_t, (0, 2, 3, 1)).reshape(2 * blocks, -1, panel_t.shape[1])
-    gathered = [lax.all_gather(turned[i:i + blocks], "col") for i in (0, blocks)]
+    gathered = [lax.all_gather(turned[:2], "col"), lax.all_gather(turned[2:], "col")]
 
     *sent, part2, part3 = copies(
         [inverse_blocks, right_side], [(share + half, cols), (share, cols)] + halves, start, []
@@ -487,7 +487,8 @@
             part, = copies([inverse_blocks], [halves[t - 2]], cut(1, [t]), here)
             arrived = send(part, [(t, 1)])
             inverse[1].append([arrived, swap(arrived)])
-            after = after + [arrived]
+        if t in (3, 4):
+            after = after + inverse[1][t - 1][:1]
         if t == n:
             inverse[1][0] = received[n]
         if t == n + LAG - 1:
@@ -505,17 +506,21 @@
             remaining = update(
                 right_side,
                 0,
-                [(gathered[0], 0, blocks, 0, n_col, 0, 0)],
+                [(gathered[0], 0, 2, 0, n_col, 0, 0)],
                 chunks_of(0, 0, n),
                 here,
-                (0, blocks),
+                (0, 2),
                 fresh=True,
             )
+    both = [x + y for x, y in zip(chunks_of(0, 0, n), chunks_of(1, 0, n))]
     remaining, solved = update(
-        remaining,
+        [remaining, right_side],
         1,
-        [(gathered[1], 0, blocks, 0, n_col, 0, 0)],
-        chunks_of(1, 0, n),
+        [
+            (gathered[1], 2, 3, 0, n_col, 0, 0),
+            (gathered[1], 0, blocks, 0, n_col, n * share, 1),
+        ],
+        both,
         [],
         (0, blocks),
         solved=[[chunks_of(k, r, r + 1)[r] for r in range(n_row)] for k in range(2)],

time: 192 us -> 190 us (0.990)
  starting transfers between devices: 52 us -> 43.5 us
  waiting for transfers between devices: 64.6 us -> 71.2 us
  local copies, waits for them, and re-layouts: 9.81 us -> 7.65 us
    ppermute x24, starting transfers between devices: 51.4 us -> 42.4 us  [send(): return lax.ppermute(value, 'row', pairs)]
    ppermute x24, waiting for transfers between devices: 58.8 us -> 64.9 us  [send(): return lax.ppermute(value, 'row', pairs)]
    unnamed x49 -> x54, local copies, waits for them, and re-layouts: 7.92 us -> 2.79 us
    transpose x0 -> x1, local copies, waits for them, and re-layouts: none -> 2.37 us  [body(): jnp.transpose(panel_t, (0, 2, 3, 1))]
    pallas_call x3, Pallas kernels: 42.8 us -> 45.2 us  [update(): pl.pallas_call(kernel, grid_spec=pltpu.PrefetchScalarGridSpec(num_scalar_...]
  transfers between devices with their start and end apart: 30 -> 30, of which waited for: 8 -> 11; matrix products, arithmetic and copies ran while one was open for 0% -> 1% of each run, Pallas kernels for 17% -> 15%
where the time goes in v4:
time: 190 us; the launch traced here: 189 us
  waiting for transfers between devices  71.2 us (37%)
  Pallas kernels  51.6 us (27%)
  starting transfers between devices  43.5 us (23%)
  between operations  14.7 us (8%)
  local copies, waits for them, and re-layouts  7.65 us (4%)
    ppermute x24, waiting for transfers between devices, send(): return lax.ppermute(value, 'row', pairs)  64.9 us
    pallas_call x3, Pallas kernels, update(): pl.pallas_call(kernel, grid_spec=pltpu.PrefetchScalarGridSpec(num_scalar_...  45.2 us
    ppermute x24, starting transfers between devices, send(): return lax.ppermute(value, 'row', pairs)  42.4 us
    all_gather x1, waiting for transfers between devices, body(): lax.all_gather(turned[2:], 'col')  6.24 us
    pallas_call x8, Pallas kernels, slot(): pl.pallas_call(kernel, grid=(1,), in_specs=specs + [ANY] * (1 + len(rhs)...  3.99 us
  transfers between devices with their start and end apart: 30, of which 11 were waited for; matrix products, arithmetic and copies ran while one was open for 1% of the time, Pallas kernels for 15%

profile of v4, /device:TPU:18, one launch (start us, length us, event | category | flops | bytes accessed | tf_op | source)
XLA Modules:
  0.0 188.7 jit_solution(3379718821671374778)
XLA Ops:
  7.2 2.4 %copy.7 = f32[2,3,1024,128]{3,2,1,0:T(8,128)S(1)} copy(f32[2,3,1024,128]{2,3,1,0:T(8,128)} %bitcast.11) | data formatting | bytes 6291456 | tf_op jit(solution)/shard_map/transpose | solution.py:442
  10.7 1.5 slice.9
  12.2 1.2 shard_map.50
  14.8 2.6 %collective-permute-start.1 = (f32[128,768]{1,0:T(8,128)S(1)}, f32[128,768]{1,0:T(8,128)S(1)}, u32[]{:S(2)}, u32[]{:S(2)}) collective-permute-start(f32[128,768]{1,0:T(8,128)S(1)} %get-tuple-element.9), channel_id=1, source_target_pairs={{16,8},{17,9},{18,10},{19,11},{20,12},{21,13},{22,14},{23,15}} | collective-permute-start | bytes 1179656 | tf_op jit(solution)/shard_map/ppermute | solution.py:396
  18.0 18.5 %collective-permute-done.1.refs_4_.refs_0_ = f32[128,768]{1,0:T(8,128)S(1)} collective-permute-done((f32[128,768]{1,0:T(8,128)S(1)}, f32[128,768]{1,0:T(8,128)S(1)}, u32[]{:S(2)}, u32[]{:S(2)}) %collective-permute-start.1) | collective-permute-done | bytes 393248 | tf_op jit(solution)/shard_map/ppermute | solution.py:396
  36.6 1.3 collective-permute-start.7
  38.0 1.1 shard_map.53
  39.1 4.5 %collective-permute-start.8 = (f32[128,768]{1,0:T(8,128)S(1)}, f32[128,768]{1,0:T(8,128)S(1)}, u32[]{:S(2)}, u32[]{:S(2)}) collective-permute-start(f32[128,768]{1,0:T(8,128)S(1)} %shard_map.53), channel_id=1, source_target_pairs={{16,8},{17,9},{18,10},{19,11},{20,12},{21,13},{22,14},{23,15}} | collective-permute-start | bytes 1179656 | tf_op jit(solution)/shard_map/ppermute | solution.py:396
  45.9 1.3 collective-permute-start.11
  47.2 5.4 %collective-permute-done.8.refs_8_.refs_0_ = f32[128,768]{1,0:T(8,128)S(1)} collective-permute-done((f32[128,768]{1,0:T(8,128)S(1)}, f32[128,768]{1,0:T(8,128)S(1)}, u32[]{:S(2)}, u32[]{:S(2)}) %collective-permute-start.8) | collective-permute-done | bytes 393248 | tf_op jit(solution)/shard_map/ppermute | solution.py:396
  55.0 6.3 %collective-permute-start.14 = (f32[256,512]{1,0:T(8,128)S(1)}, f32[256,512]{1,0:T(8,128)S(1)}, u32[]{:S(2)}, u32[]{:S(2)}) collective-permute-start(f32[256,512]{1,0:T(8,128)S(1)} %shard_map.54.refs_4_.refs_8_.refs_14_), channel_id=1, source_target_pairs={{0,8},{8,16},{16,24},{1,9},{9,17},{17,25},{2,10},{10,18},{18,26},{... | collective-permute-start | bytes 1572872 | tf_op jit(solution)/shard_map/ppermute | solution.py:396
  61.3 1.5 collective-permute-start.9
  62.7 2.6 %collective-permute-done.11.refs_2_.refs_6_.refs_11_.refs_21_ = f32[256,512]{1,0:T(8,128)S(1)} collective-permute-done((f32[256,512]{1,0:T(8,128)S(1)}, f32[256,512]{1,0:T(8,128)S(1)}, u32[]{:S(2)}, u32[]{:S(2)}) %collective-permute-start.11) | collective-permute-done | bytes 524320 | tf_op jit(solution)/shard_map/ppermute | solution.py:396
  65.5 1.5 collective-permute-start.13
  67.0 6.1 %collective-permute-start.15 = (f32[256,512]{1,0:T(8,128)S(1)}, f32[256,512]{1,0:T(8,128)S(1)}, u32[]{:S(2)}, u32[]{:S(2)}) collective-permute-start(f32[256,512]{1,0:T(8,128)S(1)} %shard_map.56.refs_5_.refs_6_.refs_9_.refs_15_), channel_id=1, source_target_pairs={{8,16},{16,24},{9,17},{17,25},{10,18},{18,26},{11,19},{19,27},{12,... | collective-permute-start | bytes 1572872 | tf_op jit(solution)/shard_map/ppermute | solution.py:396
  73.3 8.5 %shard_map.57.refs_2_.refs_4_.refs_3_ = f32[1,1024,512]{2,1,0:T(8,128)S(1)} custom-call(s32[1]{0:T(128)} %bitcast.col_ref, f32[3,1024,512]{2,1,0:T(8,128)} %refs_1_.3, f32[8,2,1024,128]{3,2,1,0:T(8,128)} %bitcast.7, f32[256,512]{1,0:T(8,128)} %copy-done.2, f32[256,512]{1,0:T(8,128)} %copy-done, f32[256,512]{1,0:T(8,128)} %copy-done.7, f32[256,512]{1,0:T(8,128)} %copy-done.4, ...), custom_call_target="tpu_custom_call" | custom-call | flops 1024 | bytes 1024 | tf_op jit(solution)/shard_map/pallas_call | solution.py:363
  82.6 1.9 %collective-permute-start.16 = (f32[256,512]{1,0:T(8,128)S(1)}, f32[256,512]{1,0:T(8,128)S(1)}, u32[]{:S(2)}, u32[]{:S(2)}) collective-permute-start(f32[256,512]{1,0:T(8,128)S(1)} %shard_map.58.refs_16_), channel_id=1, source_target_pairs={{8,16},{16,24},{9,17},{17,25},{10,18},{18,26},{11,19},{19,27},{12,... | collective-permute-start | bytes 1572872 | tf_op jit(solution)/shard_map/ppermute | solution.py:396
  85.2 2.0 %collective-permute-done.15.refs_1_.refs_13_.refs_23_ = f32[256,512]{1,0:T(8,128)S(1)} collective-permute-done((f32[256,512]{1,0:T(8,128)S(1)}, f32[256,512]{1,0:T(8,128)S(1)}, u32[]{:S(2)}, u32[]{:S(2)}) %collective-permute-start.15) | collective-permute-done | bytes 524320 | tf_op jit(solution)/shard_map/ppermute | solution.py:396
  90.2 1.9 %collective-permute-start.17 = (f32[256,512]{1,0:T(8,128)S(1)}, f32[256,512]{1,0:T(8,128)S(1)}, u32[]{:S(2)}, u32[]{:S(2)}) collective-permute-start(f32[256,512]{1,0:T(8,128)S(1)} %shard_map.59.refs_17_.refs_33_), channel_id=1, source_target_pairs={{8,16},{16,24},{9,17},{17,25},{10,18},{18,26},{11,19},{19,27},{12,... | collective-permute-start | bytes 1572872 | tf_op jit(solution)/shard_map/ppermute | solution.py:396
  92.8 9.0 %collective-permute-done.16.refs_14_.refs_2_.refs_24_ = f32[256,512]{1,0:T(8,128)S(1)} collective-permute-done((f32[256,512]{1,0:T(8,128)S(1)}, f32[256,512]{1,0:T(8,128)S(1)}, u32[]{:S(2)}, u32[]{:S(2)}) %collective-permute-start.16) | collective-permute-done | bytes 524320 | tf_op jit(solution)/shard_map/ppermute | solution.py:396
  101.8 1.3 shard_map.62.refs_18_
  103.2 1.9 %collective-permute-start.25 = (f32[256,512]{1,0:T(8,128)S(1)}, f32[256,512]{1,0:T(8,128)S(1)}, u32[]{:S(2)}, u32[]{:S(2)}) collective-permute-start(f32[256,512]{1,0:T(8,128)S(1)} %shard_map.62.refs_18_), channel_id=1, source_target_pairs={{8,16},{16,24},{9,17},{17,25},{10,18},{18,26},{11,19},{19,27},{12,... | collective-permute-start | bytes 1572872 | tf_op jit(solution)/shard_map/ppermute | solution.py:396
  105.1 9.0 %collective-permute-done.17.refs_2_.refs_15_.refs_25_.refs_36_ = f32[256,512]{1,0:T(8,128)S(1)} collective-permute-done((f32[256,512]{1,0:T(8,128)S(1)}, f32[256,512]{1,0:T(8,128)S(1)}, u32[]{:S(2)}, u32[]{:S(2)}) %collective-permute-start.17) | collective-permute-done | bytes 524320 | tf_op jit(solution)/shard_map/ppermute | solution.py:396
  114.2 1.9 %collective-permute-start.20 = (f32[256,512]{1,0:T(8,128)S(1)}, f32[256,512]{1,0:T(8,128)S(1)}, u32[]{:S(2)}, u32[]{:S(2)}) collective-permute-start(f32[256,512]{1,0:T(8,128)S(1)} %shard_map.60.refs_19_), channel_id=1, source_target_pairs={{8,16},{16,24},{9,17},{17,25},{10,18},{18,26},{11,19},{19,27},{12,... | collective-permute-start | bytes 1572872 | tf_op jit(solution)/shard_map/ppermute | solution.py:396
  117.5 7.8 %collective-permute-done.25.refs_26_.refs_35_ = f32[256,512]{1,0:T(8,128)S(1)} collective-permute-done((f32[256,512]{1,0:T(8,128)S(1)}, f32[256,512]{1,0:T(8,128)S(1)}, u32[]{:S(2)}, u32[]{:S(2)}) %collective-permute-start.25) | collective-permute-done | bytes 524320 | tf_op jit(solution)/shard_map/ppermute | solution.py:396
  125.3 1.3 collective-permute-start.26
  126.6 8.4 %collective-permute-done.20.refs_16_.refs_27_ = f32[256,512]{1,0:T(8,128)S(1)} collective-permute-done((f32[256,512]{1,0:T(8,128)S(1)}, f32[256,512]{1,0:T(8,128)S(1)}, u32[]{:S(2)}, u32[]{:S(2)}) %collective-permute-start.20) | collective-permute-done | bytes 524320 | tf_op jit(solution)/shard_map/ppermute | solution.py:396
  135.0 1.5 collective-permute-start.27
  136.5 13.3 %shard_map.61.refs_0_ = f32[2,1024,512]{2,1,0:T(8,128)} custom-call(s32[1]{0:T(128)} %bitcast.col_ref, f32[3,1024,512]{2,1,0:T(8,128)} %refs_1_.3, f32[8,2,1024,128]{3,2,1,0:T(8,128)} %bitcast.8, f32[256,512]{1,0:T(8,128)} %copy-done.5, f32[256,512]{1,0:T(8,128)} %copy-done.12, f32[256,512]{1,0:T(8,128)} %collective-permute-done.9.refs_3_.refs_4_.refs_6_, ...), custom_call_target="tpu_custom_call" | custom-call | flops 1024 | bytes 1024 | tf_op jit(solution)/shard_map/pallas_call | solution.py:363
  150.8 1.5 collective-permute-done.27.refs_29_.refs_37_
  152.4 6.2 %all-gather.7.cloned.1.call-done = f32[32,1024,128]{2,1,0:T(8,128)} async-done(((f32[4,1024,128]{2,1,0:T(8,128)}), f32[32,1024,128]{2,1,0:T(8,128)}) %all-gather.7.cloned.1.call-update) | async-done | bytes 16777232 | tf_op jit(solution)/shard_map/all_gather | solution.py:443
  158.6 23.3 %shard_map.63 = (f32[3,1024,512]{2,1,0:T(8,128)}, f32[2,256,512]{2,1,0:T(8,128)}) custom-call(s32[1]{0:T(128)} %bitcast.col_ref, f32[2,1024,512]{2,1,0:T(8,128)} %shard_map.61.refs_0_, f32[3,1024,512]{2,1,0:T(8,128)} %refs_1_.3, f32[8,4,1024,128]{3,2,1,0:T(8,128)} %bitcast.5, f32[8,4,1024,128]{3,2,1,0:T(8,128)} %bitcast.6, f32[256,512]{1,0:T(8,128)} %copy-done.5, ...), custom_call_target="tpu_custom_call" | custom-call | flops 1024 | bytes 1024 | tf_op jit(solution)/shard_map/pallas_call | solution.py:363
  (101 shorter events, 15.7 us)
Async XLA Ops:
  7.2 66.1 %all-gather.5.cloned.1.call-start = ((), (), s32[]{:S(2)}) async-start(), calls=%async_computation | async-start | bytes 9437184 | tf_op jit(solution)/shard_map/all_gather | solution.py:443
  10.6 147.9 %all-gather.7.cloned.1.call-start = ((), (), s32[]{:S(2)}) async-start(), calls=%async_computation.1 | async-start | bytes 18874368 | tf_op jit(solution)/shard_map/all_gather | solution.py:443
  13.3 23.2 %collective-permute-start = (f32[384,512]{1,0:T(8,128)S(1)}, f32[384,512]{1,0:T(8,128)S(1)}, u32[]{:S(2)}, u32[]{:S(2)}) collective-permute-start(f32[384,512]{1,0:T(8,128)S(1)} %get-tuple-element.8), channel_id=1, source_target_pairs={{0,8},{1,9},{2,10},{3,11},{4,12},{5,13},{6,14},{7,15}} | collective-permute-start | bytes 2359304 | tf_op jit(solution)/shard_map/ppermute | solution.py:396
  14.1 22.4 %collective-permute-start.2 = (f32[128,1024]{1,0:T(8,128)S(1)}, f32[128,1024]{1,0:T(8,128)S(1)}, u32[]{:S(2)}, u32[]{:S(2)}) collective-permute-start(f32[128,1024]{1,0:T(8,128)S(1)} %get-tuple-element.10), channel_id=1, source_target_pairs={{24,8},{25,9},{26,10},{27,11},{28,12},{29,13},{30,14},{31,15}} | collective-permute-start | bytes 1572872 | tf_op jit(solution)/shard_map/ppermute | solution.py:396
  14.8 21.7 %collective-permute-start.1 = (f32[128,768]{1,0:T(8,128)S(1)}, f32[128,768]{1,0:T(8,128)S(1)}, u32[]{:S(2)}, u32[]{:S(2)}) collective-permute-start(f32[128,768]{1,0:T(8,128)S(1)} %get-tuple-element.9), channel_id=1, source_target_pairs={{16,8},{17,9},{18,10},{19,11},{20,12},{21,13},{22,14},{23,15}} | collective-permute-start | bytes 1179656 | tf_op jit(solution)/shard_map/ppermute | solution.py:396
  17.3 27.0 %collective-permute-start.4 = (f32[256,512]{1,0:T(8,128)S(1)}, f32[256,512]{1,0:T(8,128)S(1)}, u32[]{:S(2)}, u32[]{:S(2)}) collective-permute-start(f32[256,512]{1,0:T(8,128)S(1)} %get-tuple-element.11), channel_id=1, source_target_pairs={{0,8},{1,9},{2,10},{3,11},{4,12},{5,13},{6,14},{7,15}} | collective-permute-start | bytes 1572872 | tf_op jit(solution)/shard_map/ppermute | solution.py:396
  36.6 17.5 %collective-permute-start.7 = (f32[256,512]{1,0:T(8,128)S(1)}, f32[256,512]{1,0:T(8,128)S(1)}, u32[]{:S(2)}, u32[]{:S(2)}) collective-permute-start(f32[256,512]{1,0:T(8,128)S(1)} %shard_map.51.refs_1_.refs_2_.refs_6_.refs_12_), channel_id=1, source_target_pairs={{0,8},{8,16},{1,9},{9,17},{2,10},{10,18},{3,11},{11,19},{4,12},{12... | collective-permute-start | bytes 1572872 | tf_op jit(solution)/shard_map/ppermute | solution.py:396
  37.9 8.0 %collective-permute-start.6 = (f32[128,768]{1,0:T(8,128)S(1)}, f32[128,768]{1,0:T(8,128)S(1)}, u32[]{:S(2)}, u32[]{:S(2)}) collective-permute-start(f32[128,768]{1,0:T(8,128)S(1)} %collective-permute-done.1.refs_4_.refs_0_), channel_id=1, source_target_pairs={{0,1},{1,0},{2,3},{3,2},{4,5},{5,4},{6,7},{7,6},{8,9},{9,8},{10,11... | collective-permute-start | bytes 1179656 | tf_op jit(solution)/shard_map/ppermute | solution.py:399
  39.1 13.4 %collective-permute-start.8 = (f32[128,768]{1,0:T(8,128)S(1)}, f32[128,768]{1,0:T(8,128)S(1)}, u32[]{:S(2)}, u32[]{:S(2)}) collective-permute-start(f32[128,768]{1,0:T(8,128)S(1)} %shard_map.53), channel_id=1, source_target_pairs={{16,8},{17,9},{18,10},{19,11},{20,12},{21,13},{22,14},{23,15}} | collective-permute-start | bytes 1179656 | tf_op jit(solution)/shard_map/ppermute | solution.py:396
  43.6 11.2 %collective-permute-start.3 = (f32[256,512]{1,0:T(8,128)S(1)}, f32[256,512]{1,0:T(8,128)S(1)}, u32[]{:S(2)}, u32[]{:S(2)}) collective-permute-start(f32[256,512]{1,0:T(8,128)S(1)} %shard_map.51.refs_1_.refs_2_.refs_6_.refs_12_), channel_id=1, source_target_pairs={{8,0},{9,1},{10,2},{11,3},{12,4},{13,5},{14,6},{15,7}} | collective-permute-start | bytes 1572872 | tf_op jit(solution)/shard_map/ppermute | solution.py:396
  45.5 15.8 %collective-permute-start.10 = (f32[128,1024]{1,0:T(8,128)S(1)}, f32[128,1024]{1,0:T(8,128)S(1)}, u32[]{:S(2)}, u32[]{:S(2)}) collective-permute-start(f32[128,1024]{1,0:T(8,128)S(1)} %collective-permute-done.2.refs_5_.refs_0_), channel_id=1, source_target_pairs={{0,1},{1,0},{2,3},{3,2},{4,5},{5,4},{6,7},{7,6},{8,9},{9,8},{10,11... | collective-permute-start | bytes 1572872 | tf_op jit(solution)/shard_map/ppermute | solution.py:399
  45.9 19.5 %collective-permute-start.11 = (f32[256,512]{1,0:T(8,128)S(1)}, f32[256,512]{1,0:T(8,128)S(1)}, u32[]{:S(2)}, u32[]{:S(2)}) collective-permute-start(f32[256,512]{1,0:T(8,128)S(1)} %shard_map.52.refs_1_.refs_3_.refs_7_.refs_13_.refs_32_), channel_id=1, source_target_pairs={{0,8},{8,16},{1,9},{9,17},{2,10},{10,18},{3,11},{11,19},{4,12},{12... | collective-permute-start | bytes 1572872 | tf_op jit(solution)/shard_map/ppermute | solution.py:396
  52.6 10.1 %collective-permute-start.12 = (f32[128,1024]{1,0:T(8,128)S(1)}, f32[128,1024]{1,0:T(8,128)S(1)}, u32[]{:S(2)}, u32[]{:S(2)}) collective-permute-start(f32[128,1024]{1,0:T(8,128)S(1)} %shard_map.55), channel_id=1, source_target_pairs={{24,8},{25,9},{26,10},{27,11},{28,12},{29,13},{30,14},{31,15}} | collective-permute-start | bytes 1572872 | tf_op jit(solution)/shard_map/ppermute | solution.py:396
  54.1 11.2 %collective-permute-start.5 = (f32[256,512]{1,0:T(8,128)S(1)}, f32[256,512]{1,0:T(8,128)S(1)}, u32[]{:S(2)}, u32[]{:S(2)}) collective-permute-start(f32[256,512]{1,0:T(8,128)S(1)} %shard_map.52.refs_1_.refs_3_.refs_7_.refs_13_.refs_32_), channel_id=1, source_target_pairs={{8,0},{9,1},{10,2},{11,3},{12,4},{13,5},{14,6},{15,7}} | collective-permute-start | bytes 1572872 | tf_op jit(solution)/shard_map/ppermute | solution.py:396
  55.0 26.9 %collective-permute-start.14 = (f32[256,512]{1,0:T(8,128)S(1)}, f32[256,512]{1,0:T(8,128)S(1)}, u32[]{:S(2)}, u32[]{:S(2)}) collective-permute-start(f32[256,512]{1,0:T(8,128)S(1)} %shard_map.54.refs_4_.refs_8_.refs_14_), channel_id=1, source_target_pairs={{0,8},{8,16},{16,24},{1,9},{9,17},{17,25},{2,10},{10,18},{18,26},{... | collective-permute-start | bytes 1572872 | tf_op jit(solution)/shard_map/ppermute | solution.py:396
  61.3 21.3 %collective-permute-start.9 = (f32[256,512]{1,0:T(8,128)S(1)}, f32[256,512]{1,0:T(8,128)}, u32[]{:S(2)}, u32[]{:S(2)}) collective-permute-start(f32[256,512]{1,0:T(8,128)S(1)} %shard_map.54.refs_4_.refs_8_.refs_14_), channel_id=1, source_target_pairs={{8,0},{9,1},{10,2},{11,3},{12,4},{13,5},{14,6},{15,7}} | collective-permute-start | bytes 1572872 | tf_op jit(solution)/shard_map/ppermute | solution.py:396
  65.5 19.0 %collective-permute-start.13 = (f32[256,512]{1,0:T(8,128)S(1)}, f32[256,512]{1,0:T(8,128)}, u32[]{:S(2)}, u32[]{:S(2)}) collective-permute-start(f32[256,512]{1,0:T(8,128)S(1)} %shard_map.56.refs_5_.refs_6_.refs_9_.refs_15_), channel_id=1, source_target_pairs={{8,0},{9,1},{10,2},{11,3},{12,4},{13,5},{14,6},{15,7}} | collective-permute-start | bytes 1572872 | tf_op jit(solution)/shard_map/ppermute | solution.py:396
  67.0 20.2 %collective-permute-start.15 = (f32[256,512]{1,0:T(8,128)S(1)}, f32[256,512]{1,0:T(8,128)S(1)}, u32[]{:S(2)}, u32[]{:S(2)}) collective-permute-start(f32[256,512]{1,0:T(8,128)S(1)} %shard_map.56.refs_5_.refs_6_.refs_9_.refs_15_), channel_id=1, source_target_pairs={{8,16},{16,24},{9,17},{17,25},{10,18},{18,26},{11,19},{19,27},{12,... | collective-permute-start | bytes 1572872 | tf_op jit(solution)/shard_map/ppermute | solution.py:396
  73.1 19.0 %collective-permute-start.22 = (f32[128,768]{1,0:T(8,128)S(1)}, f32[128,768]{1,0:T(8,128)}, u32[]{:S(2)}, u32[]{:S(2)}) collective-permute-start(f32[128,768]{1,0:T(8,128)S(1)} %collective-permute-done.8.refs_8_.refs_0_), channel_id=1, source_target_pairs={{0,1},{1,0},{2,3},{3,2},{4,5},{5,4},{6,7},{7,6},{8,9},{9,8},{10,11... | collective-permute-start | bytes 1179656 | tf_op jit(solution)/shard_map/ppermute | solution.py:399
  81.9 23.2 %collective-permute-start.18 = (f32[128,1024]{1,0:T(8,128)S(1)}, f32[128,1024]{1,0:T(8,128)S(1)}, u32[]{:S(2)}, u32[]{:S(2)}) collective-permute-start(f32[128,1024]{1,0:T(8,128)S(1)} %copy-done.21), channel_id=1, source_target_pairs={{0,1},{1,0},{2,3},{3,2},{4,5},{5,4},{6,7},{7,6},{8,9},{9,8},{10,11... | collective-permute-start | bytes 1572872 | tf_op jit(solution)/shard_map/ppermute | solution.py:399
  82.6 67.3 %copy-start.15 = (f32[256,512]{1,0:T(8,128)}, f32[256,512]{1,0:T(8,128)S(1)}, u32[]{:S(2)}) copy-start(f32[256,512]{1,0:T(8,128)S(1)} %shard_map.58.refs_16_) | copy-start | bytes 1572868
  82.6 19.2 %collective-permute-start.16 = (f32[256,512]{1,0:T(8,128)S(1)}, f32[256,512]{1,0:T(8,128)S(1)}, u32[]{:S(2)}, u32[]{:S(2)}) collective-permute-start(f32[256,512]{1,0:T(8,128)S(1)} %shard_map.58.refs_16_), channel_id=1, source_target_pairs={{8,16},{16,24},{9,17},{17,25},{10,18},{18,26},{11,19},{19,27},{12,... | collective-permute-start | bytes 1572872 | tf_op jit(solution)/shard_map/ppermute | solution.py:396
  84.5 17.3 %collective-permute-start.21 = (f32[256,512]{1,0:T(8,128)S(1)}, f32[256,512]{1,0:T(8,128)S(1)}, u32[]{:S(2)}, u32[]{:S(2)}) collective-permute-start(f32[256,512]{1,0:T(8,128)S(1)} %shard_map.58.refs_16_), channel_id=1, source_target_pairs={{8,0},{9,1},{10,2},{11,3},{12,4},{13,5},{14,6},{15,7}} | collective-permute-start | bytes 1572872 | tf_op jit(solution)/shard_map/ppermute | solution.py:396
  90.2 23.9 %collective-permute-start.17 = (f32[256,512]{1,0:T(8,128)S(1)}, f32[256,512]{1,0:T(8,128)S(1)}, u32[]{:S(2)}, u32[]{:S(2)}) collective-permute-start(f32[256,512]{1,0:T(8,128)S(1)} %shard_map.59.refs_17_.refs_33_), channel_id=1, source_target_pairs={{8,16},{16,24},{9,17},{17,25},{10,18},{18,26},{11,19},{19,27},{12,... | collective-permute-start | bytes 1572872 | tf_op jit(solution)/shard_map/ppermute | solution.py:396
  92.1 22.0 %collective-permute-start.19 = (f32[256,512]{1,0:T(8,128)S(1)}, f32[256,512]{1,0:T(8,128)S(1)}, u32[]{:S(2)}, u32[]{:S(2)}) collective-permute-start(f32[256,512]{1,0:T(8,128)S(1)} %shard_map.59.refs_17_.refs_33_), channel_id=1, source_target_pairs={{8,0},{9,1},{10,2},{11,3},{12,4},{13,5},{14,6},{15,7}} | collective-permute-start | bytes 1572872 | tf_op jit(solution)/shard_map/ppermute | solution.py:396
  103.2 46.7 %copy-start.17 = (f32[256,512]{1,0:T(8,128)}, f32[256,512]{1,0:T(8,128)S(1)}, u32[]{:S(2)}) copy-start(f32[256,512]{1,0:T(8,128)S(1)} %shard_map.62.refs_18_) | copy-start | bytes 1572868
  103.2 22.1 %collective-permute-start.25 = (f32[256,512]{1,0:T(8,128)S(1)}, f32[256,512]{1,0:T(8,128)S(1)}, u32[]{:S(2)}, u32[]{:S(2)}) collective-permute-start(f32[256,512]{1,0:T(8,128)S(1)} %shard_map.62.refs_18_), channel_id=1, source_target_pairs={{8,16},{16,24},{9,17},{17,25},{10,18},{18,26},{11,19},{19,27},{12,... | collective-permute-start | bytes 1572872 | tf_op jit(solution)/shard_map/ppermute | solution.py:396
  114.2 20.8 %collective-permute-start.20 = (f32[256,512]{1,0:T(8,128)S(1)}, f32[256,512]{1,0:T(8,128)S(1)}, u32[]{:S(2)}, u32[]{:S(2)}) collective-permute-start(f32[256,512]{1,0:T(8,128)S(1)} %shard_map.60.refs_19_), channel_id=1, source_target_pairs={{8,16},{16,24},{9,17},{17,25},{10,18},{18,26},{11,19},{19,27},{12,... | collective-permute-start | bytes 1572872 | tf_op jit(solution)/shard_map/ppermute | solution.py:396
  116.1 33.8 %collective-permute-start.23 = (f32[256,512]{1,0:T(8,128)S(1)}, f32[256,512]{1,0:T(8,128)S(1)}, u32[]{:S(2)}, u32[]{:S(2)}) collective-permute-start(f32[256,512]{1,0:T(8,128)S(1)} %shard_map.62.refs_18_), channel_id=1, source_target_pairs={{8,0},{9,1},{10,2},{11,3},{12,4},{13,5},{14,6},{15,7}} | collective-permute-start | bytes 1572872 | tf_op jit(solution)/shard_map/ppermute | solution.py:396
  116.8 33.1 %collective-permute-start.24 = (f32[256,512]{1,0:T(8,128)S(1)}, f32[256,512]{1,0:T(8,128)S(1)}, u32[]{:S(2)}, u32[]{:S(2)}) collective-permute-start(f32[256,512]{1,0:T(8,128)S(1)} %shard_map.60.refs_19_), channel_id=1, source_target_pairs={{8,0},{9,1},{10,2},{11,3},{12,4},{13,5},{14,6},{15,7}} | collective-permute-start | bytes 1572872 | tf_op jit(solution)/shard_map/ppermute | solution.py:396
  125.3 24.6 %collective-permute-start.26 = (f32[256,512]{1,0:T(8,128)S(1)}, f32[256,512]{1,0:T(8,128)S(1)}, u32[]{:S(2)}, u32[]{:S(2)}) collective-permute-start(f32[256,512]{1,0:T(8,128)S(1)} %collective-permute-done.25.refs_26_.refs_35_), channel_id=1, source_target_pairs={{16,24},{17,25},{18,26},{19,27},{20,28},{21,29},{22,30},{23,31}} | collective-permute-start | bytes 1572872 | tf_op jit(solution)/shard_map/ppermute | solution.py:396
  135.0 17.3 %collective-permute-start.27 = (f32[256,512]{1,0:T(8,128)S(1)}, f32[256,512]{1,0:T(8,128)S(1)}, u32[]{:S(2)}, u32[]{:S(2)}) collective-permute-start(f32[256,512]{1,0:T(8,128)S(1)} %collective-permute-done.20.refs_16_.refs_27_), channel_id=1, source_target_pairs={{16,24},{17,25},{18,26},{19,27},{20,28},{21,29},{22,30},{23,31}} | collective-permute-start | bytes 1572872 | tf_op jit(solution)/shard_map/ppermute | solution.py:396
  (25 other events, 320.3 us)
Sparse Core Ops, SparseCore 0:
  10.8 55.4 all-gather.4
  68.7 89.8 all-gather.6

commit v5 on v4

--- a/solution.py
+++ b/solution.py
@@ -225,18 +225,18 @@
     )(*inverse, received, *rhs, *tops, *after)
 
 
-def fetch(where, refs, whole, sems, height, my_row):
+def fetch(where, refs, whole, sems, height, my_row, first, end, start, wait):
     for row, ids in enumerate(where):
 
         @pl.when((my_row == row) | (len(where) == 1))
         def _():
             copies = [
-                pltpu.make_async_copy(refs[i], whole.at[pl.ds(n * height, height)], sems.at[n])
-                for n, i in enumerate(ids)
+                pltpu.make_async_copy(refs[ids[n]], whole.at[pl.ds(n * height, height)], sems.at[n])
+                for n in range(first, end)
             ]
-            for copy in copies:
+            for copy in copies if start else []:
                 copy.start()
-            for copy in copies:
+            for copy in copies if wait else []:
                 copy.wait()
 
 
@@ -248,7 +248,9 @@
     steps = rows // tile
     arrays, where = distinct(sources)
     height = arrays[0].shape[0]
-    depth = height * len(where[0])
+    chunks = len(where[0])
+    depth = height * chunks
+    late = min(part[5] for part in parts[1:]) // height if len(parts) > 1 else 0
     given, given_where = distinct([a + b for a, b in zip(*solved)]) if solved else ([], [])
     last = len(given) > 0
     panels = []
@@ -296,12 +298,23 @@
 
         @pl.when(step == 0)
         def _():
-            fetch(where, chunk_refs, whole, sems, height, my_row)
-            hi, lo = split(whole[...])
-            x_hi[...] = hi
-            x_lo[...] = lo
+            fetch(where, chunk_refs, whole, sems, height, my_row, late, chunks, True, False)
+            fetch(where, chunk_refs, whole, sems, height, my_row, 0, late, True, False)
+            fetch(where, chunk_refs, whole, sems, height, my_row, late, chunks, False, True)
+            hi, lo = split(whole[late * height:])
+            x_hi[late * height:] = hi
+            x_lo[late * height:] = lo
             if last:
                 give(True)
+
+        if late:
+
+            @pl.when(step == (parts[0][1] - js[0]) * steps)
+            def _():
+                fetch(where, chunk_refs, whole, sems, height, my_row, 0, late, False, True)
+                hi, lo = split(whole[:late * height])
+                x_hi[:late * height] = hi
+                x_lo[:late * height] = lo
 
         j = js[0] + step // steps
         old = rhs_refs[0][0]

time: 190 us -> 189 us (level)
  no operation moved by 1% of the time
where the time goes in v5:
time: 189 us; the launch traced here: 188 us
  waiting for transfers between devices  71.2 us (38%)
  Pallas kernels  50.9 us (27%)
  starting transfers between devices  43.5 us (23%)
  between operations  14.7 us (8%)
  local copies, waits for them, and re-layouts  7.65 us (4%)
    ppermute x24, waiting for transfers between devices, send(): return lax.ppermute(value, 'row', pairs)  64.9 us
    pallas_call x3, Pallas kernels, update(): pl.pallas_call(kernel, grid_spec=pltpu.PrefetchScalarGridSpec(num_scalar_...  44.5 us
    ppermute x24, starting transfers between devices, send(): return lax.ppermute(value, 'row', pairs)  42.4 us
    all_gather x1, waiting for transfers between devices, body(): lax.all_gather(turned[2:], 'col')  6.24 us
    pallas_call x8, Pallas kernels, slot(): pl.pallas_call(kernel, grid=(1,), in_specs=specs + [ANY] * (1 + len(rhs)...  3.99 us
  transfers between devices with their start and end apart: 30, of which 11 were waited for; matrix products, arithmetic and copies ran while one was open for 1% of the time, Pallas kernels for 15%

profile of v5, /device:TPU:18, one launch (start us, length us, event | category | flops | bytes accessed | tf_op | source)
XLA Modules:
  0.0 188.1 jit_solution(10795594616029329703)
XLA Ops:
  7.2 2.4 %copy.7 = f32[2,3,1024,128]{3,2,1,0:T(8,128)S(1)} copy(f32[2,3,1024,128]{2,3,1,0:T(8,128)} %bitcast.11) | data formatting | bytes 6291456 | tf_op jit(solution)/shard_map/transpose | solution.py:455
  10.7 1.5 slice.9
  12.2 1.2 shard_map.50
  14.8 2.6 %collective-permute-start.1 = (f32[128,768]{1,0:T(8,128)S(1)}, f32[128,768]{1,0:T(8,128)S(1)}, u32[]{:S(2)}, u32[]{:S(2)}) collective-permute-start(f32[128,768]{1,0:T(8,128)S(1)} %get-tuple-element.9), channel_id=1, source_target_pairs={{16,8},{17,9},{18,10},{19,11},{20,12},{21,13},{22,14},{23,15}} | collective-permute-start | bytes 1179656 | tf_op jit(solution)/shard_map/ppermute | solution.py:409
  18.0 18.5 %collective-permute-done.1.refs_4_.refs_0_ = f32[128,768]{1,0:T(8,128)S(1)} collective-permute-done((f32[128,768]{1,0:T(8,128)S(1)}, f32[128,768]{1,0:T(8,128)S(1)}, u32[]{:S(2)}, u32[]{:S(2)}) %collective-permute-start.1) | collective-permute-done | bytes 393248 | tf_op jit(solution)/shard_map/ppermute | solution.py:409
  36.6 1.3 collective-permute-start.7
  38.0 1.1 shard_map.53
  39.1 4.5 %collective-permute-start.8 = (f32[128,768]{1,0:T(8,128)S(1)}, f32[128,768]{1,0:T(8,128)S(1)}, u32[]{:S(2)}, u32[]{:S(2)}) collective-permute-start(f32[128,768]{1,0:T(8,128)S(1)} %shard_map.53), channel_id=1, source_target_pairs={{16,8},{17,9},{18,10},{19,11},{20,12},{21,13},{22,14},{23,15}} | collective-permute-start | bytes 1179656 | tf_op jit(solution)/shard_map/ppermute | solution.py:409
  45.9 1.3 collective-permute-start.11
  47.2 5.4 %collective-permute-done.8.refs_8_.refs_0_ = f32[128,768]{1,0:T(8,128)S(1)} collective-permute-done((f32[128,768]{1,0:T(8,128)S(1)}, f32[128,768]{1,0:T(8,128)S(1)}, u32[]{:S(2)}, u32[]{:S(2)}) %collective-permute-start.8) | collective-permute-done | bytes 393248 | tf_op jit(solution)/shard_map/ppermute | solution.py:409
  55.0 6.3 %collective-permute-start.14 = (f32[256,512]{1,0:T(8,128)S(1)}, f32[256,512]{1,0:T(8,128)S(1)}, u32[]{:S(2)}, u32[]{:S(2)}) collective-permute-start(f32[256,512]{1,0:T(8,128)S(1)} %shard_map.54.refs_4_.refs_8_.refs_14_), channel_id=1, source_target_pairs={{0,8},{8,16},{16,24},{1,9},{9,17},{17,25},{2,10},{10,18},{18,26},{... | collective-permute-start | bytes 1572872 | tf_op jit(solution)/shard_map/ppermute | solution.py:409
  61.3 1.5 collective-permute-start.9
  62.7 2.6 %collective-permute-done.11.refs_2_.refs_6_.refs_11_.refs_21_ = f32[256,512]{1,0:T(8,128)S(1)} collective-permute-done((f32[256,512]{1,0:T(8,128)S(1)}, f32[256,512]{1,0:T(8,128)S(1)}, u32[]{:S(2)}, u32[]{:S(2)}) %collective-permute-start.11) | collective-permute-done | bytes 524320 | tf_op jit(solution)/shard_map/ppermute | solution.py:409
  65.5 1.5 collective-permute-start.13
  67.0 6.1 %collective-permute-start.15 = (f32[256,512]{1,0:T(8,128)S(1)}, f32[256,512]{1,0:T(8,128)S(1)}, u32[]{:S(2)}, u32[]{:S(2)}) collective-permute-start(f32[256,512]{1,0:T(8,128)S(1)} %shard_map.56.refs_5_.refs_6_.refs_9_.refs_15_), channel_id=1, source_target_pairs={{8,16},{16,24},{9,17},{17,25},{10,18},{18,26},{11,19},{19,27},{12,... | collective-permute-start | bytes 1572872 | tf_op jit(solution)/shard_map/ppermute | solution.py:409
  73.3 8.5 %shard_map.57.refs_2_.refs_4_.refs_3_ = f32[1,1024,512]{2,1,0:T(8,128)S(1)} custom-call(s32[1]{0:T(128)} %bitcast.col_ref, f32[3,1024,512]{2,1,0:T(8,128)} %refs_1_.3, f32[8,2,1024,128]{3,2,1,0:T(8,128)} %bitcast.7, f32[256,512]{1,0:T(8,128)} %copy-done.2, f32[256,512]{1,0:T(8,128)} %copy-done, f32[256,512]{1,0:T(8,128)} %copy-done.7, f32[256,512]{1,0:T(8,128)} %copy-done.4, ...), custom_call_target="tpu_custom_call" | custom-call | flops 1024 | bytes 1024 | tf_op jit(solution)/shard_map/pallas_call | solution.py:376
  82.6 1.9 %collective-permute-start.16 = (f32[256,512]{1,0:T(8,128)S(1)}, f32[256,512]{1,0:T(8,128)S(1)}, u32[]{:S(2)}, u32[]{:S(2)}) collective-permute-start(f32[256,512]{1,0:T(8,128)S(1)} %shard_map.58.refs_16_), channel_id=1, source_target_pairs={{8,16},{16,24},{9,17},{17,25},{10,18},{18,26},{11,19},{19,27},{12,... | collective-permute-start | bytes 1572872 | tf_op jit(solution)/shard_map/ppermute | solution.py:409
  85.2 2.0 %collective-permute-done.15.refs_1_.refs_13_.refs_23_ = f32[256,512]{1,0:T(8,128)S(1)} collective-permute-done((f32[256,512]{1,0:T(8,128)S(1)}, f32[256,512]{1,0:T(8,128)S(1)}, u32[]{:S(2)}, u32[]{:S(2)}) %collective-permute-start.15) | collective-permute-done | bytes 524320 | tf_op jit(solution)/shard_map/ppermute | solution.py:409
  90.2 1.9 %collective-permute-start.17 = (f32[256,512]{1,0:T(8,128)S(1)}, f32[256,512]{1,0:T(8,128)S(1)}, u32[]{:S(2)}, u32[]{:S(2)}) collective-permute-start(f32[256,512]{1,0:T(8,128)S(1)} %shard_map.59.refs_17_.refs_33_), channel_id=1, source_target_pairs={{8,16},{16,24},{9,17},{17,25},{10,18},{18,26},{11,19},{19,27},{12,... | collective-permute-start | bytes 1572872 | tf_op jit(solution)/shard_map/ppermute | solution.py:409
  92.8 9.0 %collective-permute-done.16.refs_14_.refs_2_.refs_24_ = f32[256,512]{1,0:T(8,128)S(1)} collective-permute-done((f32[256,512]{1,0:T(8,128)S(1)}, f32[256,512]{1,0:T(8,128)S(1)}, u32[]{:S(2)}, u32[]{:S(2)}) %collective-permute-start.16) | collective-permute-done | bytes 524320 | tf_op jit(solution)/shard_map/ppermute | solution.py:409
  101.8 1.3 shard_map.62.refs_18_
  103.2 1.9 %collective-permute-start.25 = (f32[256,512]{1,0:T(8,128)S(1)}, f32[256,512]{1,0:T(8,128)S(1)}, u32[]{:S(2)}, u32[]{:S(2)}) collective-permute-start(f32[256,512]{1,0:T(8,128)S(1)} %shard_map.62.refs_18_), channel_id=1, source_target_pairs={{8,16},{16,24},{9,17},{17,25},{10,18},{18,26},{11,19},{19,27},{12,... | collective-permute-start | bytes 1572872 | tf_op jit(solution)/shard_map/ppermute | solution.py:409
  105.1 9.0 %collective-permute-done.17.refs_2_.refs_15_.refs_25_.refs_36_ = f32[256,512]{1,0:T(8,128)S(1)} collective-permute-done((f32[256,512]{1,0:T(8,128)S(1)}, f32[256,512]{1,0:T(8,128)S(1)}, u32[]{:S(2)}, u32[]{:S(2)}) %collective-permute-start.17) | collective-permute-done | bytes 524320 | tf_op jit(solution)/shard_map/ppermute | solution.py:409
  114.2 1.9 %collective-permute-start.20 = (f32[256,512]{1,0:T(8,128)S(1)}, f32[256,512]{1,0:T(8,128)S(1)}, u32[]{:S(2)}, u32[]{:S(2)}) collective-permute-start(f32[256,512]{1,0:T(8,128)S(1)} %shard_map.60.refs_19_), channel_id=1, source_target_pairs={{8,16},{16,24},{9,17},{17,25},{10,18},{18,26},{11,19},{19,27},{12,... | collective-permute-start | bytes 1572872 | tf_op jit(solution)/shard_map/ppermute | solution.py:409
  117.5 7.8 %collective-permute-done.25.refs_26_.refs_35_ = f32[256,512]{1,0:T(8,128)S(1)} collective-permute-done((f32[256,512]{1,0:T(8,128)S(1)}, f32[256,512]{1,0:T(8,128)S(1)}, u32[]{:S(2)}, u32[]{:S(2)}) %collective-permute-start.25) | collective-permute-done | bytes 524320 | tf_op jit(solution)/shard_map/ppermute | solution.py:409
  125.3 1.3 collective-permute-start.26
  126.6 8.4 %collective-permute-done.20.refs_16_.refs_27_ = f32[256,512]{1,0:T(8,128)S(1)} collective-permute-done((f32[256,512]{1,0:T(8,128)S(1)}, f32[256,512]{1,0:T(8,128)S(1)}, u32[]{:S(2)}, u32[]{:S(2)}) %collective-permute-start.20) | collective-permute-done | bytes 524320 | tf_op jit(solution)/shard_map/ppermute | solution.py:409
  135.0 1.5 collective-permute-start.27
  136.5 13.3 %shard_map.61.refs_0_ = f32[2,1024,512]{2,1,0:T(8,128)} custom-call(s32[1]{0:T(128)} %bitcast.col_ref, f32[3,1024,512]{2,1,0:T(8,128)} %refs_1_.3, f32[8,2,1024,128]{3,2,1,0:T(8,128)} %bitcast.8, f32[256,512]{1,0:T(8,128)} %copy-done.5, f32[256,512]{1,0:T(8,128)} %copy-done.12, f32[256,512]{1,0:T(8,128)} %collective-permute-done.9.refs_3_.refs_4_.refs_6_, ...), custom_call_target="tpu_custom_call" | custom-call | flops 1024 | bytes 1024 | tf_op jit(solution)/shard_map/pallas_call | solution.py:376
  150.8 1.5 collective-permute-done.27.refs_29_.refs_37_
  152.4 6.2 %all-gather.7.cloned.1.call-done = f32[32,1024,128]{2,1,0:T(8,128)} async-done(((f32[4,1024,128]{2,1,0:T(8,128)}), f32[32,1024,128]{2,1,0:T(8,128)}) %all-gather.7.cloned.1.call-update) | async-done | bytes 16777232 | tf_op jit(solution)/shard_map/all_gather | solution.py:456
  158.6 22.6 %shard_map.63 = (f32[3,1024,512]{2,1,0:T(8,128)}, f32[2,256,512]{2,1,0:T(8,128)}) custom-call(s32[1]{0:T(128)} %bitcast.col_ref, f32[2,1024,512]{2,1,0:T(8,128)} %shard_map.61.refs_0_, f32[3,1024,512]{2,1,0:T(8,128)} %refs_1_.3, f32[8,4,1024,128]{3,2,1,0:T(8,128)} %bitcast.5, f32[8,4,1024,128]{3,2,1,0:T(8,128)} %bitcast.6, f32[256,512]{1,0:T(8,128)} %copy-done.5, ...), custom_call_target="tpu_custom_call" | custom-call | flops 1024 | bytes 1024 | tf_op jit(solution)/shard_map/pallas_call | solution.py:376
  (101 shorter events, 15.7 us)
Async XLA Ops:
  7.2 66.1 %all-gather.5.cloned.1.call-start = ((), (), s32[]{:S(2)}) async-start(), calls=%async_computation | async-start | bytes 9437184 | tf_op jit(solution)/shard_map/all_gather | solution.py:456
  10.6 147.9 %all-gather.7.cloned.1.call-start = ((), (), s32[]{:S(2)}) async-start(), calls=%async_computation.1 | async-start | bytes 18874368 | tf_op jit(solution)/shard_map/all_gather | solution.py:456
  13.3 23.2 %collective-permute-start = (f32[384,512]{1,0:T(8,128)S(1)}, f32[384,512]{1,0:T(8,128)S(1)}, u32[]{:S(2)}, u32[]{:S(2)}) collective-permute-start(f32[384,512]{1,0:T(8,128)S(1)} %get-tuple-element.8), channel_id=1, source_target_pairs={{0,8},{1,9},{2,10},{3,11},{4,12},{5,13},{6,14},{7,15}} | collective-permute-start | bytes 2359304 | tf_op jit(solution)/shard_map/ppermute | solution.py:409
  14.1 22.4 %collective-permute-start.2 = (f32[128,1024]{1,0:T(8,128)S(1)}, f32[128,1024]{1,0:T(8,128)S(1)}, u32[]{:S(2)}, u32[]{:S(2)}) collective-permute-start(f32[128,1024]{1,0:T(8,128)S(1)} %get-tuple-element.10), channel_id=1, source_target_pairs={{24,8},{25,9},{26,10},{27,11},{28,12},{29,13},{30,14},{31,15}} | collective-permute-start | bytes 1572872 | tf_op jit(solution)/shard_map/ppermute | solution.py:409
  14.8 21.7 %collective-permute-start.1 = (f32[128,768]{1,0:T(8,128)S(1)}, f32[128,768]{1,0:T(8,128)S(1)}, u32[]{:S(2)}, u32[]{:S(2)}) collective-permute-start(f32[128,768]{1,0:T(8,128)S(1)} %get-tuple-element.9), channel_id=1, source_target_pairs={{16,8},{17,9},{18,10},{19,11},{20,12},{21,13},{22,14},{23,15}} | collective-permute-start | bytes 1179656 | tf_op jit(solution)/shard_map/ppermute | solution.py:409
  17.3 27.0 %collective-permute-start.4 = (f32[256,512]{1,0:T(8,128)S(1)}, f32[256,512]{1,0:T(8,128)S(1)}, u32[]{:S(2)}, u32[]{:S(2)}) collective-permute-start(f32[256,512]{1,0:T(8,128)S(1)} %get-tuple-element.11), channel_id=1, source_target_pairs={{0,8},{1,9},{2,10},{3,11},{4,12},{5,13},{6,14},{7,15}} | collective-permute-start | bytes 1572872 | tf_op jit(solution)/shard_map/ppermute | solution.py:409
  36.6 17.5 %collective-permute-start.7 = (f32[256,512]{1,0:T(8,128)S(1)}, f32[256,512]{1,0:T(8,128)S(1)}, u32[]{:S(2)}, u32[]{:S(2)}) collective-permute-start(f32[256,512]{1,0:T(8,128)S(1)} %shard_map.51.refs_1_.refs_2_.refs_6_.refs_12_), channel_id=1, source_target_pairs={{0,8},{8,16},{1,9},{9,17},{2,10},{10,18},{3,11},{11,19},{4,12},{12... | collective-permute-start | bytes 1572872 | tf_op jit(solution)/shard_map/ppermute | solution.py:409
  37.9 8.0 %collective-permute-start.6 = (f32[128,768]{1,0:T(8,128)S(1)}, f32[128,768]{1,0:T(8,128)S(1)}, u32[]{:S(2)}, u32[]{:S(2)}) collective-permute-start(f32[128,768]{1,0:T(8,128)S(1)} %collective-permute-done.1.refs_4_.refs_0_), channel_id=1, source_target_pairs={{0,1},{1,0},{2,3},{3,2},{4,5},{5,4},{6,7},{7,6},{8,9},{9,8},{10,11... | collective-permute-start | bytes 1179656 | tf_op jit(solution)/shard_map/ppermute | solution.py:412
  39.1 13.4 %collective-permute-start.8 = (f32[128,768]{1,0:T(8,128)S(1)}, f32[128,768]{1,0:T(8,128)S(1)}, u32[]{:S(2)}, u32[]{:S(2)}) collective-permute-start(f32[128,768]{1,0:T(8,128)S(1)} %shard_map.53), channel_id=1, source_target_pairs={{16,8},{17,9},{18,10},{19,11},{20,12},{21,13},{22,14},{23,15}} | collective-permute-start | bytes 1179656 | tf_op jit(solution)/shard_map/ppermute | solution.py:409
  43.6 11.2 %collective-permute-start.3 = (f32[256,512]{1,0:T(8,128)S(1)}, f32[256,512]{1,0:T(8,128)S(1)}, u32[]{:S(2)}, u32[]{:S(2)}) collective-permute-start(f32[256,512]{1,0:T(8,128)S(1)} %shard_map.51.refs_1_.refs_2_.refs_6_.refs_12_), channel_id=1, source_target_pairs={{8,0},{9,1},{10,2},{11,3},{12,4},{13,5},{14,6},{15,7}} | collective-permute-start | bytes 1572872 | tf_op jit(solution)/shard_map/ppermute | solution.py:409
  45.5 15.8 %collective-permute-start.10 = (f32[128,1024]{1,0:T(8,128)S(1)}, f32[128,1024]{1,0:T(8,128)S(1)}, u32[]{:S(2)}, u32[]{:S(2)}) collective-permute-start(f32[128,1024]{1,0:T(8,128)S(1)} %collective-permute-done.2.refs_5_.refs_0_), channel_id=1, source_target_pairs={{0,1},{1,0},{2,3},{3,2},{4,5},{5,4},{6,7},{7,6},{8,9},{9,8},{10,11... | collective-permute-start | bytes 1572872 | tf_op jit(solution)/shard_map/ppermute | solution.py:412
  45.9 19.5 %collective-permute-start.11 = (f32[256,512]{1,0:T(8,128)S(1)}, f32[256,512]{1,0:T(8,128)S(1)}, u32[]{:S(2)}, u32[]{:S(2)}) collective-permute-start(f32[256,512]{1,0:T(8,128)S(1)} %shard_map.52.refs_1_.refs_3_.refs_7_.refs_13_.refs_32_), channel_id=1, source_target_pairs={{0,8},{8,16},{1,9},{9,17},{2,10},{10,18},{3,11},{11,19},{4,12},{12... | collective-permute-start | bytes 1572872 | tf_op jit(solution)/shard_map/ppermute | solution.py:409
  52.6 10.1 %collective-permute-start.12 = (f32[128,1024]{1,0:T(8,128)S(1)}, f32[128,1024]{1,0:T(8,128)S(1)}, u32[]{:S(2)}, u32[]{:S(2)}) collective-permute-start(f32[128,1024]{1,0:T(8,128)S(1)} %shard_map.55), channel_id=1, source_target_pairs={{24,8},{25,9},{26,10},{27,11},{28,12},{29,13},{30,14},{31,15}} | collective-permute-start | bytes 1572872 | tf_op jit(solution)/shard_map/ppermute | solution.py:409
  54.1 11.2 %collective-permute-start.5 = (f32[256,512]{1,0:T(8,128)S(1)}, f32[256,512]{1,0:T(8,128)S(1)}, u32[]{:S(2)}, u32[]{:S(2)}) collective-permute-start(f32[256,512]{1,0:T(8,128)S(1)} %shard_map.52.refs_1_.refs_3_.refs_7_.refs_13_.refs_32_), channel_id=1, source_target_pairs={{8,0},{9,1},{10,2},{11,3},{12,4},{13,5},{14,6},{15,7}} | collective-permute-start | bytes 1572872 | tf_op jit(solution)/shard_map/ppermute | solution.py:409
  55.0 26.9 %collective-permute-start.14 = (f32[256,512]{1,0:T(8,128)S(1)}, f32[256,512]{1,0:T(8,128)S(1)}, u32[]{:S(2)}, u32[]{:S(2)}) collective-permute-start(f32[256,512]{1,0:T(8,128)S(1)} %shard_map.54.refs_4_.refs_8_.refs_14_), channel_id=1, source_target_pairs={{0,8},{8,16},{16,24},{1,9},{9,17},{17,25},{2,10},{10,18},{18,26},{... | collective-permute-start | bytes 1572872 | tf_op jit(solution)/shard_map/ppermute | solution.py:409
  61.3 21.3 %collective-permute-start.9 = (f32[256,512]{1,0:T(8,128)S(1)}, f32[256,512]{1,0:T(8,128)}, u32[]{:S(2)}, u32[]{:S(2)}) collective-permute-start(f32[256,512]{1,0:T(8,128)S(1)} %shard_map.54.refs_4_.refs_8_.refs_14_), channel_id=1, source_target_pairs={{8,0},{9,1},{10,2},{11,3},{12,4},{13,5},{14,6},{15,7}} | collective-permute-start | bytes 1572872 | tf_op jit(solution)/shard_map/ppermute | solution.py:409
  65.5 19.0 %collective-permute-start.13 = (f32[256,512]{1,0:T(8,128)S(1)}, f32[256,512]{1,0:T(8,128)}, u32[]{:S(2)}, u32[]{:S(2)}) collective-permute-start(f32[256,512]{1,0:T(8,128)S(1)} %shard_map.56.refs_5_.refs_6_.refs_9_.refs_15_), channel_id=1, source_target_pairs={{8,0},{9,1},{10,2},{11,3},{12,4},{13,5},{14,6},{15,7}} | collective-permute-start | bytes 1572872 | tf_op jit(solution)/shard_map/ppermute | solution.py:409
  67.0 20.2 %collective-permute-start.15 = (f32[256,512]{1,0:T(8,128)S(1)}, f32[256,512]{1,0:T(8,128)S(1)}, u32[]{:S(2)}, u32[]{:S(2)}) collective-permute-start(f32[256,512]{1,0:T(8,128)S(1)} %shard_map.56.refs_5_.refs_6_.refs_9_.refs_15_), channel_id=1, source_target_pairs={{8,16},{16,24},{9,17},{17,25},{10,18},{18,26},{11,19},{19,27},{12,... | collective-permute-start | bytes 1572872 | tf_op jit(solution)/shard_map/ppermute | solution.py:409
  73.1 19.0 %collective-permute-start.22 = (f32[128,768]{1,0:T(8,128)S(1)}, f32[128,768]{1,0:T(8,128)}, u32[]{:S(2)}, u32[]{:S(2)}) collective-permute-start(f32[128,768]{1,0:T(8,128)S(1)} %collective-permute-done.8.refs_8_.refs_0_), channel_id=1, source_target_pairs={{0,1},{1,0},{2,3},{3,2},{4,5},{5,4},{6,7},{7,6},{8,9},{9,8},{10,11... | collective-permute-start | bytes 1179656 | tf_op jit(solution)/shard_map/ppermute | solution.py:412
  81.9 23.2 %collective-permute-start.18 = (f32[128,1024]{1,0:T(8,128)S(1)}, f32[128,1024]{1,0:T(8,128)S(1)}, u32[]{:S(2)}, u32[]{:S(2)}) collective-permute-start(f32[128,1024]{1,0:T(8,128)S(1)} %copy-done.21), channel_id=1, source_target_pairs={{0,1},{1,0},{2,3},{3,2},{4,5},{5,4},{6,7},{7,6},{8,9},{9,8},{10,11... | collective-permute-start | bytes 1572872 | tf_op jit(solution)/shard_map/ppermute | solution.py:412
  82.6 67.3 %copy-start.15 = (f32[256,512]{1,0:T(8,128)}, f32[256,512]{1,0:T(8,128)S(1)}, u32[]{:S(2)}) copy-start(f32[256,512]{1,0:T(8,128)S(1)} %shard_map.58.refs_16_) | copy-start | bytes 1572868
  82.6 19.2 %collective-permute-start.16 = (f32[256,512]{1,0:T(8,128)S(1)}, f32[256,512]{1,0:T(8,128)S(1)}, u32[]{:S(2)}, u32[]{:S(2)}) collective-permute-start(f32[256,512]{1,0:T(8,128)S(1)} %shard_map.58.refs_16_), channel_id=1, source_target_pairs={{8,16},{16,24},{9,17},{17,25},{10,18},{18,26},{11,19},{19,27},{12,... | collective-permute-start | bytes 1572872 | tf_op jit(solution)/shard_map/ppermute | solution.py:409
  84.5 17.3 %collective-permute-start.21 = (f32[256,512]{1,0:T(8,128)S(1)}, f32[256,512]{1,0:T(8,128)S(1)}, u32[]{:S(2)}, u32[]{:S(2)}) collective-permute-start(f32[256,512]{1,0:T(8,128)S(1)} %shard_map.58.refs_16_), channel_id=1, source_target_pairs={{8,0},{9,1},{10,2},{11,3},{12,4},{13,5},{14,6},{15,7}} | collective-permute-start | bytes 1572872 | tf_op jit(solution)/shard_map/ppermute | solution.py:409
  90.2 23.9 %collective-permute-start.17 = (f32[256,512]{1,0:T(8,128)S(1)}, f32[256,512]{1,0:T(8,128)S(1)}, u32[]{:S(2)}, u32[]{:S(2)}) collective-permute-start(f32[256,512]{1,0:T(8,128)S(1)} %shard_map.59.refs_17_.refs_33_), channel_id=1, source_target_pairs={{8,16},{16,24},{9,17},{17,25},{10,18},{18,26},{11,19},{19,27},{12,... | collective-permute-start | bytes 1572872 | tf_op jit(solution)/shard_map/ppermute | solution.py:409
  92.1 22.0 %collective-permute-start.19 = (f32[256,512]{1,0:T(8,128)S(1)}, f32[256,512]{1,0:T(8,128)S(1)}, u32[]{:S(2)}, u32[]{:S(2)}) collective-permute-start(f32[256,512]{1,0:T(8,128)S(1)} %shard_map.59.refs_17_.refs_33_), channel_id=1, source_target_pairs={{8,0},{9,1},{10,2},{11,3},{12,4},{13,5},{14,6},{15,7}} | collective-permute-start | bytes 1572872 | tf_op jit(solution)/shard_map/ppermute | solution.py:409
  103.2 46.7 %copy-start.17 = (f32[256,512]{1,0:T(8,128)}, f32[256,512]{1,0:T(8,128)S(1)}, u32[]{:S(2)}) copy-start(f32[256,512]{1,0:T(8,128)S(1)} %shard_map.62.refs_18_) | copy-start | bytes 1572868
  103.2 22.1 %collective-permute-start.25 = (f32[256,512]{1,0:T(8,128)S(1)}, f32[256,512]{1,0:T(8,128)S(1)}, u32[]{:S(2)}, u32[]{:S(2)}) collective-permute-start(f32[256,512]{1,0:T(8,128)S(1)} %shard_map.62.refs_18_), channel_id=1, source_target_pairs={{8,16},{16,24},{9,17},{17,25},{10,18},{18,26},{11,19},{19,27},{12,... | collective-permute-start | bytes 1572872 | tf_op jit(solution)/shard_map/ppermute | solution.py:409
  114.2 20.8 %collective-permute-start.20 = (f32[256,512]{1,0:T(8,128)S(1)}, f32[256,512]{1,0:T(8,128)S(1)}, u32[]{:S(2)}, u32[]{:S(2)}) collective-permute-start(f32[256,512]{1,0:T(8,128)S(1)} %shard_map.60.refs_19_), channel_id=1, source_target_pairs={{8,16},{16,24},{9,17},{17,25},{10,18},{18,26},{11,19},{19,27},{12,... | collective-permute-start | bytes 1572872 | tf_op jit(solution)/shard_map/ppermute | solution.py:409
  116.1 33.8 %collective-permute-start.23 = (f32[256,512]{1,0:T(8,128)S(1)}, f32[256,512]{1,0:T(8,128)S(1)}, u32[]{:S(2)}, u32[]{:S(2)}) collective-permute-start(f32[256,512]{1,0:T(8,128)S(1)} %shard_map.62.refs_18_), channel_id=1, source_target_pairs={{8,0},{9,1},{10,2},{11,3},{12,4},{13,5},{14,6},{15,7}} | collective-permute-start | bytes 1572872 | tf_op jit(solution)/shard_map/ppermute | solution.py:409
  116.8 33.1 %collective-permute-start.24 = (f32[256,512]{1,0:T(8,128)S(1)}, f32[256,512]{1,0:T(8,128)S(1)}, u32[]{:S(2)}, u32[]{:S(2)}) collective-permute-start(f32[256,512]{1,0:T(8,128)S(1)} %shard_map.60.refs_19_), channel_id=1, source_target_pairs={{8,0},{9,1},{10,2},{11,3},{12,4},{13,5},{14,6},{15,7}} | collective-permute-start | bytes 1572872 | tf_op jit(solution)/shard_map/ppermute | solution.py:409
  125.3 24.6 %collective-permute-start.26 = (f32[256,512]{1,0:T(8,128)S(1)}, f32[256,512]{1,0:T(8,128)S(1)}, u32[]{:S(2)}, u32[]{:S(2)}) collective-permute-start(f32[256,512]{1,0:T(8,128)S(1)} %collective-permute-done.25.refs_26_.refs_35_), channel_id=1, source_target_pairs={{16,24},{17,25},{18,26},{19,27},{20,28},{21,29},{22,30},{23,31}} | collective-permute-start | bytes 1572872 | tf_op jit(solution)/shard_map/ppermute | solution.py:409
  135.0 17.3 %collective-permute-start.27 = (f32[256,512]{1,0:T(8,128)S(1)}, f32[256,512]{1,0:T(8,128)S(1)}, u32[]{:S(2)}, u32[]{:S(2)}) collective-permute-start(f32[256,512]{1,0:T(8,128)S(1)} %collective-permute-done.20.refs_16_.refs_27_), channel_id=1, source_target_pairs={{16,24},{17,25},{18,26},{19,27},{20,28},{21,29},{22,30},{23,31}} | collective-permute-start | bytes 1572872 | tf_op jit(solution)/shard_map/ppermute | solution.py:409
  (25 other events, 320.3 us)
Sparse Core Ops, SparseCore 0:
  10.8 55.4 all-gather.4
  68.7 89.8 all-gather.6

commit v6 on v5

--- a/solution.py
+++ b/solution.py
@@ -300,10 +300,12 @@
         def _():
             fetch(where, chunk_refs, whole, sems, height, my_row, late, chunks, True, False)
             fetch(where, chunk_refs, whole, sems, height, my_row, 0, late, True, False)
-            fetch(where, chunk_refs, whole, sems, height, my_row, late, chunks, False, True)
-            hi, lo = split(whole[late * height:])
-            x_hi[late * height:] = hi
-            x_lo[late * height:] = lo
+            for n in range(late, chunks):
+                fetch(where, chunk_refs, whole, sems, height, my_row, n, n + 1, False, True)
+                rows_n = slice(n * height, (n + 1) * height)
+                hi, lo = split(whole[rows_n])
+                x_hi[rows_n] = hi
+                x_lo[rows_n] = lo
             if last:
                 give(True)
 

time: 189 us -> 189 us (level)
  no operation moved by 1% of the time
where the time goes in v6:
time: 189 us; the launch traced here: 188 us
  waiting for transfers between devices  71.9 us (38%)
  Pallas kernels  50 us (26%)
  starting transfers between devices  43.5 us (23%)
  between operations  14.7 us (8%)
  local copies, waits for them, and re-layouts  7.65 us (4%)
    ppermute x24, waiting for transfers between devices, send(): return lax.ppermute(value, 'row', pairs)  65.4 us
    pallas_call x3, Pallas kernels, update(): pl.pallas_call(kernel, grid_spec=pltpu.PrefetchScalarGridSpec(num_scalar_...  43.6 us
    ppermute x24, starting transfers between devices, send(): return lax.ppermute(value, 'row', pairs)  42.4 us
    all_gather x1, waiting for transfers between devices, body(): lax.all_gather(turned[2:], 'col')  6.47 us
    pallas_call x8, Pallas kernels, slot(): pl.pallas_call(kernel, grid=(1,), in_specs=specs + [ANY] * (1 + len(rhs)...  3.99 us
  transfers between devices with their start and end apart: 30, of which 11 were waited for; matrix products, arithmetic and copies ran while one was open for 1% of the time, Pallas kernels for 15%

profile of v6, /device:TPU:18, one launch (start us, length us, event | category | flops | bytes accessed | tf_op | source)
XLA Modules:
  0.0 187.9 jit_solution(12311711335327808713)
XLA Ops:
  7.2 2.4 %copy.7 = f32[2,3,1024,128]{3,2,1,0:T(8,128)S(1)} copy(f32[2,3,1024,128]{2,3,1,0:T(8,128)} %bitcast.11) | data formatting | bytes 6291456 | tf_op jit(solution)/shard_map/transpose | solution.py:457
  10.7 1.5 slice.9
  12.2 1.2 shard_map.50
  14.8 2.6 %collective-permute-start.1 = (f32[128,768]{1,0:T(8,128)S(1)}, f32[128,768]{1,0:T(8,128)S(1)}, u32[]{:S(2)}, u32[]{:S(2)}) collective-permute-start(f32[128,768]{1,0:T(8,128)S(1)} %get-tuple-element.9), channel_id=1, source_target_pairs={{16,8},{17,9},{18,10},{19,11},{20,12},{21,13},{22,14},{23,15}} | collective-permute-start | bytes 1179656 | tf_op jit(solution)/shard_map/ppermute | solution.py:411
  18.0 18.5 %collective-permute-done.1.refs_4_.refs_0_ = f32[128,768]{1,0:T(8,128)S(1)} collective-permute-done((f32[128,768]{1,0:T(8,128)S(1)}, f32[128,768]{1,0:T(8,128)S(1)}, u32[]{:S(2)}, u32[]{:S(2)}) %collective-permute-start.1) | collective-permute-done | bytes 393248 | tf_op jit(solution)/shard_map/ppermute | solution.py:411
  36.6 1.3 collective-permute-start.7
  38.0 1.1 shard_map.53
  39.1 4.5 %collective-permute-start.8 = (f32[128,768]{1,0:T(8,128)S(1)}, f32[128,768]{1,0:T(8,128)S(1)}, u32[]{:S(2)}, u32[]{:S(2)}) collective-permute-start(f32[128,768]{1,0:T(8,128)S(1)} %shard_map.53), channel_id=1, source_target_pairs={{16,8},{17,9},{18,10},{19,11},{20,12},{21,13},{22,14},{23,15}} | collective-permute-start | bytes 1179656 | tf_op jit(solution)/shard_map/ppermute | solution.py:411
  45.9 1.3 collective-permute-start.11
  47.2 5.4 %collective-permute-done.8.refs_8_.refs_0_ = f32[128,768]{1,0:T(8,128)S(1)} collective-permute-done((f32[128,768]{1,0:T(8,128)S(1)}, f32[128,768]{1,0:T(8,128)S(1)}, u32[]{:S(2)}, u32[]{:S(2)}) %collective-permute-start.8) | collective-permute-done | bytes 393248 | tf_op jit(solution)/shard_map/ppermute | solution.py:411
  55.0 6.3 %collective-permute-start.14 = (f32[256,512]{1,0:T(8,128)S(1)}, f32[256,512]{1,0:T(8,128)S(1)}, u32[]{:S(2)}, u32[]{:S(2)}) collective-permute-start(f32[256,512]{1,0:T(8,128)S(1)} %shard_map.54.refs_4_.refs_8_.refs_14_), channel_id=1, source_target_pairs={{0,8},{8,16},{16,24},{1,9},{9,17},{17,25},{2,10},{10,18},{18,26},{... | collective-permute-start | bytes 1572872 | tf_op jit(solution)/shard_map/ppermute | solution.py:411
  61.3 1.5 collective-permute-start.9
  62.7 2.6 %collective-permute-done.11.refs_2_.refs_6_.refs_11_.refs_21_ = f32[256,512]{1,0:T(8,128)S(1)} collective-permute-done((f32[256,512]{1,0:T(8,128)S(1)}, f32[256,512]{1,0:T(8,128)S(1)}, u32[]{:S(2)}, u32[]{:S(2)}) %collective-permute-start.11) | collective-permute-done | bytes 524320 | tf_op jit(solution)/shard_map/ppermute | solution.py:411
  65.5 1.5 collective-permute-start.13
  67.0 6.1 %collective-permute-start.15 = (f32[256,512]{1,0:T(8,128)S(1)}, f32[256,512]{1,0:T(8,128)S(1)}, u32[]{:S(2)}, u32[]{:S(2)}) collective-permute-start(f32[256,512]{1,0:T(8,128)S(1)} %shard_map.56.refs_5_.refs_6_.refs_9_.refs_15_), channel_id=1, source_target_pairs={{8,16},{16,24},{9,17},{17,25},{10,18},{18,26},{11,19},{19,27},{12,... | collective-permute-start | bytes 1572872 | tf_op jit(solution)/shard_map/ppermute | solution.py:411
  73.3 8.3 %shard_map.57.refs_2_.refs_4_.refs_3_ = f32[1,1024,512]{2,1,0:T(8,128)S(1)} custom-call(s32[1]{0:T(128)} %bitcast.col_ref, f32[3,1024,512]{2,1,0:T(8,128)} %refs_1_.3, f32[8,2,1024,128]{3,2,1,0:T(8,128)} %bitcast.7, f32[256,512]{1,0:T(8,128)} %copy-done.2, f32[256,512]{1,0:T(8,128)} %copy-done, f32[256,512]{1,0:T(8,128)} %copy-done.7, f32[256,512]{1,0:T(8,128)} %copy-done.4, ...), custom_call_target="tpu_custom_call" | custom-call | flops 1024 | bytes 1024 | tf_op jit(solution)/shard_map/pallas_call | solution.py:378
  82.4 1.9 %collective-permute-start.16 = (f32[256,512]{1,0:T(8,128)S(1)}, f32[256,512]{1,0:T(8,128)S(1)}, u32[]{:S(2)}, u32[]{:S(2)}) collective-permute-start(f32[256,512]{1,0:T(8,128)S(1)} %shard_map.58.refs_16_), channel_id=1, source_target_pairs={{8,16},{16,24},{9,17},{17,25},{10,18},{18,26},{11,19},{19,27},{12,... | collective-permute-start | bytes 1572872 | tf_op jit(solution)/shard_map/ppermute | solution.py:411
  85.0 2.2 %collective-permute-done.15.refs_1_.refs_13_.refs_23_ = f32[256,512]{1,0:T(8,128)S(1)} collective-permute-done((f32[256,512]{1,0:T(8,128)S(1)}, f32[256,512]{1,0:T(8,128)S(1)}, u32[]{:S(2)}, u32[]{:S(2)}) %collective-permute-start.15) | collective-permute-done | bytes 524320 | tf_op jit(solution)/shard_map/ppermute | solution.py:411
  90.2 1.9 %collective-permute-start.17 = (f32[256,512]{1,0:T(8,128)S(1)}, f32[256,512]{1,0:T(8,128)S(1)}, u32[]{:S(2)}, u32[]{:S(2)}) collective-permute-start(f32[256,512]{1,0:T(8,128)S(1)} %shard_map.59.refs_17_.refs_33_), channel_id=1, source_target_pairs={{8,16},{16,24},{9,17},{17,25},{10,18},{18,26},{11,19},{19,27},{12,... | collective-permute-start | bytes 1572872 | tf_op jit(solution)/shard_map/ppermute | solution.py:411
  92.8 8.7 %collective-permute-done.16.refs_14_.refs_2_.refs_24_ = f32[256,512]{1,0:T(8,128)S(1)} collective-permute-done((f32[256,512]{1,0:T(8,128)S(1)}, f32[256,512]{1,0:T(8,128)S(1)}, u32[]{:S(2)}, u32[]{:S(2)}) %collective-permute-start.16) | collective-permute-done | bytes 524320 | tf_op jit(solution)/shard_map/ppermute | solution.py:411
  101.6 1.3 shard_map.62.refs_18_
  102.9 1.9 %collective-permute-start.25 = (f32[256,512]{1,0:T(8,128)S(1)}, f32[256,512]{1,0:T(8,128)S(1)}, u32[]{:S(2)}, u32[]{:S(2)}) collective-permute-start(f32[256,512]{1,0:T(8,128)S(1)} %shard_map.62.refs_18_), channel_id=1, source_target_pairs={{8,16},{16,24},{9,17},{17,25},{10,18},{18,26},{11,19},{19,27},{12,... | collective-permute-start | bytes 1572872 | tf_op jit(solution)/shard_map/ppermute | solution.py:411
  104.9 9.2 %collective-permute-done.17.refs_2_.refs_15_.refs_25_.refs_36_ = f32[256,512]{1,0:T(8,128)S(1)} collective-permute-done((f32[256,512]{1,0:T(8,128)S(1)}, f32[256,512]{1,0:T(8,128)S(1)}, u32[]{:S(2)}, u32[]{:S(2)}) %collective-permute-start.17) | collective-permute-done | bytes 524320 | tf_op jit(solution)/shard_map/ppermute | solution.py:411
  114.2 1.9 %collective-permute-start.20 = (f32[256,512]{1,0:T(8,128)S(1)}, f32[256,512]{1,0:T(8,128)S(1)}, u32[]{:S(2)}, u32[]{:S(2)}) collective-permute-start(f32[256,512]{1,0:T(8,128)S(1)} %shard_map.60.refs_19_), channel_id=1, source_target_pairs={{8,16},{16,24},{9,17},{17,25},{10,18},{18,26},{11,19},{19,27},{12,... | collective-permute-start | bytes 1572872 | tf_op jit(solution)/shard_map/ppermute | solution.py:411
  117.5 7.8 %collective-permute-done.25.refs_26_.refs_35_ = f32[256,512]{1,0:T(8,128)S(1)} collective-permute-done((f32[256,512]{1,0:T(8,128)S(1)}, f32[256,512]{1,0:T(8,128)S(1)}, u32[]{:S(2)}, u32[]{:S(2)}) %collective-permute-start.25) | collective-permute-done | bytes 524320 | tf_op jit(solution)/shard_map/ppermute | solution.py:411
  125.3 1.3 collective-permute-start.26
  126.6 8.2 %collective-permute-done.20.refs_16_.refs_27_ = f32[256,512]{1,0:T(8,128)S(1)} collective-permute-done((f32[256,512]{1,0:T(8,128)S(1)}, f32[256,512]{1,0:T(8,128)S(1)}, u32[]{:S(2)}, u32[]{:S(2)}) %collective-permute-start.20) | collective-permute-done | bytes 524320 | tf_op jit(solution)/shard_map/ppermute | solution.py:411
  134.8 1.5 collective-permute-start.27
  136.3 12.9 %shard_map.61.refs_0_ = f32[2,1024,512]{2,1,0:T(8,128)} custom-call(s32[1]{0:T(128)} %bitcast.col_ref, f32[3,1024,512]{2,1,0:T(8,128)} %refs_1_.3, f32[8,2,1024,128]{3,2,1,0:T(8,128)} %bitcast.8, f32[256,512]{1,0:T(8,128)} %copy-done.5, f32[256,512]{1,0:T(8,128)} %copy-done.12, f32[256,512]{1,0:T(8,128)} %collective-permute-done.9.refs_3_.refs_4_.refs_6_, ...), custom_call_target="tpu_custom_call" | custom-call | flops 1024 | bytes 1024 | tf_op jit(solution)/shard_map/pallas_call | solution.py:378
  150.2 2.0 %collective-permute-done.27.refs_29_.refs_37_ = f32[256,512]{1,0:T(8,128)S(1)} collective-permute-done((f32[256,512]{1,0:T(8,128)S(1)}, f32[256,512]{1,0:T(8,128)S(1)}, u32[]{:S(2)}, u32[]{:S(2)}) %collective-permute-start.27) | collective-permute-done | bytes 524320 | tf_op jit(solution)/shard_map/ppermute | solution.py:411
  152.1 6.5 %all-gather.7.cloned.1.call-done = f32[32,1024,128]{2,1,0:T(8,128)} async-done(((f32[4,1024,128]{2,1,0:T(8,128)}), f32[32,1024,128]{2,1,0:T(8,128)}) %all-gather.7.cloned.1.call-update) | async-done | bytes 16777232 | tf_op jit(solution)/shard_map/all_gather | solution.py:458
  158.6 22.4 %shard_map.63 = (f32[3,1024,512]{2,1,0:T(8,128)}, f32[2,256,512]{2,1,0:T(8,128)}) custom-call(s32[1]{0:T(128)} %bitcast.col_ref, f32[2,1024,512]{2,1,0:T(8,128)} %shard_map.61.refs_0_, f32[3,1024,512]{2,1,0:T(8,128)} %refs_1_.3, f32[8,4,1024,128]{3,2,1,0:T(8,128)} %bitcast.5, f32[8,4,1024,128]{3,2,1,0:T(8,128)} %bitcast.6, f32[256,512]{1,0:T(8,128)} %copy-done.5, ...), custom_call_target="tpu_custom_call" | custom-call | flops 1024 | bytes 1024 | tf_op jit(solution)/shard_map/pallas_call | solution.py:378
  (101 shorter events, 15.7 us)
Async XLA Ops:
  7.2 66.1 %all-gather.5.cloned.1.call-start = ((), (), s32[]{:S(2)}) async-start(), calls=%async_computation | async-start | bytes 9437184 | tf_op jit(solution)/shard_map/all_gather | solution.py:458
  10.6 147.9 %all-gather.7.cloned.1.call-start = ((), (), s32[]{:S(2)}) async-start(), calls=%async_computation.1 | async-start | bytes 18874368 | tf_op jit(solution)/shard_map/all_gather | solution.py:458
  13.3 23.2 %collective-permute-start = (f32[384,512]{1,0:T(8,128)S(1)}, f32[384,512]{1,0:T(8,128)S(1)}, u32[]{:S(2)}, u32[]{:S(2)}) collective-permute-start(f32[384,512]{1,0:T(8,128)S(1)} %get-tuple-element.8), channel_id=1, source_target_pairs={{0,8},{1,9},{2,10},{3,11},{4,12},{5,13},{6,14},{7,15}} | collective-permute-start | bytes 2359304 | tf_op jit(solution)/shard_map/ppermute | solution.py:411
  14.1 22.4 %collective-permute-start.2 = (f32[128,1024]{1,0:T(8,128)S(1)}, f32[128,1024]{1,0:T(8,128)S(1)}, u32[]{:S(2)}, u32[]{:S(2)}) collective-permute-start(f32[128,1024]{1,0:T(8,128)S(1)} %get-tuple-element.10), channel_id=1, source_target_pairs={{24,8},{25,9},{26,10},{27,11},{28,12},{29,13},{30,14},{31,15}} | collective-permute-start | bytes 1572872 | tf_op jit(solution)/shard_map/ppermute | solution.py:411
  14.8 21.7 %collective-permute-start.1 = (f32[128,768]{1,0:T(8,128)S(1)}, f32[128,768]{1,0:T(8,128)S(1)}, u32[]{:S(2)}, u32[]{:S(2)}) collective-permute-start(f32[128,768]{1,0:T(8,128)S(1)} %get-tuple-element.9), channel_id=1, source_target_pairs={{16,8},{17,9},{18,10},{19,11},{20,12},{21,13},{22,14},{23,15}} | collective-permute-start | bytes 1179656 | tf_op jit(solution)/shard_map/ppermute | solution.py:411
  17.3 27.0 %collective-permute-start.4 = (f32[256,512]{1,0:T(8,128)S(1)}, f32[256,512]{1,0:T(8,128)S(1)}, u32[]{:S(2)}, u32[]{:S(2)}) collective-permute-start(f32[256,512]{1,0:T(8,128)S(1)} %get-tuple-element.11), channel_id=1, source_target_pairs={{0,8},{1,9},{2,10},{3,11},{4,12},{5,13},{6,14},{7,15}} | collective-permute-start | bytes 1572872 | tf_op jit(solution)/shard_map/ppermute | solution.py:411
  36.6 17.5 %collective-permute-start.7 = (f32[256,512]{1,0:T(8,128)S(1)}, f32[256,512]{1,0:T(8,128)S(1)}, u32[]{:S(2)}, u32[]{:S(2)}) collective-permute-start(f32[256,512]{1,0:T(8,128)S(1)} %shard_map.51.refs_1_.refs_2_.refs_6_.refs_12_), channel_id=1, source_target_pairs={{0,8},{8,16},{1,9},{9,17},{2,10},{10,18},{3,11},{11,19},{4,12},{12... | collective-permute-start | bytes 1572872 | tf_op jit(solution)/shard_map/ppermute | solution.py:411
  37.9 8.0 %collective-permute-start.6 = (f32[128,768]{1,0:T(8,128)S(1)}, f32[128,768]{1,0:T(8,128)S(1)}, u32[]{:S(2)}, u32[]{:S(2)}) collective-permute-start(f32[128,768]{1,0:T(8,128)S(1)} %collective-permute-done.1.refs_4_.refs_0_), channel_id=1, source_target_pairs={{0,1},{1,0},{2,3},{3,2},{4,5},{5,4},{6,7},{7,6},{8,9},{9,8},{10,11... | collective-permute-start | bytes 1179656 | tf_op jit(solution)/shard_map/ppermute | solution.py:414
  39.1 13.4 %collective-permute-start.8 = (f32[128,768]{1,0:T(8,128)S(1)}, f32[128,768]{1,0:T(8,128)S(1)}, u32[]{:S(2)}, u32[]{:S(2)}) collective-permute-start(f32[128,768]{1,0:T(8,128)S(1)} %shard_map.53), channel_id=1, source_target_pairs={{16,8},{17,9},{18,10},{19,11},{20,12},{21,13},{22,14},{23,15}} | collective-permute-start | bytes 1179656 | tf_op jit(solution)/shard_map/ppermute | solution.py:411
  43.6 11.2 %collective-permute-start.3 = (f32[256,512]{1,0:T(8,128)S(1)}, f32[256,512]{1,0:T(8,128)S(1)}, u32[]{:S(2)}, u32[]{:S(2)}) collective-permute-start(f32[256,512]{1,0:T(8,128)S(1)} %shard_map.51.refs_1_.refs_2_.refs_6_.refs_12_), channel_id=1, source_target_pairs={{8,0},{9,1},{10,2},{11,3},{12,4},{13,5},{14,6},{15,7}} | collective-permute-start | bytes 1572872 | tf_op jit(solution)/shard_map/ppermute | solution.py:411
  45.5 15.8 %collective-permute-start.10 = (f32[128,1024]{1,0:T(8,128)S(1)}, f32[128,1024]{1,0:T(8,128)S(1)}, u32[]{:S(2)}, u32[]{:S(2)}) collective-permute-start(f32[128,1024]{1,0:T(8,128)S(1)} %collective-permute-done.2.refs_5_.refs_0_), channel_id=1, source_target_pairs={{0,1},{1,0},{2,3},{3,2},{4,5},{5,4},{6,7},{7,6},{8,9},{9,8},{10,11... | collective-permute-start | bytes 1572872 | tf_op jit(solution)/shard_map/ppermute | solution.py:414
  45.9 19.5 %collective-permute-start.11 = (f32[256,512]{1,0:T(8,128)S(1)}, f32[256,512]{1,0:T(8,128)S(1)}, u32[]{:S(2)}, u32[]{:S(2)}) collective-permute-start(f32[256,512]{1,0:T(8,128)S(1)} %shard_map.52.refs_1_.refs_3_.refs_7_.refs_13_.refs_32_), channel_id=1, source_target_pairs={{0,8},{8,16},{1,9},{9,17},{2,10},{10,18},{3,11},{11,19},{4,12},{12... | collective-permute-start | bytes 1572872 | tf_op jit(solution)/shard_map/ppermute | solution.py:411
  52.6 10.1 %collective-permute-start.12 = (f32[128,1024]{1,0:T(8,128)S(1)}, f32[128,1024]{1,0:T(8,128)S(1)}, u32[]{:S(2)}, u32[]{:S(2)}) collective-permute-start(f32[128,1024]{1,0:T(8,128)S(1)} %shard_map.55), channel_id=1, source_target_pairs={{24,8},{25,9},{26,10},{27,11},{28,12},{29,13},{30,14},{31,15}} | collective-permute-start | bytes 1572872 | tf_op jit(solution)/shard_map/ppermute | solution.py:411
  54.1 11.2 %collective-permute-start.5 = (f32[256,512]{1,0:T(8,128)S(1)}, f32[256,512]{1,0:T(8,128)S(1)}, u32[]{:S(2)}, u32[]{:S(2)}) collective-permute-start(f32[256,512]{1,0:T(8,128)S(1)} %shard_map.52.refs_1_.refs_3_.refs_7_.refs_13_.refs_32_), channel_id=1, source_target_pairs={{8,0},{9,1},{10,2},{11,3},{12,4},{13,5},{14,6},{15,7}} | collective-permute-start | bytes 1572872 | tf_op jit(solution)/shard_map/ppermute | solution.py:411
  55.0 26.6 %collective-permute-start.14 = (f32[256,512]{1,0:T(8,128)S(1)}, f32[256,512]{1,0:T(8,128)S(1)}, u32[]{:S(2)}, u32[]{:S(2)}) collective-permute-start(f32[256,512]{1,0:T(8,128)S(1)} %shard_map.54.refs_4_.refs_8_.refs_14_), channel_id=1, source_target_pairs={{0,8},{8,16},{16,24},{1,9},{9,17},{17,25},{2,10},{10,18},{18,26},{... | collective-permute-start | bytes 1572872 | tf_op jit(solution)/shard_map/ppermute | solution.py:411
  61.3 21.0 %collective-permute-start.9 = (f32[256,512]{1,0:T(8,128)S(1)}, f32[256,512]{1,0:T(8,128)}, u32[]{:S(2)}, u32[]{:S(2)}) collective-permute-start(f32[256,512]{1,0:T(8,128)S(1)} %shard_map.54.refs_4_.refs_8_.refs_14_), channel_id=1, source_target_pairs={{8,0},{9,1},{10,2},{11,3},{12,4},{13,5},{14,6},{15,7}} | collective-permute-start | bytes 1572872 | tf_op jit(solution)/shard_map/ppermute | solution.py:411
  65.5 18.8 %collective-permute-start.13 = (f32[256,512]{1,0:T(8,128)S(1)}, f32[256,512]{1,0:T(8,128)}, u32[]{:S(2)}, u32[]{:S(2)}) collective-permute-start(f32[256,512]{1,0:T(8,128)S(1)} %shard_map.56.refs_5_.refs_6_.refs_9_.refs_15_), channel_id=1, source_target_pairs={{8,0},{9,1},{10,2},{11,3},{12,4},{13,5},{14,6},{15,7}} | collective-permute-start | bytes 1572872 | tf_op jit(solution)/shard_map/ppermute | solution.py:411
  67.0 20.2 %collective-permute-start.15 = (f32[256,512]{1,0:T(8,128)S(1)}, f32[256,512]{1,0:T(8,128)S(1)}, u32[]{:S(2)}, u32[]{:S(2)}) collective-permute-start(f32[256,512]{1,0:T(8,128)S(1)} %shard_map.56.refs_5_.refs_6_.refs_9_.refs_15_), channel_id=1, source_target_pairs={{8,16},{16,24},{9,17},{17,25},{10,18},{18,26},{11,19},{19,27},{12,... | collective-permute-start | bytes 1572872 | tf_op jit(solution)/shard_map/ppermute | solution.py:411
  73.1 19.0 %collective-permute-start.22 = (f32[128,768]{1,0:T(8,128)S(1)}, f32[128,768]{1,0:T(8,128)}, u32[]{:S(2)}, u32[]{:S(2)}) collective-permute-start(f32[128,768]{1,0:T(8,128)S(1)} %collective-permute-done.8.refs_8_.refs_0_), channel_id=1, source_target_pairs={{0,1},{1,0},{2,3},{3,2},{4,5},{5,4},{6,7},{7,6},{8,9},{9,8},{10,11... | collective-permute-start | bytes 1179656 | tf_op jit(solution)/shard_map/ppermute | solution.py:414
  81.6 23.2 %collective-permute-start.18 = (f32[128,1024]{1,0:T(8,128)S(1)}, f32[128,1024]{1,0:T(8,128)S(1)}, u32[]{:S(2)}, u32[]{:S(2)}) collective-permute-start(f32[128,1024]{1,0:T(8,128)S(1)} %copy-done.21), channel_id=1, source_target_pairs={{0,1},{1,0},{2,3},{3,2},{4,5},{5,4},{6,7},{7,6},{8,9},{9,8},{10,11... | collective-permute-start | bytes 1572872 | tf_op jit(solution)/shard_map/ppermute | solution.py:414
  82.4 66.8 %copy-start.15 = (f32[256,512]{1,0:T(8,128)}, f32[256,512]{1,0:T(8,128)S(1)}, u32[]{:S(2)}) copy-start(f32[256,512]{1,0:T(8,128)S(1)} %shard_map.58.refs_16_) | copy-start | bytes 1572868
  82.4 19.2 %collective-permute-start.16 = (f32[256,512]{1,0:T(8,128)S(1)}, f32[256,512]{1,0:T(8,128)S(1)}, u32[]{:S(2)}, u32[]{:S(2)}) collective-permute-start(f32[256,512]{1,0:T(8,128)S(1)} %shard_map.58.refs_16_), channel_id=1, source_target_pairs={{8,16},{16,24},{9,17},{17,25},{10,18},{18,26},{11,19},{19,27},{12,... | collective-permute-start | bytes 1572872 | tf_op jit(solution)/shard_map/ppermute | solution.py:411
  84.3 17.3 %collective-permute-start.21 = (f32[256,512]{1,0:T(8,128)S(1)}, f32[256,512]{1,0:T(8,128)S(1)}, u32[]{:S(2)}, u32[]{:S(2)}) collective-permute-start(f32[256,512]{1,0:T(8,128)S(1)} %shard_map.58.refs_16_), channel_id=1, source_target_pairs={{8,0},{9,1},{10,2},{11,3},{12,4},{13,5},{14,6},{15,7}} | collective-permute-start | bytes 1572872 | tf_op jit(solution)/shard_map/ppermute | solution.py:411
  90.2 23.9 %collective-permute-start.17 = (f32[256,512]{1,0:T(8,128)S(1)}, f32[256,512]{1,0:T(8,128)S(1)}, u32[]{:S(2)}, u32[]{:S(2)}) collective-permute-start(f32[256,512]{1,0:T(8,128)S(1)} %shard_map.59.refs_17_.refs_33_), channel_id=1, source_target_pairs={{8,16},{16,24},{9,17},{17,25},{10,18},{18,26},{11,19},{19,27},{12,... | collective-permute-start | bytes 1572872 | tf_op jit(solution)/shard_map/ppermute | solution.py:411
  92.1 22.0 %collective-permute-start.19 = (f32[256,512]{1,0:T(8,128)S(1)}, f32[256,512]{1,0:T(8,128)S(1)}, u32[]{:S(2)}, u32[]{:S(2)}) collective-permute-start(f32[256,512]{1,0:T(8,128)S(1)} %shard_map.59.refs_17_.refs_33_), channel_id=1, source_target_pairs={{8,0},{9,1},{10,2},{11,3},{12,4},{13,5},{14,6},{15,7}} | collective-permute-start | bytes 1572872 | tf_op jit(solution)/shard_map/ppermute | solution.py:411
  102.9 46.3 %copy-start.17 = (f32[256,512]{1,0:T(8,128)}, f32[256,512]{1,0:T(8,128)S(1)}, u32[]{:S(2)}) copy-start(f32[256,512]{1,0:T(8,128)S(1)} %shard_map.62.refs_18_) | copy-start | bytes 1572868
  102.9 22.4 %collective-permute-start.25 = (f32[256,512]{1,0:T(8,128)S(1)}, f32[256,512]{1,0:T(8,128)S(1)}, u32[]{:S(2)}, u32[]{:S(2)}) collective-permute-start(f32[256,512]{1,0:T(8,128)S(1)} %shard_map.62.refs_18_), channel_id=1, source_target_pairs={{8,16},{16,24},{9,17},{17,25},{10,18},{18,26},{11,19},{19,27},{12,... | collective-permute-start | bytes 1572872 | tf_op jit(solution)/shard_map/ppermute | solution.py:411
  114.2 20.6 %collective-permute-start.20 = (f32[256,512]{1,0:T(8,128)S(1)}, f32[256,512]{1,0:T(8,128)S(1)}, u32[]{:S(2)}, u32[]{:S(2)}) collective-permute-start(f32[256,512]{1,0:T(8,128)S(1)} %shard_map.60.refs_19_), channel_id=1, source_target_pairs={{8,16},{16,24},{9,17},{17,25},{10,18},{18,26},{11,19},{19,27},{12,... | collective-permute-start | bytes 1572872 | tf_op jit(solution)/shard_map/ppermute | solution.py:411
  116.1 33.1 %collective-permute-start.23 = (f32[256,512]{1,0:T(8,128)S(1)}, f32[256,512]{1,0:T(8,128)S(1)}, u32[]{:S(2)}, u32[]{:S(2)}) collective-permute-start(f32[256,512]{1,0:T(8,128)S(1)} %shard_map.62.refs_18_), channel_id=1, source_target_pairs={{8,0},{9,1},{10,2},{11,3},{12,4},{13,5},{14,6},{15,7}} | collective-permute-start | bytes 1572872 | tf_op jit(solution)/shard_map/ppermute | solution.py:411
  116.8 32.4 %collective-permute-start.24 = (f32[256,512]{1,0:T(8,128)S(1)}, f32[256,512]{1,0:T(8,128)S(1)}, u32[]{:S(2)}, u32[]{:S(2)}) collective-permute-start(f32[256,512]{1,0:T(8,128)S(1)} %shard_map.60.refs_19_), channel_id=1, source_target_pairs={{8,0},{9,1},{10,2},{11,3},{12,4},{13,5},{14,6},{15,7}} | collective-permute-start | bytes 1572872 | tf_op jit(solution)/shard_map/ppermute | solution.py:411
  125.3 24.0 %collective-permute-start.26 = (f32[256,512]{1,0:T(8,128)S(1)}, f32[256,512]{1,0:T(8,128)S(1)}, u32[]{:S(2)}, u32[]{:S(2)}) collective-permute-start(f32[256,512]{1,0:T(8,128)S(1)} %collective-permute-done.25.refs_26_.refs_35_), channel_id=1, source_target_pairs={{16,24},{17,25},{18,26},{19,27},{20,28},{21,29},{22,30},{23,31}} | collective-permute-start | bytes 1572872 | tf_op jit(solution)/shard_map/ppermute | solution.py:411
  134.8 17.3 %collective-permute-start.27 = (f32[256,512]{1,0:T(8,128)S(1)}, f32[256,512]{1,0:T(8,128)S(1)}, u32[]{:S(2)}, u32[]{:S(2)}) collective-permute-start(f32[256,512]{1,0:T(8,128)S(1)} %collective-permute-done.20.refs_16_.refs_27_), channel_id=1, source_target_pairs={{16,24},{17,25},{18,26},{19,27},{20,28},{21,29},{22,30},{23,31}} | collective-permute-start | bytes 1572872 | tf_op jit(solution)/shard_map/ppermute | solution.py:411
  (25 other events, 319.4 us)
Sparse Core Ops, SparseCore 0:
  10.8 55.4 all-gather.4
  68.7 89.8 all-gather.6
